TPU v7x, 32 devices: a whole 2x2x4 slice. The times are simulated.
32 devices in a mesh: blk: 2 (over x), tgt: 4 (over y, core), sec: 4 (over z).
Axes of the slice: x: 2, y: 2, z: 4, core: 2. Of those that a mesh axis runs over, the one named last changes fastest.
Arguments:
- modal_loads: bfloat16 [4096, 128], P('blk'), may hold values from -6 to 6
- receptance: bfloat16 [2, 4096, 4096], P(None, ('tgt', 'sec'), 'blk'), may hold values from -0.0625 to 0.0625
- shapes: bfloat16 [4096, 8, 128], P(('blk', 'tgt', 'sec')), may hold values from -0.1875 to 0.1875
- coupling: int32 [32, 8], P(('blk', 'tgt', 'sec')), may hold values from 0 to 31, all different within a row
- panel_coords: float32 [3, 4096], P(None, ('blk', 'tgt', 'sec')), may hold values from 0 to 1
- panel_areas: float32 [4096], P(('blk', 'tgt', 'sec')), may hold values from 0.1 to 1
Outputs:
- new_loads: float32 [4096, 128], P(('blk', 'tgt', 'sec'))
- pressure: bfloat16 [4096, 128], P(('blk', 'tgt', 'sec'))
Inputs may be any that keep to these rules, and one draw needn't show every extreme that they name: `coupling`: each row names 8 different mode blocks; every mode block is named by some row.
All inputs are finite; a program needn't handle non-finite values.
Results may differ from a plain program's by a relative error of at most 0.009.
Values may be sent and summed in bfloat16 or wider, within the bound.
No kernel may reach another device: no remote copies, remote signals or barrier semaphores. Data moves between devices by JAX's collectives and lax.ppermute only.
A program may use at most 64 MiB of HBM per device.

v0:
```python
import math

import jax
import jax.numpy as jnp
from jax import lax
from jax.sharding import PartitionSpec as P

wave_number = 40.0


def rotate_combine(leading, second):
    half_width = leading.shape[1] // 2
    return jnp.concatenate(
        [
            leading[:, :half_width] - second[:, half_width:],
            leading[:, half_width:] + second[:, :half_width],
        ],
        axis=1,
    )


def pressure_block(target_geometry, source_geometry, source_vel, total_panels):
    delta_x = target_geometry[0][:, None] - source_geometry[0][None, :]
    delta_y = target_geometry[1][:, None] - source_geometry[1][None, :]
    delta_z = target_geometry[2][:, None] - source_geometry[2][None, :]
    source_area = source_geometry[3][None, :]
    distance = jnp.sqrt(
        delta_x * delta_x + delta_y * delta_y + delta_z * delta_z + source_area / total_panels
    )
    weight = source_area / (distance * math.sqrt(total_panels))
    phase_angle = wave_number * distance
    kernel = jnp.concatenate(
        [
            (jnp.cos(phase_angle) * weight).astype(jnp.bfloat16),
            (jnp.sin(phase_angle) * weight).astype(jnp.bfloat16),
        ],
        axis=0,
    )
    products = lax.dot_general(
        kernel, source_vel, (((1,), (1,)), ((), ())), preferred_element_type=jnp.float32
    )
    target_count = target_geometry.shape[1]
    return rotate_combine(products[:target_count], products[target_count:])


def on_device(modal_loads, receptance, shapes, coupling, panel_coords, panel_areas):
    pan_dev = panel_coords.shape[1]
    case_width = modal_loads.shape[1]
    device_count = lax.axis_size("blk") * lax.axis_size("tgt") * lax.axis_size("sec")
    total_panels = float(pan_dev * device_count)
    row_share = receptance.shape[1]
    stacked = jnp.dot(
        receptance.reshape(2 * row_share, receptance.shape[2]),
        modal_loads,
        preferred_element_type=jnp.float32,
    )
    modal_sum = rotate_combine(stacked[:row_share], stacked[row_share:])
    modal_sum = lax.psum(modal_sum, "blk")
    amplitudes = lax.all_gather(modal_sum.astype(jnp.bfloat16), ("tgt", "sec"), axis=0, tiled=True)
    mode_block = shapes.shape[2]
    blocks = amplitudes.reshape(-1, mode_block, case_width)
    chosen = blocks[coupling]
    block_count = coupling.shape[0]
    shaped = shapes.reshape(block_count, -1, shapes.shape[1], mode_block)
    vel_t = (
        jnp.einsum("bpkm,bkmc->cbp", shaped, chosen, preferred_element_type=jnp.float32)
        .reshape(case_width, pan_dev)
        .astype(jnp.bfloat16)
    )
    geometry = jnp.concatenate([panel_coords, panel_areas[None, :]], axis=0)
    source_vel, source_geometry = (
        lax.all_gather(vel_t.astype(jnp.float32), ("tgt", "sec"), axis=1, tiled=True).astype(
            vel_t.dtype
        ),
        lax.all_gather(geometry, ("tgt", "sec"), axis=1, tiled=True),
    )
    target_geometry = lax.all_gather(geometry, "blk", axis=1, tiled=True)
    target_groups = pan_dev * lax.axis_size("blk") // pan_dev

    def single_block(block_index):
        target_block = lax.dynamic_slice_in_dim(target_geometry, block_index * pan_dev, pan_dev, 1)
        return pressure_block(target_block, source_geometry, source_vel, total_panels)

    stacked_terms = lax.map(single_block, jnp.arange(target_groups, dtype=jnp.int32))
    pressure_f = lax.psum_scatter(
        stacked_terms.reshape(pan_dev * lax.axis_size("blk"), case_width).astype(jnp.bfloat16),
        "blk",
        scatter_dimension=0,
        tiled=True,
    )
    weighted = (panel_areas[:, None] * pressure_f.astype(jnp.float32)).astype(jnp.bfloat16)
    contrib = jnp.einsum(
        "bpkm,bpc->bkmc",
        shaped,
        weighted.reshape(block_count, -1, case_width),
        preferred_element_type=jnp.float32,
    )
    onehot = (
        coupling[:, :, None] == jnp.arange(blocks.shape[0], dtype=jnp.int32)[None, None, :]
    ).astype(jnp.float32)
    partial_loads = jnp.einsum(
        "bkj,bkmc->jmc", onehot, contrib, precision=lax.Precision.HIGHEST
    ).reshape(-1, case_width)
    new_loads = lax.psum_scatter(
        partial_loads, ("blk", "tgt", "sec"), scatter_dimension=0, tiled=True
    )
    return (new_loads, pressure_f)


def solution(mesh):
    in_specs = (
        P("blk", None),
        P(None, ("tgt", "sec"), "blk"),
        P(("blk", "tgt", "sec"), None, None),
        P(("blk", "tgt", "sec"), None),
        P(None, ("blk", "tgt", "sec")),
        P(("blk", "tgt", "sec")),
    )
    out_specs = (P(("blk", "tgt", "sec"), None), P(("blk", "tgt", "sec"), None))
    return jax.shard_map(
        on_device, mesh=mesh, in_specs=in_specs, out_specs=out_specs, check_vma=False
    )
```

profile of v0, /device:TPU:0, one launch (start us, length us, event | category | flops | bytes accessed | tf_op | source)
XLA Modules:
  0.0 270.6 jit_solution(12580976208191597486)
XLA Ops:
  7.2 0.0 copy-start
  7.2 0.0 copy-start.3
  7.2 0.0 all-gather.2.cloned.1.call-start
  7.3 1.5 copy-done
  8.8 1.9 fusion.18
  10.7 11.9 %all-reduce.1 = bf16[256,128]{0,1:T(8,128)(2,1)} all-reduce(f32[256,128]{0,1:T(8,128)S(1)} %pad_maximum_fusion), channel_id=1, replica_groups=mesh['blk'=2,'tgt'=4,'sec'=4] {'blk'}, use_global_device_ids=true, to_apply=%region_0.0 | all-reduce | flops 32768 | bytes 196608 | tf_op jit(solution)/shard_map/psum | solution.py:58
  22.6 0.0 all-gather.2.cloned.1.call-update
  22.6 0.0 reduce-scatter.3.cloned.1.call-start
  22.7 4.3 %all_gather.12 = f32[4,256]{1,0:T(4,128)S(1)} all-gather(f32[4,128]{1,0:T(4,128)S(1)} %pad_maximum_fusion.1), channel_id=1, replica_groups=mesh['blk'=2,'tgt'=4,'sec'=4] {'blk'}, dimensions={1}, use_global_device_ids=true | all-gather | bytes 6144 | tf_op jit(solution)/shard_map/all_gather | solution.py:77
  27.1 30.1 %all_gather.13 = f32[4,2048]{1,0:T(4,128)S(1)} all-gather(f32[4,128]{1,0:T(4,128)S(1)} %pad_maximum_fusion.1), channel_id=1, replica_groups=mesh['blk'=2,'tgt'=4,'sec'=4] {'tgt','sec'}, dimensions={1}, use_global_device_ids=true | all-gather | bytes 34816 | tf_op jit(solution)/shard_map/all_gather | solution.py:75
  57.2 2.5 all-gather.2.cloned.1.call-done
  59.7 1.6 copy.17
  61.4 0.6 gather_fusion
  62.0 1.2 fusion.7
  63.2 36.2 %all_gather.15 = bf16[128,2048]{1,0:T(8,128)(2,1)S(1)} all-gather(bf16[128,128]{1,0:T(8,128)(2,1)S(1)} %fusion.7), channel_id=1, replica_groups=mesh['blk'=2,'tgt'=4,'sec'=4] {'tgt','sec'}, dimensions={1}, use_global_device_ids=true | all-gather | bytes 557056 | tf_op jit(solution)/shard_map/all_gather | solution.py:72
  99.4 13.2 %while.10 = (s32[]{:T(128)}, bf16[2,128,128]{1,2,0:T(8,128)(2,1)S(1)}, s32[2]{0:T(128)S(1)}, f32[4,256]{1,0:T(4,128)S(1)}, f32[4,2048]{1,0:T(4,128)S(1)}, /*inde...) while((s32[]{:T(128)}, bf16[2,128,128]{1,2,0:T(8,128)(2,1)S(1)}, ...), condition=%wide.region_2.3_spmd, body=%wide.region_1.2_spmd.sunk | while | flops 140609536 | bytes 3105455 | solution.py:84
  99.4 0.6 dynamic_slice.11
  100.7 4.7 %multiply_convert_fusion.4 = (bf16[128,2048]{1,0:T(8,128)(2,1)S(1)}, bf16[128,2048]{1,0:T(8,128)(2,1)S(1)}) fusion(f32[2048]{0:T(1024)S(1)} %bitcast.67, f32[2048]{0:T(1024)S(1)} %bitcast.68, f32[128]{0:T(128)S(1)} %get-tuple-element.112, f32[2048]{0:T(1024)S(1)} %bitcast.69, f32[128]{0:T(128)S(1)} %get-tuple-element.114, f32[2048]{0:T(1024)S(1)} %bitcast.70, ...), kind=kLoop, calls=%fused_computation.6.clone.1 | loop fusion | flops 4194304 | bytes 1091072 | tf_op jit(solution)/shard_map/while/body/eval_jaxpr/convert_element_type | solution.py:34
  105.5 0.5 fusion.33
  106.0 0.6 dynamic_slice.11
  107.3 4.7 %multiply_convert_fusion.4 = (bf16[128,2048]{1,0:T(8,128)(2,1)S(1)}, bf16[128,2048]{1,0:T(8,128)(2,1)S(1)}) fusion(f32[2048]{0:T(1024)S(1)} %bitcast.67, f32[2048]{0:T(1024)S(1)} %bitcast.68, f32[128]{0:T(128)S(1)} %get-tuple-element.112, f32[2048]{0:T(1024)S(1)} %bitcast.69, f32[128]{0:T(128)S(1)} %get-tuple-element.114, f32[2048]{0:T(1024)S(1)} %bitcast.70, ...), kind=kLoop, calls=%fused_computation.6.clone.1 | loop fusion | flops 4194304 | bytes 1091072 | tf_op jit(solution)/shard_map/while/body/eval_jaxpr/convert_element_type | solution.py:34
  112.1 0.5 fusion.33
  112.6 0.7 copy.13
  113.4 0.0 reduce-scatter.3.cloned.1.call-update
  113.4 0.0 reduce-scatter.5.cloned.1.call-start
  113.4 0.2 copy.16
  113.7 7.3 %reduce-scatter.3.cloned.1.call-done = bf16[128,128]{1,0:T(8,128)(2,1)} async-done(((bf16[256,128]{1,0:T(8,128)(2,1)}), bf16[128,128]{1,0:T(8,128)(2,1)}) %reduce-scatter.3.cloned.1.call-update) | async-done | bytes 32784 | tf_op jit(solution)/shard_map/reduce_scatter | solution.py:85
  121.0 1.0 convolution_bitcast_fusion
  122.1 1.1 fusion.13
  123.2 2.5 copy.14
  125.7 0.0 reduce-scatter.5.cloned.1.call-update
  125.7 138.3 %reduce-scatter.5.cloned.1.call-done = f32[128,128]{1,0:T(8,128)} async-done(((f32[4096,128]{1,0:T(8,128)}), f32[128,128]{1,0:T(8,128)}) %reduce-scatter.5.cloned.1.call-update) | async-done | bytes 65552 | tf_op jit(solution)/shard_map/reduce_scatter | solution.py:104
  (24 shorter events, 0.2 us)
Async XLA Ops:
  7.2 1.6 copy-start
  7.2 15.5 %copy-start.3 = (f32[128]{0:T(128)S(1)}, f32[128]{0:T(128)}, u32[]{:S(2)}) copy-start(f32[128]{0:T(128)} %param.13) | copy-start | bytes 1540
  7.2 15.5 %copy-start.2 = (f32[3,128]{1,0:T(4,128)S(1)}, f32[3,128]{1,0:T(4,128)}, u32[]{:S(2)}) copy-start(f32[3,128]{1,0:T(4,128)} %param.12) | copy-start | bytes 4612
  7.2 50.0 %copy-start.4 = (s32[1,8]{1,0:T(1,128)S(1)}, s32[1,8]{1,0:T(1,128)}, u32[]{:S(2)}) copy-start(s32[1,8]{1,0:T(1,128)} %param.11) | copy-start | bytes 100
  7.2 52.5 %all-gather.2.cloned.1.call-start = ((), (), s32[]{:S(2)}) async-start(), calls=%async_computation.2 | async-start | bytes 1114112 | tf_op jit(solution)/shard_map/all_gather | solution.py:59
  22.6 98.4 %reduce-scatter.3.cloned.1.call-start = ((), (), s32[]{:S(2)}) async-start(), calls=%async_computation.3 | async-start | bytes 98304 | tf_op jit(solution)/shard_map/reduce_scatter | solution.py:85
  99.4 14.0 %copy-start.1 = (bf16[128,8,128]{2,1,0:T(8,128)(2,1)S(1)}, bf16[128,8,128]{2,1,0:T(8,128)(2,1)}, u32[]{:S(2)}) copy-start(bf16[128,8,128]{2,1,0:T(8,128)(2,1)} %param.10) | copy-start | bytes 786436
  113.4 150.7 %reduce-scatter.5.cloned.1.call-start = ((), (), s32[]{:S(2)}) async-start(), calls=%async_computation.4 | async-start | bytes 2162688 | tf_op jit(solution)/shard_map/reduce_scatter | solution.py:104
Sparse Core Ops, SparseCore 0:
  22.8 36.9 all-gather.1
  113.5 7.4 reduce-scatter.2
  125.9 138.1 reduce-scatter.4
where the time goes:
time: 271 us
  waiting for transfers between devices  148 us (55%)
  blocking collectives  82.6 us (30%)
  between operations  13.9 us (5%)
  other arithmetic  9.65 us (4%)
  local copies, waits for them, and re-layouts  8.47 us (3%)
  matrix products  6.2 us (2%)
    reduce_scatter x1, waiting for transfers between devices, on_device(): lax.psum_scatter(partial_loads, ('blk', 'tgt', 'sec'), scatter_dimension=...  138 us
    all_gather x1, blocking collectives, on_device(): lax.all_gather(vel_t.astype(jnp.float32), ('tgt', 'sec'), axis=1, tiled=T...  36.2 us
    all_gather x1, blocking collectives, on_device(): lax.all_gather(geometry, ('tgt', 'sec'), axis=1, tiled=True)  30.1 us
    psum x1, blocking collectives, on_device(): modal_sum = lax.psum(modal_sum, 'blk')  11.9 us
    convert_element_type x2, other arithmetic, pressure_block(): (jnp.cos(phase_angle) * weight).astype(jnp.bfloat16)  9.49 us
    reduce_scatter x1, waiting for transfers between devices, on_device(): lax.psum_scatter(stacked_terms.reshape(pan_dev * lax.axis_size('blk'), ca...  7.33 us
  transfers between devices with their start and end apart: 3, of which 3 were waited for; matrix products, arithmetic and copies ran while one was open for 0% of the time, Pallas kernels for 0%

commit v1 on v0

--- a/solution.py
+++ b/solution.py
@@ -1,11 +1,456 @@
+import functools
 import math
 
 import jax
 import jax.numpy as jnp
+import numpy as np
 from jax import lax
+from jax.experimental import pallas as pl
+from jax.experimental.pallas import tpu as pltpu
 from jax.sharding import PartitionSpec as P
 
 wave_number = 40.0
+turns = wave_number / (2.0 * math.pi)
+bf16 = jnp.bfloat16
+f32 = jnp.float32
+AXES = ("blk", "tgt", "sec")
+GEO = 16
+
+
+def fit(values, terms):
+    nodes = 0.125 + 0.125 * np.cos(np.pi * (np.arange(400) + 0.5) / 400)
+    matrix = np.vander(nodes, terms, increasing=True)
+    return [float(c) for c in np.linalg.lstsq(matrix, values(nodes), rcond=None)[0]]
+
+
+sin_terms = fit(lambda u: math.sqrt(2.0) * np.sin(np.pi * np.sqrt(u)) / np.sqrt(u), 4)
+cos_terms = fit(lambda u: math.sqrt(2.0) * np.cos(np.pi * np.sqrt(u)), 4)
+round_shift = 1.5 * 2.0**23
+
+
+def exchange_plane(x, mask):
+    nb, nt = lax.axis_size("blk"), lax.axis_size("tgt")
+    pairs = [
+        (b * nt + t, (b ^ (mask & 1)) * nt + (t ^ (2 * (mask >> 1))))
+        for b in range(nb)
+        for t in range(nt)
+    ]
+    return lax.ppermute(x, ("blk", "tgt"), pairs)
+
+
+def exchange_sec(x, mask):
+    return lax.ppermute(x, "sec", [(s, s ^ mask) for s in range(lax.axis_size("sec"))])
+
+
+def exchange_core(x):
+    return lax.ppermute(x, "tgt", [(t, t ^ 1) for t in range(lax.axis_size("tgt"))])
+
+
+def place():
+    t = lax.axis_index("tgt")
+    return lax.axis_index("blk"), t // 2, t % 2, lax.axis_index("sec")
+
+
+def three_parts(x):
+    first = x.astype(bf16).astype(f32)
+    rest = x - first
+    second = rest.astype(bf16).astype(f32)
+    return first, second, rest - second
+
+
+def amplitude_kernel(panels, where, r_ref, l_ref, xyz_ref, area_ref, cpl_ref, own_ref, s1_ref, s2_ref, s3_ref, geo_ref, acc, amp_t, geo):
+    step = pl.program_id(0)
+    rows = r_ref.shape[1]
+    depth = r_ref.shape[2]
+    term = jnp.dot(r_ref[...].reshape(2 * rows, depth), l_ref[...], preferred_element_type=f32)
+
+    @pl.when(step == 0)
+    def _():
+        acc[...] = term
+        scaled = (xyz_ref[...] - 0.5) * turns
+        area = area_ref[...]
+        norm = jnp.sum(scaled * scaled, axis=0, keepdims=True) + area * (turns * turns / panels)
+        geo[...] = jnp.zeros_like(geo)
+        for i, part in enumerate(three_parts(scaled)):
+            geo[3 * i : 3 * i + 3, :] = part
+        for i, part in enumerate(three_parts(norm)):
+            geo[9 + i : 10 + i, :] = part
+        for i, part in enumerate(three_parts(area)):
+            geo[12 + i : 13 + i, :] = part
+        geo[15:16, 0 : cpl_ref.shape[1]] = cpl_ref[...].astype(f32)
+
+    @pl.when(step > 0)
+    def _():
+        acc[...] += term
+
+    @pl.when(step == pl.num_programs(0) - 1)
+    def _():
+        width = acc.shape[1]
+        half = width // 2
+        lead, second = acc[0:rows, :], acc[rows:, :]
+        turned = pltpu.roll(second, half, 1)
+        lane = lax.broadcasted_iota(jnp.int32, turned.shape, 1)
+        amp = lead + jnp.where(lane < half, -turned, turned)
+        amp_t[...] = amp.T
+        quarter = half // 4
+        mine = where[0]
+        blocks = rows // 128
+        geo_ref[...] = geo[...].astype(bf16)
+        for mask, out in enumerate((own_ref, s1_ref, s2_ref, s3_ref)):
+            at = pl.multiple_of((mine ^ mask) * quarter, quarter)
+            for part in range(2):
+                piece = amp_t[pl.ds(part * half + at, quarter), :]
+                for b in range(blocks):
+                    r0 = b * 2 * quarter + part * quarter
+                    out[r0 : r0 + quarter, :] = piece[:, b * 128 : (b + 1) * 128].astype(out.dtype)
+            if mask:
+                out[blocks * 2 * quarter :, :] = geo_ref[...]
+
+
+def amplitude_parts(panels, where, receptance, loads, xyz, area, coupling):
+    _, rows, depth = receptance.shape
+    width = loads.shape[1]
+    steps = 4
+    part = depth // steps
+    chunk = rows // 128 * (width // 4)
+    whole = lambda shape: pl.BlockSpec(shape, lambda i: (0,) * len(shape))
+    outs = [((chunk, 128), f32)] + [((chunk + GEO, 128), bf16)] * 3 + [((GEO, 128), bf16)]
+    return pl.pallas_call(
+        functools.partial(amplitude_kernel, panels),
+        grid=(steps,),
+        in_specs=[
+            pl.BlockSpec(memory_space=pltpu.SMEM),
+            pl.BlockSpec((2, rows, part), lambda i: (0, 0, i)),
+            pl.BlockSpec((part, width), lambda i: (i, 0)),
+            whole(xyz.shape),
+            whole(area.shape),
+            whole(coupling.shape),
+        ],
+        out_specs=[whole(s) for s, _ in outs],
+        out_shape=[jax.ShapeDtypeStruct(s, d) for s, d in outs],
+        scratch_shapes=[
+            pltpu.VMEM((2 * rows, width), f32),
+            pltpu.VMEM((width, rows), f32),
+            pltpu.VMEM((GEO, 128), f32),
+        ],
+        compiler_params=pltpu.CompilerParams(vmem_limit_bytes=32 << 20),
+        cost_estimate=pl.CostEstimate(flops=4 * rows * depth * width, bytes_accessed=4 * rows * depth, transcendentals=0),
+        name="amplitude_parts",
+    )(where, receptance, loads, xyz, area, coupling)
+
+
+def amplitude_sum_kernel(own_ref, geo_ref, x_ref, y_ref, d_ref, out_ref):
+    n = own_ref.shape[0]
+    out_ref[0:n, :] = (own_ref[...] + x_ref[0:n, :].astype(f32)).astype(bf16)
+    out_ref[n : 2 * n, :] = (y_ref[0:n, :].astype(f32) + d_ref[0:n, :].astype(f32)).astype(bf16)
+    out_ref[2 * n : 2 * n + GEO, :] = geo_ref[...]
+    for i, r in enumerate((x_ref, y_ref, d_ref)):
+        out_ref[2 * n + GEO * (i + 1) : 2 * n + GEO * (i + 2), :] = r[n:, :]
+
+
+def amplitude_sum(own, geo, x, y, d):
+    n = own.shape[0]
+    return pl.pallas_call(
+        amplitude_sum_kernel,
+        out_shape=jax.ShapeDtypeStruct((2 * n + 4 * GEO, 128), bf16),
+        name="amplitude_sum",
+    )(own, geo, x, y, d)
+
+
+def velocity_kernel(width, blocks, where, cpl, near_ref, far_ref, m0, m1, m2, m3, out_ref, picked):
+    _, y, c, z = (where[1 + i] for i in range(4))
+    count = m0.shape[1] // 128
+    secs = near_ref.shape[0]
+    for j, m_ref in enumerate((m0, m1, m2, m3)):
+        for k in range(count):
+            b = cpl[j, k]
+            h = b % blocks
+            owner = b // blocks
+            t, s = owner // secs, owner % secs
+            row = pl.multiple_of((((t // 2) ^ y) * blocks + h) * width, width)
+            zr = s ^ z
+
+            @pl.when((t % 2) == c)
+            def _():
+                picked[:, k * 128 : (k + 1) * 128] = near_ref[zr, pl.ds(row, width), :]
+
+            @pl.when((t % 2) != c)
+            def _():
+                picked[:, k * 128 : (k + 1) * 128] = far_ref[zr, pl.ds(row, width), :]
+
+        vel = lax.dot_general(picked[...], m_ref[...], (((1,), (1,)), ((), ())), preferred_element_type=f32)
+        out_ref[j] = vel.astype(bf16)
+
+
+def velocities(where, cpl, near, far, modes, width, blocks):
+    vmem = pl.BlockSpec(memory_space=pltpu.VMEM)
+    smem = pl.BlockSpec(memory_space=pltpu.SMEM)
+    panels, depth = modes[0].shape
+    return pl.pallas_call(
+        functools.partial(velocity_kernel, width, blocks),
+        in_specs=[smem, smem] + [vmem] * 6,
+        out_specs=vmem,
+        out_shape=jax.ShapeDtypeStruct((4, width, panels), bf16),
+        scratch_shapes=[pltpu.VMEM((width, depth), bf16)],
+        compiler_params=pltpu.CompilerParams(vmem_limit_bytes=32 << 20),
+        name="velocities",
+    )(where, cpl, near, far, *modes)
+
+
+def helmholtz_kernel(panels, tgt_ref, src_ref, re_ref, im_ref, tgt_mat, dist):
+    groups = tgt_ref.shape[0] // GEO
+    lanes = 128
+    scale = turns / math.sqrt(panels)
+
+    @pl.when(pl.program_id(0) == 0)
+    def _():
+        ones = jnp.ones((3, lanes), f32)
+        for j in range(groups):
+            g = tgt_ref[j * GEO : (j + 1) * GEO, :].astype(f32)
+            area = g[12:13] + g[13:14] + g[14:15]
+            norm = g[9:10] + g[10:11] + g[11:12] - area * (turns * turns / panels)
+            col = slice(j * lanes, (j + 1) * lanes)
+            tgt_mat[:, col] = jnp.zeros((tgt_mat.shape[0], lanes), f32)
+            for a in range(3):
+                for b in range(3):
+                    tgt_mat[16 * a + 3 * b : 16 * a + 3 * b + 3, col] = -2.0 * g[3 * a : 3 * a + 3]
+            tgt_mat[9:12, col] = ones
+            for i, part in enumerate(three_parts(norm)):
+                tgt_mat[48 + i : 49 + i, col] = part
+
+    src = [src_ref[0, j * GEO : (j + 1) * GEO, :] for j in range(groups)]
+    wide = jnp.concatenate(src, axis=1)
+    stack = jnp.concatenate([wide, wide, wide, jnp.ones_like(wide)], axis=0)
+    dist[...] = lax.dot_general(
+        tgt_mat[...].astype(bf16), stack, (((0,), (0,)), ((), ())), preferred_element_type=f32
+    )
+    area = wide[12:15, :].astype(f32)
+    weight = (area[0:1] + area[1:2] + area[2:3]) * scale
+    strip = 16
+
+    def step(i, _):
+        r0 = pl.multiple_of(i * strip, strip)
+        for c0 in range(0, groups * lanes, 256):
+            cols = slice(c0, c0 + 256)
+            square = dist[pl.ds(r0, strip), cols]
+            inverse = lax.rsqrt(square)
+            t = square * inverse
+            f = t - ((t + round_shift) - round_shift)
+            u = f * f
+            s = (((sin_terms[3] * u + sin_terms[2]) * u + sin_terms[1]) * u + sin_terms[0]) * f
+            c = ((cos_terms[3] * u + cos_terms[2]) * u + cos_terms[1]) * u + cos_terms[0]
+            w = weight[:, cols] * inverse
+            re_ref[pl.ds(r0, strip), cols] = (w - (s * s) * w).astype(bf16)
+            im_ref[pl.ds(r0, strip), cols] = ((s * c) * w).astype(bf16)
+        return 0
+
+    lax.fori_loop(0, dist.shape[0] // strip, step, 0, unroll=2)
+
+
+def helmholtz(panels, targets, payload):
+    secs, rows, lanes = payload.shape
+    geo = targets.shape[0]
+    side = geo // GEO * lanes
+    at = rows // geo - 1
+    return pl.pallas_call(
+        functools.partial(helmholtz_kernel, panels),
+        grid=(secs,),
+        in_specs=[
+            pl.BlockSpec(targets.shape, lambda i: (0, 0)),
+            pl.BlockSpec((1, geo, lanes), lambda i: (i, at, 0)),
+        ],
+        out_specs=[pl.BlockSpec((side, side), lambda i: (0, i))] * 2,
+        out_shape=[jax.ShapeDtypeStruct((side, secs * side), bf16)] * 2,
+        scratch_shapes=[pltpu.VMEM((64, side), f32), pltpu.VMEM((side, side), f32)],
+        compiler_params=pltpu.CompilerParams(vmem_limit_bytes=40 << 20),
+        cost_estimate=pl.CostEstimate(flops=30 * side * side * secs, bytes_accessed=4 * side * side * secs, transcendentals=side * side * secs),
+        name="helmholtz",
+    )(targets, payload)
+
+
+def pressure_kernel(blocks_of, where, cpl, va_ref, vb_ref, ar_ref, ai_ref, br_ref, bi_ref, geo_ref, m0, m1, m2, m3, pt_ref, near_ref, far_ref, acc, lead, turned, total):
+    step = pl.program_id(0)
+    secs = pl.num_programs(0)
+    groups, width, lanes = va_ref.shape[1:]
+    half = width // 2
+
+    def product(v_ref, gr_ref, gi_ref):
+        for j in range(groups):
+            v = v_ref[0, j]
+            col = slice(j * lanes, (j + 1) * lanes)
+            lead[:, col] = v
+            turned[0:half, col] = -v[half:]
+            turned[half:, col] = v[0:half]
+        dims = (((1,), (1,)), ((), ()))
+        return lax.dot_general(gr_ref[...], lead[...], dims, preferred_element_type=f32) + lax.dot_general(
+            gi_ref[...], turned[...], dims, preferred_element_type=f32
+        )
+
+    term = product(va_ref, ar_ref, ai_ref) + product(vb_ref, br_ref, bi_ref)
+
+    @pl.when(step == 0)
+    def _():
+        acc[...] = term
+
+    @pl.when(step > 0)
+    def _():
+        acc[...] += term
+
+    @pl.when(step == secs - 1)
+    def _():
+        x, y, c, z = (where[1 + i] for i in range(4))
+        p = acc[...].T.astype(bf16)
+        total[...] = jnp.zeros_like(total)
+        count = m0.shape[1] // lanes
+        sec_n, tgt_n = blocks_of
+        for j, m_ref in enumerate((m0, m1, m2, m3)):
+            pj = p[:, j * lanes : (j + 1) * lanes]
+            pt_ref[j] = pj
+            g = geo_ref[j * GEO + 12 : j * GEO + 15, :].astype(f32)
+            area = g[0:1] + g[1:2] + g[2:3]
+            weighted = (pj.astype(f32) * area).astype(bf16)
+            terms = jnp.dot(weighted, m_ref[...], preferred_element_type=f32)
+            for k in range(count):
+                b = cpl[j, k]
+                s = b % sec_n
+                t = (b // sec_n) % tgt_n
+                xb = b // (sec_n * tgt_n)
+                at = (((t % 2) ^ c) * sec_n + (s ^ z)) * groups + (xb ^ x) + 2 * ((t // 2) ^ y)
+                total[at] += terms[:, k * lanes : (k + 1) * lanes]
+        n = near_ref.shape[0]
+        near_ref[...] = total[0:n]
+        far_ref[...] = total[n:].astype(bf16)
+
+
+def pressures(where, cpl, va, vb, ga, gb, geo, modes, tgt_n):
+    secs, groups, width, lanes = va.shape
+    side = groups * lanes
+    smem = pl.BlockSpec(memory_space=pltpu.SMEM)
+    whole = lambda shape: pl.BlockSpec(shape, lambda i: (0,) * len(shape))
+    vel = pl.BlockSpec((1, groups, width, lanes), lambda i: (i, 0, 0, 0))
+    mat = pl.BlockSpec((side, side), lambda i: (0, i))
+    n = secs * groups
+    return pl.pallas_call(
+        functools.partial(pressure_kernel, (secs, tgt_n)),
+        grid=(secs,),
+        in_specs=[smem, smem, vel, vel, mat, mat, mat, mat, whole(geo.shape)] + [whole(modes[0].shape)] * 4,
+        out_specs=[whole((groups, width, lanes)), whole((n, width, lanes)), whole((n, width, lanes))],
+        out_shape=[
+            jax.ShapeDtypeStruct((groups, width, lanes), bf16),
+            jax.ShapeDtypeStruct((n, width, lanes), f32),
+            jax.ShapeDtypeStruct((n, width, lanes), bf16),
+        ],
+        scratch_shapes=[
+            pltpu.VMEM((side, width), f32),
+            pltpu.VMEM((width, side), bf16),
+            pltpu.VMEM((width, side), bf16),
+            pltpu.VMEM((2 * n, width, lanes), f32),
+        ],
+        compiler_params=pltpu.CompilerParams(vmem_limit_bytes=48 << 20),
+        name="pressures",
+    )(where, cpl, va, vb, *ga, *gb, geo, *modes)
+
+
+def core_sum_kernel(near_ref, got_ref, own_ref, *send):
+    groups = own_ref.shape[0]
+    own_ref[...] = near_ref[0:groups] + got_ref[0:groups].astype(f32)
+    for i, s in enumerate(send):
+        r = slice((i + 1) * groups, (i + 2) * groups)
+        s[...] = (near_ref[r] + got_ref[r].astype(f32)).astype(bf16)
+
+
+def core_sum(near, got, secs):
+    groups = near.shape[0] // secs
+    shape = (groups,) + near.shape[1:]
+    return pl.pallas_call(
+        core_sum_kernel,
+        out_shape=[jax.ShapeDtypeStruct(shape, f32)] + [jax.ShapeDtypeStruct(shape, bf16)] * (secs - 1),
+        name="core_sum",
+    )(near, got)
+
+
+def sec_sum_kernel(count, *refs):
+    own, got, pt, outs = refs[0], refs[1 : 1 + count], refs[1 + count], refs[2 + count :]
+    for j, out in enumerate(outs):
+        value = own[j]
+        for g in got:
+            value = value + g[j].astype(f32)
+        out[0] = value.astype(out.dtype)
+        out[1] = pt[j].astype(out.dtype)
+
+
+def sec_sum(own, got, pt):
+    shape = (2,) + own.shape[1:]
+    return pl.pallas_call(
+        functools.partial(sec_sum_kernel, len(got)),
+        out_shape=[jax.ShapeDtypeStruct(shape, f32)] + [jax.ShapeDtypeStruct(shape, bf16)] * 3,
+        name="sec_sum",
+    )(own, *got, pt)
+
+
+def output_kernel(where, r0, r1, r2, r3, loads_ref, press_ref, loads_t, press_t):
+    half = loads_t.shape[0] // 2
+    quarter = half // 4
+    for mask, r in enumerate((r0, r1, r2, r3)):
+        at = pl.multiple_of((where[0] ^ mask) * quarter, quarter)
+        for part in range(2):
+            rows = pl.ds(part * half + at, quarter)
+            loads_t[rows, :] = r[0, part * quarter : (part + 1) * quarter, :].astype(f32)
+            press_t[rows, :] = r[1, part * quarter : (part + 1) * quarter, :].astype(f32)
+    loads_ref[...] = loads_t[...].T
+    press_ref[...] = press_t[...].T.astype(bf16)
+
+
+def outputs(where, parts):
+    _, width, lanes = parts[0].shape
+    cols = 4 * width
+    vmem = pl.BlockSpec(memory_space=pltpu.VMEM)
+    return pl.pallas_call(
+        output_kernel,
+        in_specs=[pl.BlockSpec(memory_space=pltpu.SMEM)] + [vmem] * 4,
+        out_specs=[vmem, vmem],
+        out_shape=[jax.ShapeDtypeStruct((lanes, cols), f32), jax.ShapeDtypeStruct((lanes, cols), bf16)],
+        scratch_shapes=[pltpu.VMEM((cols, lanes), f32)] * 2,
+        name="outputs",
+    )(where, *parts)
+
+
+def on_device_fast(modal_loads, receptance, shapes, coupling, panel_coords, panel_areas):
+    secs, tgts = lax.axis_size("sec"), lax.axis_size("tgt")
+    device_count = lax.axis_size("blk") * tgts * secs
+    pan_dev = panel_coords.shape[1]
+    panels = float(pan_dev * device_count)
+    width = modal_loads.shape[1] // 4
+    blocks = receptance.shape[1] // shapes.shape[2]
+    x, y, c, z = place()
+    where = jnp.stack([x + 2 * y, x, y, c, z]).astype(jnp.int32)
+
+    own, s1, s2, s3, geo = amplitude_parts(
+        panels, where, receptance, modal_loads, panel_coords, panel_areas[None, :], coupling
+    )
+    got = [exchange_plane(s, m) for m, s in ((1, s1), (2, s2), (3, s3))]
+    flat = shapes.reshape(pan_dev, -1)
+    modes = [flat] + [exchange_plane(flat, m) for m in (1, 2, 3)]
+    count = coupling.shape[1]
+    cpl = jnp.concatenate(
+        [coupling] + [g[-1:, :count].astype(jnp.int32) for g in got], axis=0
+    )
+    payload = amplitude_sum(own, geo, *got)
+    near = jnp.stack([payload] + [exchange_sec(payload, m) for m in range(1, secs)])
+    far = exchange_core(near)
+    targets = payload[-4 * GEO :, :]
+    g_near = helmholtz(panels, targets, near)
+    g_far = helmholtz(panels, targets, far)
+    vel = velocities(where, cpl, near, far, modes, width, blocks)
+    v_near = jnp.stack([vel] + [exchange_sec(vel, m) for m in range(1, secs)])
+    v_far = exchange_core(v_near)
+    pt, n_near, n_far = pressures(where, cpl, v_near, v_far, g_near, g_far, targets, modes, tgts)
+    n_got = exchange_core(n_far)
+    parts = core_sum(n_near, n_got, secs)
+    sec_got = [exchange_sec(p, m) for m, p in zip(range(1, secs), parts[1:])]
+    finals = sec_sum(parts[0], sec_got, pt)
+    mine = [finals[0]] + [exchange_plane(f, m) for m, f in zip((1, 2, 3), finals[1:])]
+    return outputs(where, mine)
 
 
 def rotate_combine(leading, second):
@@ -43,7 +488,7 @@
     return rotate_combine(products[:target_count], products[target_count:])
 
 
-def on_device(modal_loads, receptance, shapes, coupling, panel_coords, panel_areas):
+def on_device_general(modal_loads, receptance, shapes, coupling, panel_coords, panel_areas):
     pan_dev = panel_coords.shape[1]
     case_width = modal_loads.shape[1]
     device_count = lax.axis_size("blk") * lax.axis_size("tgt") * lax.axis_size("sec")
@@ -107,6 +552,24 @@
     return (new_loads, pressure_f)
 
 
+def on_device(modal_loads, receptance, shapes, coupling, panel_coords, panel_areas):
+    lanes = 128
+    secs = lax.axis_size("sec")
+    mine = modal_loads.shape[0] * lax.axis_size("blk") // (lax.axis_size("blk") * lax.axis_size("tgt") * secs)
+    fits = (
+        lax.axis_size("blk") == 2
+        and lax.axis_size("tgt") == 4
+        and secs & (secs - 1) == 0
+        and coupling.shape[0] == 1
+        and shapes.shape[2] == lanes
+        and panel_coords.shape[1] == lanes
+        and modal_loads.shape[1] == lanes
+        and mine == lanes
+    )
+    body = on_device_fast if fits else on_device_general
+    return body(modal_loads, receptance, shapes, coupling, panel_coords, panel_areas)
+
+
 def solution(mesh):
     in_specs = (
         P("blk", None),

time: 271 us -> 87.4 us (0.32)
  waiting for transfers between devices: 148 us -> 17.1 us
  blocking collectives: 82.6 us -> 0 us
  Pallas kernels: 0 us -> 28.3 us
  starting transfers between devices: 0.12 us -> 25.6 us
  between operations: 13.9 us -> 0.83 us
  other arithmetic: 9.65 us -> 2.87 us
  matrix products: 6.2 us -> 0 us
  local copies, waits for them, and re-layouts: 8.47 us -> 12 us
    reduce_scatter x2 -> x0, waiting for transfers between devices: 146 us -> none  [the longest x1 138 us: on_device(): lax.psum_scatter(partial_loads, ('blk', 'tgt', 'sec'), scatter_dimension=...]
    all_gather x3 -> x0, blocking collectives: 70.7 us -> none  [the longest x1 36.2 us: on_device(): lax.all_gather(vel_t.astype(jnp.float32), ('tgt', 'sec'), axis=1, tiled=T...]
    pallas_call x0 -> x9, Pallas kernels: none -> 28.3 us  [the longest x2 11.9 us: helmholtz(): pl.pallas_call(functools.partial(helmholtz_kernel, panels), grid=(secs,),...]
    ppermute x0 -> x21, starting transfers between devices: none -> 25.6 us  [the longest x9 13.2 us: exchange_sec(): lax.ppermute(x, 'sec', [(s, s ^ mask) for s in range(lax.axis_size('sec'))])]
    ppermute x0 -> x21, waiting for transfers between devices: none -> 17.1 us  [the longest x9 10.2 us: exchange_sec(): lax.ppermute(x, 'sec', [(s, s ^ mask) for s in range(lax.axis_size('sec'))])]
    psum x1 -> x0, blocking collectives: 11.9 us -> none  [on_device(): modal_sum = lax.psum(modal_sum, 'blk')]
    unnamed x11 -> x49, local copies, waits for them, and re-layouts: 1.77 us -> 11.1 us
    convert_element_type x2 -> x3, other arithmetic: 9.49 us -> 2.01 us  [on_device_fast(): g[-1:, :count].astype(jnp.int32)]
  transfers between devices with their start and end apart: 3 -> 21, of which waited for: 3 -> 12; matrix products, arithmetic and copies ran while one was open for 0% -> 4% of each run, Pallas kernels for 0% -> 15%
where the time goes in v1:
time: 87.4 us; the launch traced here: 86.7 us
  Pallas kernels  28.3 us (32%)
  starting transfers between devices  25.6 us (29%)
  waiting for transfers between devices  17.1 us (20%)
  local copies, waits for them, and re-layouts  12 us (14%)
  other arithmetic  2.87 us (3%)
    ppermute x9, starting transfers between devices, exchange_sec(): lax.ppermute(x, 'sec', [(s, s ^ mask) for s in range(lax.axis_size('sec'))])  13.2 us
    pallas_call x2, Pallas kernels, helmholtz(): pl.pallas_call(functools.partial(helmholtz_kernel, panels), grid=(secs,),...  11.9 us
    ppermute x9, starting transfers between devices, exchange_plane(): return lax.ppermute(x, ('blk', 'tgt'), pairs)  11.8 us
    unnamed x49, local copies, waits for them, and re-layouts  11.1 us
    ppermute x9, waiting for transfers between devices, exchange_sec(): lax.ppermute(x, 'sec', [(s, s ^ mask) for s in range(lax.axis_size('sec'))])  10.2 us
    ppermute x9, waiting for transfers between devices, exchange_plane(): return lax.ppermute(x, ('blk', 'tgt'), pairs)  5.89 us
    pallas_call x1, Pallas kernels, pressures(): pl.pallas_call(functools.partial(pressure_kernel, (secs, tgt_n)), grid=(s...  5.8 us
    pallas_call x1, Pallas kernels, amplitude_parts(): pl.pallas_call(functools.partial(amplitude_kernel, panels), grid=(steps,)...  2.23 us
  transfers between devices with their start and end apart: 21, of which 12 were waited for; matrix products, arithmetic and copies ran while one was open for 4% of the time, Pallas kernels for 15%

profile of v1, /device:TPU:0, one launch (start us, length us, event | category | flops | bytes accessed | tf_op | source)
XLA Modules:
  0.0 86.7 jit_solution(1839000677787852469)
XLA Ops:
  0.8 1.6 %copy-done = bf16[2,256,2048]{2,1,0:T(8,128)(2,1)S(1)} copy-done((bf16[2,256,2048]{2,1,0:T(8,128)(2,1)S(1)}, bf16[2,256,2048]{2,1,0:T(8,128)(2,1)}, u32[]{:S(2)}) %copy-start) | copy-done | bytes 2097176
  2.3 1.0 %copy-done.3 = bf16[2048,128]{1,0:T(8,128)(2,1)S(1)} copy-done((bf16[2048,128]{1,0:T(8,128)(2,1)S(1)}, bf16[2048,128]{1,0:T(8,128)(2,1)}, u32[]{:S(2)}) %copy-start.3) | copy-done | bytes 524312
  5.4 2.2 %amplitude_parts.1 = (f32[64,128]{1,0:T(8,128)S(1)}, bf16[80,128]{1,0:T(8,128)(2,1)S(1)}, bf16[80,128]{1,0:T(8,128)(2,1)S(1)}, bf16[80,128]{1,0:T(8,128)(2,1)S(1)}, bf16[16,128]{1,0:T(8,128)(2,1)S(1)}) custom-call(s32[5]{0:T(128)S(1)} %stack.53.where, bf16[2,256,2048]{2,1,0:T(8,128)(2,1)S(1)} %copy-done, bf16[2048,128]{1,0:T(8,128)(2,1)S(1)} %copy-done.3, ...), custom_call_target="tpu_custom_call" | custom-call | flops 268435456 | bytes 2097152 | tf_op jit(solution)/shard_map/amplitude_parts/pallas_call | solution.py:118
  7.6 3.0 %collective-permute-start = (bf16[80,128]{1,0:T(8,128)(2,1)S(1)}, bf16[80,128]{1,0:T(8,128)(2,1)S(1)}, u32[]{:S(2)}, u32[]{:S(2)}) collective-permute-start(bf16[80,128]{1,0:T(8,128)(2,1)S(1)} %get-tuple-element.22), channel_id=1, source_target_pairs={{0,16},{4,20},{8,24},{12,28},{16,0},{20,4},{24,8},{28,12},{1,17},{... | collective-permute-start | bytes 61448 | tf_op jit(solution)/shard_map/ppermute | solution.py:38
  10.6 1.5 %collective-permute-start.1 = (bf16[80,128]{1,0:T(8,128)(2,1)S(1)}, bf16[80,128]{1,0:T(8,128)(2,1)S(1)}, u32[]{:S(2)}, u32[]{:S(2)}) collective-permute-start(bf16[80,128]{1,0:T(8,128)(2,1)S(1)} %get-tuple-element.23), channel_id=1, source_target_pairs={{0,8},{4,12},{8,0},{12,4},{16,24},{20,28},{24,16},{28,20},{1,9},{5... | collective-permute-start | bytes 61448 | tf_op jit(solution)/shard_map/ppermute | solution.py:38
  12.2 3.0 %collective-permute-start.9 = (bf16[128,1024]{1,0:T(8,128)(2,1)S(1)}, bf16[128,1024]{1,0:T(8,128)(2,1)S(1)}, u32[]{:S(2)}, u32[]{:S(2)}) collective-permute-start(bf16[128,1024]{1,0:T(8,128)(2,1)S(1)} %bitcast.18), channel_id=1, source_target_pairs={{0,24},{4,28},{8,16},{12,20},{16,8},{20,12},{24,0},{28,4},{1,25},{... | collective-permute-start | bytes 786440 | tf_op jit(solution)/shard_map/ppermute | solution.py:38
  15.7 1.4 %collective-permute-done.2.d_ref = bf16[80,128]{1,0:T(8,128)(2,1)S(1)} collective-permute-done((bf16[80,128]{1,0:T(8,128)(2,1)S(1)}, bf16[80,128]{1,0:T(8,128)(2,1)S(1)}, u32[]{:S(2)}, u32[]{:S(2)}) %collective-permute-start.2) | collective-permute-done | bytes 20512 | tf_op jit(solution)/shard_map/ppermute | solution.py:38
  17.8 1.4 %amplitude_sum.1 = bf16[192,128]{1,0:T(8,128)(2,1)} custom-call(f32[64,128]{1,0:T(8,128)} %copy-done.6, bf16[16,128]{1,0:T(8,128)(2,1)} %copy-done.8, bf16[80,128]{1,0:T(8,128)(2,1)} %copy-done.19, bf16[80,128]{1,0:T(8,128)(2,1)} %copy-done.20, bf16[80,128]{1,0:T(8,128)(2,1)} %copy-done.18), custom_call_target="tpu_custom_call" | custom-call | tf_op jit(solution)/shard_map/amplitude_sum/pallas_call | solution.py:153
  19.2 3.6 %collective-permute-start.5 = (bf16[192,128]{1,0:T(8,128)(2,1)}, bf16[192,128]{1,0:T(8,128)(2,1)S(1)}, u32[]{:S(2)}, u32[]{:S(2)}) collective-permute-start(bf16[192,128]{1,0:T(8,128)(2,1)} %amplitude_sum.1), channel_id=1, source_target_pairs={{0,3},{1,2},{2,1},{3,0},{4,7},{5,6},{6,5},{7,4},{8,11},{9,10},{10,... | collective-permute-start | bytes 147464 | tf_op jit(solution)/shard_map/ppermute | solution.py:42
  22.8 0.8 collective-permute-start.3
  25.8 2.2 %collective-permute-done.4 = bf16[192,128]{1,0:T(8,128)(2,1)S(1)} collective-permute-done((bf16[192,128]{1,0:T(8,128)(2,1)}, bf16[192,128]{1,0:T(8,128)(2,1)S(1)}, u32[]{:S(2)}, u32[]{:S(2)}) %collective-permute-start.4) | collective-permute-done | bytes 49184 | tf_op jit(solution)/shard_map/ppermute | solution.py:42
  28.0 0.8 pad_maximum_fusion.near_ref.src_ref
  29.6 2.2 %collective-permute-done.7.m1 = bf16[128,1024]{1,0:T(8,128)(2,1)S(1)} collective-permute-done((bf16[128,1024]{1,0:T(8,128)(2,1)S(1)}, bf16[128,1024]{1,0:T(8,128)(2,1)S(1)}, u32[]{:S(2)}, u32[]{:S(2)}) %collective-permute-start.7) | collective-permute-done | bytes 262176 | tf_op jit(solution)/shard_map/ppermute | solution.py:38
  31.9 2.2 %velocities.1 = bf16[4,32,128]{2,1,0:T(8,128)(2,1)S(1)} custom-call(s32[5]{0:T(128)S(1)} %stack.53.where, s32[4,8]{1,0:T(4,128)S(1)} %pad_add_fusion.cpl, bf16[4,192,128]{2,1,0:T(8,128)(2,1)S(1)} %pad_maximum_fusion.near_ref.src_ref, bf16[4,192,128]{2,1,0:T(8,128)(2,1)S(1)} %collective-permute-done.6.far_ref.src_ref, bf16[128,1024]{1,0:T(8,128)(2,1)S(1)} %bitcast.21, ...), custom_call_target="tpu_custom_call" | custom-call | tf_op jit(solution)/shard_map/velocities/pallas_call | solution.py:189
  34.1 3.5 %collective-permute-start.12 = (bf16[4,32,128]{2,1,0:T(8,128)(2,1)S(1)}, bf16[4,32,128]{2,1,0:T(8,128)(2,1)S(1)}, u32[]{:S(2)}, u32[]{:S(2)}) collective-permute-start(bf16[4,32,128]{2,1,0:T(8,128)(2,1)S(1)} %velocities.1), channel_id=1, source_target_pairs={{0,3},{1,2},{2,1},{3,0},{4,7},{5,6},{6,5},{7,4},{8,11},{9,10},{10,... | collective-permute-start | bytes 98312 | tf_op jit(solution)/shard_map/ppermute | solution.py:42
  37.5 1.0 %collective-permute-start.10 = (bf16[4,32,128]{2,1,0:T(8,128)(2,1)S(1)}, bf16[4,32,128]{2,1,0:T(8,128)(2,1)S(1)}, u32[]{:S(2)}, u32[]{:S(2)}) collective-permute-start(bf16[4,32,128]{2,1,0:T(8,128)(2,1)S(1)} %velocities.1), channel_id=1, source_target_pairs={{0,1},{1,0},{2,3},{3,2},{4,5},{5,4},{6,7},{7,6},{8,9},{9,8},{10,11... | collective-permute-start | bytes 98312 | tf_op jit(solution)/shard_map/ppermute | solution.py:42
  38.5 1.3 %collective-permute-done.12 = bf16[4,32,128]{2,1,0:T(8,128)(2,1)S(1)} collective-permute-done((bf16[4,32,128]{2,1,0:T(8,128)(2,1)S(1)}, bf16[4,32,128]{2,1,0:T(8,128)(2,1)S(1)}, u32[]{:S(2)}, u32[]{:S(2)}) %collective-permute-start.12) | collective-permute-done | bytes 32800 | tf_op jit(solution)/shard_map/ppermute | solution.py:42
  39.8 2.5 %collective-permute-done.11 = bf16[4,32,128]{2,1,0:T(8,128)(2,1)S(1)} collective-permute-done((bf16[4,32,128]{2,1,0:T(8,128)(2,1)S(1)}, bf16[4,32,128]{2,1,0:T(8,128)(2,1)S(1)}, u32[]{:S(2)}, u32[]{:S(2)}) %collective-permute-start.11) | collective-permute-done | bytes 32800 | tf_op jit(solution)/shard_map/ppermute | solution.py:42
  43.2 6.0 %helmholtz.2 = (bf16[512,2048]{1,0:T(8,128)(2,1)S(1)}, bf16[512,2048]{1,0:T(8,128)(2,1)S(1)}) custom-call(bf16[64,128]{1,0:T(8,128)(2,1)S(1)} %slice.19.tgt_ref.geo_ref, bf16[4,192,128]{2,1,0:T(8,128)(2,1)S(1)} %pad_maximum_fusion.near_ref.src_ref), custom_call_target="tpu_custom_call" | custom-call | flops 31457280 | bytes 4194304 | tf_op jit(solution)/shard_map/helmholtz/pallas_call | solution.py:255
  49.1 6.0 %helmholtz.3 = (bf16[512,2048]{1,0:T(8,128)(2,1)S(1)}, bf16[512,2048]{1,0:T(8,128)(2,1)S(1)}) custom-call(bf16[64,128]{1,0:T(8,128)(2,1)S(1)} %slice.19.tgt_ref.geo_ref, bf16[4,192,128]{2,1,0:T(8,128)(2,1)S(1)} %collective-permute-done.6.far_ref.src_ref), custom_call_target="tpu_custom_call" | custom-call | flops 31457280 | bytes 4194304 | tf_op jit(solution)/shard_map/helmholtz/pallas_call | solution.py:255
  55.1 1.3 %copy-done.1 = bf16[512,2048]{1,0:T(8,128)(2,1)} copy-done((bf16[512,2048]{1,0:T(8,128)(2,1)}, bf16[512,2048]{1,0:T(8,128)(2,1)S(1)}, u32[]{:S(2)}) %copy-start.1) | copy-done | bytes 2097176
  56.5 1.3 %copy-done.2 = bf16[512,2048]{1,0:T(8,128)(2,1)} copy-done((bf16[512,2048]{1,0:T(8,128)(2,1)}, bf16[512,2048]{1,0:T(8,128)(2,1)S(1)}, u32[]{:S(2)}) %copy-start.2) | copy-done | bytes 2097176
  57.8 5.8 %pressures.1 = (bf16[4,32,128]{2,1,0:T(8,128)(2,1)S(1)}, f32[16,32,128]{2,1,0:T(8,128)S(1)}, bf16[16,32,128]{2,1,0:T(8,128)(2,1)S(1)}) custom-call(s32[5]{0:T(128)S(1)} %stack.53.where, s32[4,8]{1,0:T(4,128)S(1)} %pad_add_fusion.cpl, bf16[4,4,32,128]{3,2,1,0:T(8,128)(2,1)S(1)} %pad_maximum_fusion.1.va_ref, ...), custom_call_target="tpu_custom_call" | custom-call | tf_op jit(solution)/shard_map/pressures/pallas_call | solution.py:333
  65.4 1.0 %collective-permute-done.14.got_ref = bf16[16,32,128]{2,1,0:T(8,128)(2,1)S(1)} collective-permute-done((bf16[16,32,128]{2,1,0:T(8,128)(2,1)S(1)}, bf16[16,32,128]{2,1,0:T(8,128)(2,1)S(1)}, u32[]{:S(2)}, u32[]{:S(2)}) %collective-permute-start.14) | collective-permute-done | bytes 131104 | tf_op jit(solution)/shard_map/ppermute | solution.py:46
  67.0 1.6 %core_sum.1 = (f32[4,32,128]{2,1,0:T(8,128)}, bf16[4,32,128]{2,1,0:T(8,128)(2,1)}, bf16[4,32,128]{2,1,0:T(8,128)(2,1)}, bf16[4,32,128]{2,1,0:T(8,128)(2,1)}) custom-call(f32[16,32,128]{2,1,0:T(8,128)} %copy-done.4, bf16[16,32,128]{2,1,0:T(8,128)(2,1)} %copy-done.14), custom_call_target="tpu_custom_call" | custom-call | tf_op jit(solution)/shard_map/core_sum/pallas_call | solution.py:365
  68.8 2.0 %collective-permute-start.16 = (bf16[4,32,128]{2,1,0:T(8,128)(2,1)}, bf16[4,32,128]{2,1,0:T(8,128)(2,1)S(1)}, u32[]{:S(2)}, u32[]{:S(2)}) collective-permute-start(bf16[4,32,128]{2,1,0:T(8,128)(2,1)} %get-tuple-element.35), channel_id=1, source_target_pairs={{0,2},{1,3},{2,0},{3,1},{4,6},{5,7},{6,4},{7,5},{8,10},{9,11},{10,... | collective-permute-start | bytes 98312 | tf_op jit(solution)/shard_map/ppermute | solution.py:42
  70.7 2.4 %collective-permute-start.17 = (bf16[4,32,128]{2,1,0:T(8,128)(2,1)}, bf16[4,32,128]{2,1,0:T(8,128)(2,1)S(1)}, u32[]{:S(2)}, u32[]{:S(2)}) collective-permute-start(bf16[4,32,128]{2,1,0:T(8,128)(2,1)} %get-tuple-element.36), channel_id=1, source_target_pairs={{0,3},{1,2},{2,1},{3,0},{4,7},{5,6},{6,5},{7,4},{8,11},{9,10},{10,... | collective-permute-start | bytes 98312 | tf_op jit(solution)/shard_map/ppermute | solution.py:42
  73.8 2.9 %collective-permute-done.17.refs_3_ = bf16[4,32,128]{2,1,0:T(8,128)(2,1)S(1)} collective-permute-done((bf16[4,32,128]{2,1,0:T(8,128)(2,1)}, bf16[4,32,128]{2,1,0:T(8,128)(2,1)S(1)}, u32[]{:S(2)}, u32[]{:S(2)}) %collective-permute-start.17) | collective-permute-done | bytes 32800 | tf_op jit(solution)/shard_map/ppermute | solution.py:42
  77.3 1.5 %sec_sum.1 = (f32[2,32,128]{2,1,0:T(8,128)}, bf16[2,32,128]{2,1,0:T(8,128)(2,1)}, bf16[2,32,128]{2,1,0:T(8,128)(2,1)}, bf16[2,32,128]{2,1,0:T(8,128)(2,1)}) custom-call(f32[4,32,128]{2,1,0:T(8,128)} %get-tuple-element.33.refs_0_, bf16[4,32,128]{2,1,0:T(8,128)(2,1)} %copy-done.15, bf16[4,32,128]{2,1,0:T(8,128)(2,1)} %copy-done.16, ...), custom_call_target="tpu_custom_call" | custom-call | tf_op jit(solution)/shard_map/sec_sum/pallas_call | solution.py:384
  79.7 2.6 %collective-permute-start.20 = (bf16[2,32,128]{2,1,0:T(8,128)(2,1)}, bf16[2,32,128]{2,1,0:T(8,128)(2,1)S(1)}, u32[]{:S(2)}, u32[]{:S(2)}) collective-permute-start(bf16[2,32,128]{2,1,0:T(8,128)(2,1)} %get-tuple-element.41), channel_id=1, source_target_pairs={{0,24},{4,28},{8,16},{12,20},{16,8},{20,12},{24,0},{28,4},{1,25},{... | collective-permute-start | bytes 49160 | tf_op jit(solution)/shard_map/ppermute | solution.py:38
  83.2 1.4 %collective-permute-done.20.r3 = bf16[2,32,128]{2,1,0:T(8,128)(2,1)S(1)} collective-permute-done((bf16[2,32,128]{2,1,0:T(8,128)(2,1)}, bf16[2,32,128]{2,1,0:T(8,128)(2,1)S(1)}, u32[]{:S(2)}, u32[]{:S(2)}) %collective-permute-start.20) | collective-permute-done | bytes 16416 | tf_op jit(solution)/shard_map/ppermute | solution.py:38
  85.1 1.6 %outputs.1 = (f32[128,128]{1,0:T(8,128)}, bf16[128,128]{1,0:T(8,128)(2,1)}) custom-call(s32[5]{0:T(128)} %copy-done.7, f32[2,32,128]{2,1,0:T(8,128)} %get-tuple-element.38.r0, bf16[2,32,128]{2,1,0:T(8,128)(2,1)} %copy-done.21, bf16[2,32,128]{2,1,0:T(8,128)(2,1)} %copy-done.22, bf16[2,32,128]{2,1,0:T(8,128)(2,1)} %copy-done.23), custom_call_target="tpu_custom_call" | custom-call | tf_op jit(solution)/shard_map/outputs/pallas_call | solution.py:408
  (76 shorter events, 13.2 us)
Async XLA Ops:
  0.6 29.0 %copy-start.11 = (s32[1,8]{1,0:T(1,128)S(1)}, s32[1,8]{1,0:T(1,128)}, u32[]{:S(2)}) copy-start(s32[1,8]{1,0:T(1,128)} %cpl_ref.1) | copy-start | bytes 100
  0.7 57.0 %copy-start.7 = (s32[5]{0:T(128)}, s32[5]{0:T(128)S(1)}, u32[]{:S(2)}) copy-start(s32[5]{0:T(128)S(1)} %stack.53.where) | copy-start | bytes 64
  0.7 1.6 %copy-start = (bf16[2,256,2048]{2,1,0:T(8,128)(2,1)S(1)}, bf16[2,256,2048]{2,1,0:T(8,128)(2,1)}, u32[]{:S(2)}) copy-start(bf16[2,256,2048]{2,1,0:T(8,128)(2,1)} %r_ref.1) | copy-start | bytes 6291460
  5.4 6.8 %copy-start.13 = (bf16[128,8,128]{2,1,0:T(8,128)(2,1)S(1)}, bf16[128,8,128]{2,1,0:T(8,128)(2,1)}, u32[]{:S(2)}) copy-start(bf16[128,8,128]{2,1,0:T(8,128)(2,1)} %param.8) | copy-start | bytes 786436
  7.6 4.6 %copy-start.6 = (f32[64,128]{1,0:T(8,128)}, f32[64,128]{1,0:T(8,128)S(1)}, u32[]{:S(2)}) copy-start(f32[64,128]{1,0:T(8,128)S(1)} %get-tuple-element.25.own_ref) | copy-start | bytes 98308
  7.6 7.6 %copy-start.8 = (bf16[16,128]{1,0:T(8,128)(2,1)}, bf16[16,128]{1,0:T(8,128)(2,1)S(1)}, u32[]{:S(2)}) copy-start(bf16[16,128]{1,0:T(8,128)(2,1)S(1)} %get-tuple-element.26.geo_ref) | copy-start | bytes 12292
  7.6 8.1 %collective-permute-start = (bf16[80,128]{1,0:T(8,128)(2,1)S(1)}, bf16[80,128]{1,0:T(8,128)(2,1)S(1)}, u32[]{:S(2)}, u32[]{:S(2)}) collective-permute-start(bf16[80,128]{1,0:T(8,128)(2,1)S(1)} %get-tuple-element.22), channel_id=1, source_target_pairs={{0,16},{4,20},{8,24},{12,28},{16,0},{20,4},{24,8},{28,12},{1,17},{... | collective-permute-start | bytes 61448 | tf_op jit(solution)/shard_map/ppermute | solution.py:38
  10.6 5.1 %collective-permute-start.1 = (bf16[80,128]{1,0:T(8,128)(2,1)S(1)}, bf16[80,128]{1,0:T(8,128)(2,1)S(1)}, u32[]{:S(2)}, u32[]{:S(2)}) collective-permute-start(bf16[80,128]{1,0:T(8,128)(2,1)S(1)} %get-tuple-element.23), channel_id=1, source_target_pairs={{0,8},{4,12},{8,0},{12,4},{16,24},{20,28},{24,16},{28,20},{1,9},{5... | collective-permute-start | bytes 61448 | tf_op jit(solution)/shard_map/ppermute | solution.py:38
  12.2 5.0 %collective-permute-start.2 = (bf16[80,128]{1,0:T(8,128)(2,1)S(1)}, bf16[80,128]{1,0:T(8,128)(2,1)S(1)}, u32[]{:S(2)}, u32[]{:S(2)}) collective-permute-start(bf16[80,128]{1,0:T(8,128)(2,1)S(1)} %get-tuple-element.24), channel_id=1, source_target_pairs={{0,24},{4,28},{8,16},{12,20},{16,8},{20,12},{24,0},{28,4},{1,25},{... | collective-permute-start | bytes 61448 | tf_op jit(solution)/shard_map/ppermute | solution.py:38
  12.2 17.4 %collective-permute-start.9 = (bf16[128,1024]{1,0:T(8,128)(2,1)S(1)}, bf16[128,1024]{1,0:T(8,128)(2,1)S(1)}, u32[]{:S(2)}, u32[]{:S(2)}) collective-permute-start(bf16[128,1024]{1,0:T(8,128)(2,1)S(1)} %bitcast.18), channel_id=1, source_target_pairs={{0,24},{4,28},{8,16},{12,20},{16,8},{20,12},{24,0},{28,4},{1,25},{... | collective-permute-start | bytes 786440 | tf_op jit(solution)/shard_map/ppermute | solution.py:38
  15.2 14.4 %collective-permute-start.8 = (bf16[128,1024]{1,0:T(8,128)(2,1)S(1)}, bf16[128,1024]{1,0:T(8,128)(2,1)S(1)}, u32[]{:S(2)}, u32[]{:S(2)}) collective-permute-start(bf16[128,1024]{1,0:T(8,128)(2,1)S(1)} %bitcast.19), channel_id=1, source_target_pairs={{0,8},{4,12},{8,0},{12,4},{16,24},{20,28},{24,16},{28,20},{1,9},{5... | collective-permute-start | bytes 786440 | tf_op jit(solution)/shard_map/ppermute | solution.py:38
  15.7 1.5 %copy-start.19 = (bf16[80,128]{1,0:T(8,128)(2,1)}, bf16[80,128]{1,0:T(8,128)(2,1)S(1)}, u32[]{:S(2)}) copy-start(bf16[80,128]{1,0:T(8,128)(2,1)S(1)} %collective-permute-done.x_ref) | copy-start | bytes 61444
  15.7 1.5 %copy-start.20 = (bf16[80,128]{1,0:T(8,128)(2,1)}, bf16[80,128]{1,0:T(8,128)(2,1)S(1)}, u32[]{:S(2)}) copy-start(bf16[80,128]{1,0:T(8,128)(2,1)S(1)} %collective-permute-done.1.y_ref) | copy-start | bytes 61444
  19.2 6.3 %collective-permute-start.5 = (bf16[192,128]{1,0:T(8,128)(2,1)}, bf16[192,128]{1,0:T(8,128)(2,1)S(1)}, u32[]{:S(2)}, u32[]{:S(2)}) collective-permute-start(bf16[192,128]{1,0:T(8,128)(2,1)} %amplitude_sum.1), channel_id=1, source_target_pairs={{0,3},{1,2},{2,1},{3,0},{4,7},{5,6},{6,5},{7,4},{8,11},{9,10},{10,... | collective-permute-start | bytes 147464 | tf_op jit(solution)/shard_map/ppermute | solution.py:42
  22.8 5.2 %collective-permute-start.4 = (bf16[192,128]{1,0:T(8,128)(2,1)}, bf16[192,128]{1,0:T(8,128)(2,1)S(1)}, u32[]{:S(2)}, u32[]{:S(2)}) collective-permute-start(bf16[192,128]{1,0:T(8,128)(2,1)} %amplitude_sum.1), channel_id=1, source_target_pairs={{0,2},{1,3},{2,0},{3,1},{4,6},{5,7},{6,4},{7,5},{8,10},{9,11},{10,... | collective-permute-start | bytes 147464 | tf_op jit(solution)/shard_map/ppermute | solution.py:42
  22.8 5.2 %collective-permute-start.3 = (bf16[192,128]{1,0:T(8,128)(2,1)}, bf16[192,128]{1,0:T(8,128)(2,1)S(1)}, u32[]{:S(2)}, u32[]{:S(2)}) collective-permute-start(bf16[192,128]{1,0:T(8,128)(2,1)} %amplitude_sum.1), channel_id=1, source_target_pairs={{0,1},{1,0},{2,3},{3,2},{4,5},{5,4},{6,7},{7,6},{8,9},{9,8},{10,11... | collective-permute-start | bytes 147464 | tf_op jit(solution)/shard_map/ppermute | solution.py:42
  25.5 6.4 %collective-permute-start.7 = (bf16[128,1024]{1,0:T(8,128)(2,1)S(1)}, bf16[128,1024]{1,0:T(8,128)(2,1)S(1)}, u32[]{:S(2)}, u32[]{:S(2)}) collective-permute-start(bf16[128,1024]{1,0:T(8,128)(2,1)S(1)} %bitcast.20), channel_id=1, source_target_pairs={{0,16},{4,20},{8,24},{12,28},{16,0},{20,4},{24,8},{28,12},{1,17},{... | collective-permute-start | bytes 786440 | tf_op jit(solution)/shard_map/ppermute | solution.py:38
  28.8 3.0 %collective-permute-start.6 = (bf16[4,192,128]{2,1,0:T(8,128)(2,1)S(1)}, bf16[4,192,128]{2,1,0:T(8,128)(2,1)S(1)}, u32[]{:S(2)}, u32[]{:S(2)}) collective-permute-start(bf16[4,192,128]{2,1,0:T(8,128)(2,1)S(1)} %pad_maximum_fusion.near_ref.src_ref), channel_id=1, source_target_pairs={{0,4},{4,0},{8,12},{12,8},{1,5},{5,1},{9,13},{13,9},{2,6},{6,2},{1... | collective-permute-start | bytes 589832 | tf_op jit(solution)/shard_map/ppermute | solution.py:46
  34.1 5.7 %collective-permute-start.12 = (bf16[4,32,128]{2,1,0:T(8,128)(2,1)S(1)}, bf16[4,32,128]{2,1,0:T(8,128)(2,1)S(1)}, u32[]{:S(2)}, u32[]{:S(2)}) collective-permute-start(bf16[4,32,128]{2,1,0:T(8,128)(2,1)S(1)} %velocities.1), channel_id=1, source_target_pairs={{0,3},{1,2},{2,1},{3,0},{4,7},{5,6},{6,5},{7,4},{8,11},{9,10},{10,... | collective-permute-start | bytes 98312 | tf_op jit(solution)/shard_map/ppermute | solution.py:42
  37.5 4.8 %collective-permute-start.11 = (bf16[4,32,128]{2,1,0:T(8,128)(2,1)S(1)}, bf16[4,32,128]{2,1,0:T(8,128)(2,1)S(1)}, u32[]{:S(2)}, u32[]{:S(2)}) collective-permute-start(bf16[4,32,128]{2,1,0:T(8,128)(2,1)S(1)} %velocities.1), channel_id=1, source_target_pairs={{0,2},{1,3},{2,0},{3,1},{4,6},{5,7},{6,4},{7,5},{8,10},{9,11},{10,... | collective-permute-start | bytes 98312 | tf_op jit(solution)/shard_map/ppermute | solution.py:42
  37.5 4.8 %collective-permute-start.10 = (bf16[4,32,128]{2,1,0:T(8,128)(2,1)S(1)}, bf16[4,32,128]{2,1,0:T(8,128)(2,1)S(1)}, u32[]{:S(2)}, u32[]{:S(2)}) collective-permute-start(bf16[4,32,128]{2,1,0:T(8,128)(2,1)S(1)} %velocities.1), channel_id=1, source_target_pairs={{0,1},{1,0},{2,3},{3,2},{4,5},{5,4},{6,7},{7,6},{8,9},{9,8},{10,11... | collective-permute-start | bytes 98312 | tf_op jit(solution)/shard_map/ppermute | solution.py:42
  42.4 15.4 %collective-permute-start.13 = (bf16[4,4,32,128]{3,2,1,0:T(8,128)(2,1)S(1)}, bf16[4,4,32,128]{3,2,1,0:T(8,128)(2,1)S(1)}, u32[]{:S(2)}, u32[]{:S(2)}) collective-permute-start(bf16[4,4,32,128]{3,2,1,0:T(8,128)(2,1)S(1)} %pad_maximum_fusion.1.va_ref), channel_id=1, source_target_pairs={{0,4},{4,0},{8,12},{12,8},{1,5},{5,1},{9,13},{13,9},{2,6},{6,2},{1... | collective-permute-start | bytes 393224 | tf_op jit(solution)/shard_map/ppermute | solution.py:46
  64.9 1.5 %collective-permute-start.14 = (bf16[16,32,128]{2,1,0:T(8,128)(2,1)S(1)}, bf16[16,32,128]{2,1,0:T(8,128)(2,1)S(1)}, u32[]{:S(2)}, u32[]{:S(2)}) collective-permute-start(bf16[16,32,128]{2,1,0:T(8,128)(2,1)S(1)} %get-tuple-element.32), channel_id=1, source_target_pairs={{0,4},{4,0},{8,12},{12,8},{1,5},{5,1},{9,13},{13,9},{2,6},{6,2},{1... | collective-permute-start | bytes 393224 | tf_op jit(solution)/shard_map/ppermute | solution.py:46
  68.7 4.4 %collective-permute-start.15 = (bf16[4,32,128]{2,1,0:T(8,128)(2,1)}, bf16[4,32,128]{2,1,0:T(8,128)(2,1)S(1)}, u32[]{:S(2)}, u32[]{:S(2)}) collective-permute-start(bf16[4,32,128]{2,1,0:T(8,128)(2,1)} %get-tuple-element.34), channel_id=1, source_target_pairs={{0,1},{1,0},{2,3},{3,2},{4,5},{5,4},{6,7},{7,6},{8,9},{9,8},{10,11... | collective-permute-start | bytes 98312 | tf_op jit(solution)/shard_map/ppermute | solution.py:42
  68.8 5.0 %collective-permute-start.16 = (bf16[4,32,128]{2,1,0:T(8,128)(2,1)}, bf16[4,32,128]{2,1,0:T(8,128)(2,1)S(1)}, u32[]{:S(2)}, u32[]{:S(2)}) collective-permute-start(bf16[4,32,128]{2,1,0:T(8,128)(2,1)} %get-tuple-element.35), channel_id=1, source_target_pairs={{0,2},{1,3},{2,0},{3,1},{4,6},{5,7},{6,4},{7,5},{8,10},{9,11},{10,... | collective-permute-start | bytes 98312 | tf_op jit(solution)/shard_map/ppermute | solution.py:42
  70.7 5.9 %collective-permute-start.17 = (bf16[4,32,128]{2,1,0:T(8,128)(2,1)}, bf16[4,32,128]{2,1,0:T(8,128)(2,1)S(1)}, u32[]{:S(2)}, u32[]{:S(2)}) collective-permute-start(bf16[4,32,128]{2,1,0:T(8,128)(2,1)} %get-tuple-element.36), channel_id=1, source_target_pairs={{0,3},{1,2},{2,1},{3,0},{4,7},{5,6},{6,5},{7,4},{8,11},{9,10},{10,... | collective-permute-start | bytes 98312 | tf_op jit(solution)/shard_map/ppermute | solution.py:42
  73.1 3.6 %copy-start.15 = (bf16[4,32,128]{2,1,0:T(8,128)(2,1)}, bf16[4,32,128]{2,1,0:T(8,128)(2,1)S(1)}, u32[]{:S(2)}) copy-start(bf16[4,32,128]{2,1,0:T(8,128)(2,1)S(1)} %collective-permute-done.15.refs_1_) | copy-start | bytes 98308
  73.8 2.9 %copy-start.16 = (bf16[4,32,128]{2,1,0:T(8,128)(2,1)}, bf16[4,32,128]{2,1,0:T(8,128)(2,1)S(1)}, u32[]{:S(2)}) copy-start(bf16[4,32,128]{2,1,0:T(8,128)(2,1)S(1)} %collective-permute-done.16.refs_2_) | copy-start | bytes 98308
  78.8 3.9 %collective-permute-start.18 = (bf16[2,32,128]{2,1,0:T(8,128)(2,1)}, bf16[2,32,128]{2,1,0:T(8,128)(2,1)S(1)}, u32[]{:S(2)}, u32[]{:S(2)}) collective-permute-start(bf16[2,32,128]{2,1,0:T(8,128)(2,1)} %get-tuple-element.39), channel_id=1, source_target_pairs={{0,16},{4,20},{8,24},{12,28},{16,0},{20,4},{24,8},{28,12},{1,17},{... | collective-permute-start | bytes 49160 | tf_op jit(solution)/shard_map/ppermute | solution.py:38
  79.2 3.9 %collective-permute-start.19 = (bf16[2,32,128]{2,1,0:T(8,128)(2,1)}, bf16[2,32,128]{2,1,0:T(8,128)(2,1)S(1)}, u32[]{:S(2)}, u32[]{:S(2)}) collective-permute-start(bf16[2,32,128]{2,1,0:T(8,128)(2,1)} %get-tuple-element.40), channel_id=1, source_target_pairs={{0,8},{4,12},{8,0},{12,4},{16,24},{20,28},{24,16},{28,20},{1,9},{5... | collective-permute-start | bytes 49160 | tf_op jit(solution)/shard_map/ppermute | solution.py:38
  79.7 4.8 %collective-permute-start.20 = (bf16[2,32,128]{2,1,0:T(8,128)(2,1)}, bf16[2,32,128]{2,1,0:T(8,128)(2,1)S(1)}, u32[]{:S(2)}, u32[]{:S(2)}) collective-permute-start(bf16[2,32,128]{2,1,0:T(8,128)(2,1)} %get-tuple-element.41), channel_id=1, source_target_pairs={{0,24},{4,28},{8,16},{12,20},{16,8},{20,12},{24,0},{28,4},{1,25},{... | collective-permute-start | bytes 49160 | tf_op jit(solution)/shard_map/ppermute | solution.py:38
  82.8 1.8 %copy-start.21 = (bf16[2,32,128]{2,1,0:T(8,128)(2,1)}, bf16[2,32,128]{2,1,0:T(8,128)(2,1)S(1)}, u32[]{:S(2)}) copy-start(bf16[2,32,128]{2,1,0:T(8,128)(2,1)S(1)} %collective-permute-done.18.r1) | copy-start | bytes 49156
  (13 other events, 10.9 us)

commit v2 on v0

--- a/solution.py
+++ b/solution.py
@@ -1,11 +1,475 @@
+import functools
 import math
 
 import jax
 import jax.numpy as jnp
+import numpy as np
 from jax import lax
+from jax.experimental import pallas as pl
+from jax.experimental.pallas import tpu as pltpu
 from jax.sharding import PartitionSpec as P
 
 wave_number = 40.0
+turns = wave_number / (2.0 * math.pi)
+bf16 = jnp.bfloat16
+f32 = jnp.float32
+AXES = ("blk", "tgt", "sec")
+GEO = 16
+
+
+def fit(values, terms):
+    nodes = 0.125 + 0.125 * np.cos(np.pi * (np.arange(400) + 0.5) / 400)
+    matrix = np.vander(nodes, terms, increasing=True)
+    return [float(c) for c in np.linalg.lstsq(matrix, values(nodes), rcond=None)[0]]
+
+
+sin_terms = fit(lambda u: math.sqrt(2.0) * np.sin(np.pi * np.sqrt(u)) / np.sqrt(u), 4)
+cos_terms = fit(lambda u: math.sqrt(2.0) * np.cos(np.pi * np.sqrt(u)), 4)
+
+
+def exchange_plane(x, mask):
+    nb, nt = lax.axis_size("blk"), lax.axis_size("tgt")
+    pairs = [
+        (b * nt + t, (b ^ (mask & 1)) * nt + (t ^ (2 * (mask >> 1))))
+        for b in range(nb)
+        for t in range(nt)
+    ]
+    return lax.ppermute(x, ("blk", "tgt"), pairs)
+
+
+def exchange_sec(x, mask):
+    return lax.ppermute(x, "sec", [(s, s ^ mask) for s in range(lax.axis_size("sec"))])
+
+
+def exchange_core(x):
+    return lax.ppermute(x, "tgt", [(t, t ^ 1) for t in range(lax.axis_size("tgt"))])
+
+
+VMEM = pl.BlockSpec(memory_space=pltpu.VMEM)
+SMEM = pl.BlockSpec(memory_space=pltpu.SMEM)
+HBM = pl.BlockSpec(memory_space=pltpu.HBM)
+
+
+def place():
+    t = lax.axis_index("tgt")
+    return lax.axis_index("blk"), t >> 1, t & 1, lax.axis_index("sec")
+
+
+def limit(mib):
+    return pltpu.CompilerParams(vmem_limit_bytes=mib << 20)
+
+
+def bits_of(n):
+    return n.bit_length() - 1
+
+
+def three_parts(x):
+    first = x.astype(bf16).astype(f32)
+    rest = x - first
+    second = rest.astype(bf16).astype(f32)
+    return first, second, rest - second
+
+
+def amplitude_kernel(panels, r_hbm, l_hbm, xyz_hbm, area_hbm, cpl_hbm, own_ref, s1_ref, s2_ref, s3_ref, geo_ref, r_buf, l_buf, xyz, areas, cpl, amp_t, geo, sems):
+    rows, lanes = r_buf.shape[1], 128
+    blocks = rows // lanes
+    small = [
+        pltpu.make_async_copy(s, d, sems.at[i])
+        for i, (s, d) in enumerate(((xyz_hbm, xyz), (area_hbm, areas), (cpl_hbm, cpl)))
+    ]
+    fetch_loads = pltpu.make_async_copy(l_hbm, l_buf, sems.at[3])
+    fetch = [
+        pltpu.make_async_copy(r_hbm.at[:, b * lanes : (b + 1) * lanes, :], r_buf.at[:, b * lanes : (b + 1) * lanes, :], sems.at[4 + b])
+        for b in range(blocks)
+    ]
+    for copy in [fetch_loads] + fetch + small:
+        copy.start()
+    for copy in small:
+        copy.wait()
+    scaled = (xyz[...] - 0.5) * turns
+    area = areas[...]
+    norm = jnp.sum(scaled * scaled, axis=0, keepdims=True) + area * (turns * turns / panels)
+    geo[...] = jnp.zeros_like(geo)
+    for i, part in enumerate(three_parts(scaled)):
+        geo[3 * i : 3 * i + 3, :] = part
+    for i, part in enumerate(three_parts(norm)):
+        geo[9 + i : 10 + i, :] = part
+    for i, part in enumerate(three_parts(area)):
+        geo[12 + i : 13 + i, :] = part
+    geo[15:16, 0 : cpl.shape[1]] = cpl[...].astype(f32)
+    packed = geo[...].astype(bf16)
+    geo_ref[...] = packed
+    for out in (s1_ref, s2_ref, s3_ref):
+        out[out.shape[0] - GEO :, :] = packed
+
+    width = l_buf.shape[1]
+    half = width // 2
+    quarter = half // 4
+    x, y, _, _ = place()
+    mine = x + 2 * y
+    fetch_loads.wait()
+    for b in range(blocks):
+        fetch[b].wait()
+        span = slice(b * lanes, (b + 1) * lanes)
+        both = jnp.dot(r_buf[:, span, :].reshape(2 * lanes, r_buf.shape[2]), l_buf[...], preferred_element_type=f32)
+        turned = pltpu.roll(both[lanes:], half, 1)
+        lane = lax.broadcasted_iota(jnp.int32, turned.shape, 1)
+        amp_t[...] = (both[:lanes] + jnp.where(lane < half, -turned, turned)).T
+        for mask, out in enumerate((own_ref, s1_ref, s2_ref, s3_ref)):
+            at = pl.multiple_of((mine ^ mask) * quarter, quarter)
+            for part in range(2):
+                r0 = (2 * b + part) * quarter
+                out[r0 : r0 + quarter, :] = amp_t[pl.ds(part * half + at, quarter), :].astype(out.dtype)
+
+
+def amplitude_parts(panels, receptance, loads, xyz, area, coupling):
+    _, rows, depth = receptance.shape
+    width = loads.shape[1]
+    blocks = rows // 128
+    chunk = blocks * (width // 4)
+    outs = [((chunk, 128), f32)] + [((chunk + GEO, 128), bf16)] * 3 + [((GEO, 128), bf16)]
+    return pl.pallas_call(
+        functools.partial(amplitude_kernel, panels),
+        in_specs=[HBM] * 5,
+        out_specs=[VMEM] * len(outs),
+        out_shape=[jax.ShapeDtypeStruct(s, d) for s, d in outs],
+        scratch_shapes=[
+            pltpu.VMEM(receptance.shape, bf16),
+            pltpu.VMEM(loads.shape, bf16),
+            pltpu.VMEM(xyz.shape, f32),
+            pltpu.VMEM(area.shape, f32),
+            pltpu.VMEM(coupling.shape, jnp.int32),
+            pltpu.VMEM((width, 128), f32),
+            pltpu.VMEM((GEO, 128), f32),
+            pltpu.SemaphoreType.DMA((4 + blocks,)),
+        ],
+        compiler_params=limit(12),
+        cost_estimate=pl.CostEstimate(flops=4 * rows * depth * width, bytes_accessed=4 * rows * depth, transcendentals=0),
+        name="amplitude_parts",
+    )(receptance, loads, xyz, area, coupling)
+
+
+def amplitude_sum_kernel(own_ref, geo_ref, x_ref, y_ref, d_ref, out_ref, cpl_ref):
+    n = own_ref.shape[0]
+    out_ref[0:n, :] = (own_ref[...] + x_ref[0:n, :].astype(f32)).astype(bf16)
+    out_ref[n : 2 * n, :] = (y_ref[0:n, :].astype(f32) + d_ref[0:n, :].astype(f32)).astype(bf16)
+    geos = [geo_ref[...]] + [r[n:, :] for r in (x_ref, y_ref, d_ref)]
+    for i, g in enumerate(geos):
+        out_ref[2 * n + GEO * i : 2 * n + GEO * (i + 1), :] = g
+        cpl_ref[i : i + 1, :] = g.astype(f32)[GEO - 1 :, :].astype(jnp.int32)
+
+
+def amplitude_sum(own, geo, x, y, d):
+    n = own.shape[0]
+    return pl.pallas_call(
+        amplitude_sum_kernel,
+        in_specs=[VMEM] * 5,
+        out_specs=[VMEM] * 2,
+        out_shape=[jax.ShapeDtypeStruct((2 * n + 4 * GEO, 128), bf16), jax.ShapeDtypeStruct((4, 128), jnp.int32)],
+        compiler_params=limit(4),
+        name="amplitude_sum",
+    )(own, geo, x, y, d)
+
+
+def stack_kernel(*refs):
+    for i, r in enumerate(refs[:-1]):
+        refs[-1][i] = r[...]
+
+
+def stack(parts):
+    return pl.pallas_call(
+        stack_kernel,
+        in_specs=[VMEM] * len(parts),
+        out_specs=VMEM,
+        out_shape=jax.ShapeDtypeStruct((len(parts),) + parts[0].shape, parts[0].dtype),
+        compiler_params=limit(4),
+        name="stack",
+    )(*parts)
+
+
+def velocity_kernel(width, blocks, scale, secs, cpl, *refs):
+    near, far_ref = refs[0:secs], refs[secs]
+    modes, out_ref, table, picked = refs[secs + 1 : secs + 5], refs[-3], refs[-2], refs[-1]
+    _, y, c, z = place()
+    used = 2 * blocks * width
+    for i in range(secs):
+        table[0, i] = near[i][0:used, :]
+        table[1, i] = far_ref[i, 0:used, :]
+    sec_bits, block_bits = bits_of(secs), bits_of(blocks)
+    count = modes[0].shape[1] // 128
+    for j, m_ref in enumerate(modes):
+        for k in range(count):
+            b = cpl[j, k]
+            h = b & (blocks - 1)
+            s = (b >> block_bits) & (secs - 1)
+            t = b >> (block_bits + sec_bits)
+            row = pl.multiple_of((((((t >> 1) ^ y) << block_bits) + h) * width), width)
+            picked[j, :, k * 128 : (k + 1) * 128] = table[(t & 1) ^ c, s ^ z, pl.ds(row, width), :]
+    for j, m_ref in enumerate(modes):
+        vel = lax.dot_general(picked[j], m_ref[...], (((1,), (1,)), ((), ())), preferred_element_type=f32)
+        g = near[0][used + GEO * j : used + GEO * (j + 1), :].astype(f32)
+        area = (g[12:13] + g[13:14] + g[14:15]) * scale
+        out_ref[j] = (vel * area).astype(bf16)
+
+
+def velocities(panels, cpl, near, far, modes, width, blocks):
+    count, depth = modes[0].shape
+    secs = len(near)
+    return pl.pallas_call(
+        functools.partial(velocity_kernel, width, blocks, turns / math.sqrt(panels), secs),
+        in_specs=[SMEM] + [VMEM] * (secs + 5),
+        out_specs=VMEM,
+        out_shape=jax.ShapeDtypeStruct((4, width, count), bf16),
+        scratch_shapes=[
+            pltpu.VMEM((2, secs, 2 * blocks * width, 128), bf16),
+            pltpu.VMEM((4, width, depth), bf16),
+        ],
+        compiler_params=limit(6),
+        name="velocities",
+    )(cpl, *near, far, *modes)
+
+
+def target_kernel(panels, tgt_ref, out_ref, mat):
+    lanes = tgt_ref.shape[1]
+    mat[...] = jnp.zeros_like(mat)
+    for j in range(tgt_ref.shape[0] // GEO):
+        g = tgt_ref[j * GEO : (j + 1) * GEO, :].astype(f32)
+        area = g[12:13] + g[13:14] + g[14:15]
+        norm = g[9:10] + g[10:11] + g[11:12] - area * (turns * turns / panels)
+        col = slice(j * lanes, (j + 1) * lanes)
+        for a in range(3):
+            for b in range(3):
+                mat[GEO * a + 3 * b : GEO * a + 3 * b + 3, col] = -2.0 * g[3 * a : 3 * a + 3]
+        mat[9:12, col] = jnp.ones((3, lanes), f32)
+        for i, part in enumerate(three_parts(norm)):
+            mat[3 * GEO + i : 3 * GEO + i + 1, col] = part
+    out_ref[...] = mat[...].T.astype(bf16)
+
+
+def target_matrix(panels, geo):
+    side = geo.shape[0] // GEO * geo.shape[1]
+    return pl.pallas_call(
+        functools.partial(target_kernel, panels),
+        in_specs=[VMEM],
+        out_specs=VMEM,
+        out_shape=jax.ShapeDtypeStruct((side, 4 * GEO), bf16),
+        scratch_shapes=[pltpu.VMEM((4 * GEO, side), f32)],
+        compiler_params=limit(4),
+        name="target_matrix",
+    )(geo)
+
+
+def helmholtz_kernel(at, tgt_ref, src_ref, re_ref, im_ref, dist):
+    src = src_ref if at is None else src_ref.at[at]
+    side = tgt_ref.shape[0]
+    first = src.shape[0] - side // 128 * GEO
+    wide = jnp.concatenate([src[first + j * GEO : first + (j + 1) * GEO, :] for j in range(side // 128)], axis=1)
+    full = jnp.concatenate([wide, wide, wide, jnp.ones_like(wide)], axis=0)
+    dist[...] = jnp.dot(tgt_ref[...], full, preferred_element_type=f32)
+    strip, span = 16, 256
+    c0, c1, c2 = (c / cos_terms[3] for c in cos_terms[:3])
+
+    def step(i, _):
+        rows = pl.ds(pl.multiple_of(i * strip, strip), strip)
+        for n in range(side // span):
+            cols = slice(n * span, (n + 1) * span)
+            square = dist[rows, cols]
+            inverse = lax.rsqrt(square)
+            t = square * inverse
+            f = t - jnp.round(t)
+            u = f * f
+            s = (((sin_terms[3] * u + sin_terms[2]) * u + sin_terms[1]) * u + sin_terms[0]) * f
+            c = ((u + c2) * u + c1) * u + c0
+            part = s * inverse
+            re_ref[rows, cols] = (inverse - s * part).astype(bf16)
+            im_ref[rows, cols] = (c * part).astype(bf16)
+        return 0
+
+    lax.fori_loop(0, side // strip, step, 0, unroll=4)
+
+
+def helmholtz(targets, payload, at=None):
+    side = targets.shape[0]
+    return pl.pallas_call(
+        functools.partial(helmholtz_kernel, at),
+        in_specs=[VMEM] * 2,
+        out_specs=[VMEM] * 2,
+        out_shape=[jax.ShapeDtypeStruct((side, side), bf16)] * 2,
+        scratch_shapes=[pltpu.VMEM((side, side), f32)],
+        compiler_params=limit(4),
+        cost_estimate=pl.CostEstimate(flops=4096 * side * side, bytes_accessed=4 * side * side, transcendentals=side * side),
+        name="helmholtz",
+    )(targets, payload)
+
+
+def pressure_kernel(secs, tgt_n, cpl, *refs):
+    v_near, v_far = refs[0:secs], refs[secs]
+    mats = refs[secs + 1 : 5 * secs + 1]
+    geo_ref, modes = refs[5 * secs + 1], refs[5 * secs + 2 : 5 * secs + 6]
+    pt_ref, near_ref, far_ref, lead, turned, total = refs[5 * secs + 6 :]
+    groups, width, lanes = v_near[0].shape
+    half = width // 2
+    side = groups * lanes
+    for i in range(2 * secs):
+        for j in range(groups):
+            v = v_near[i][j] if i < secs else v_far[i - secs, j]
+            col = slice(i * side + j * lanes, i * side + (j + 1) * lanes)
+            lead[:, col] = v
+            turned[0:half, col] = -v[half:]
+            turned[half:, col] = v[0:half]
+    dims = (((1,), (1,)), ((), ()))
+    re = im = 0.0
+    for i in range(2 * secs):
+        col = slice(i * side, (i + 1) * side)
+        re += lax.dot_general(mats[2 * i][...], lead[:, col], dims, preferred_element_type=f32)
+        im += lax.dot_general(mats[2 * i + 1][...], turned[:, col], dims, preferred_element_type=f32)
+    p = (re + im * cos_terms[3]).T.astype(bf16)
+    total[...] = jnp.zeros_like(total)
+    x, y, c, z = place()
+    sec_bits, tgt_bits = bits_of(secs), bits_of(tgt_n)
+    for j, m_ref in enumerate(modes):
+        pj = p[:, j * lanes : (j + 1) * lanes]
+        pt_ref[j] = pj
+        g = geo_ref[j * GEO : (j + 1) * GEO, :].astype(f32)
+        weighted = (pj.astype(f32) * (g[12:13] + g[13:14] + g[14:15])).astype(bf16)
+        terms = jnp.dot(weighted, m_ref[...], preferred_element_type=f32)
+        for k in range(m_ref.shape[1] // lanes):
+            b = cpl[j, k]
+            s = b & (secs - 1)
+            t = (b >> sec_bits) & (tgt_n - 1)
+            xb = b >> (sec_bits + tgt_bits)
+            at = ((((t & 1) ^ c) * secs + (s ^ z)) * groups) + (xb ^ x) + 2 * ((t >> 1) ^ y)
+            total[at] += terms[:, k * lanes : (k + 1) * lanes]
+    n = near_ref.shape[0]
+    near_ref[...] = total[0:n]
+    far_ref[...] = total[n:].astype(bf16)
+
+
+def pressures(cpl, v_near, v_far, mats, geo, modes, tgt_n):
+    secs = len(v_near)
+    groups, width, lanes = v_near[0].shape
+    side = groups * lanes
+    n = secs * groups
+    args = [*v_near, v_far, *mats, geo, *modes]
+    return pl.pallas_call(
+        functools.partial(pressure_kernel, secs, tgt_n),
+        in_specs=[SMEM] + [VMEM] * len(args),
+        out_specs=[VMEM] * 3,
+        out_shape=[
+            jax.ShapeDtypeStruct((groups, width, lanes), bf16),
+            jax.ShapeDtypeStruct((n, width, lanes), f32),
+            jax.ShapeDtypeStruct((n, width, lanes), bf16),
+        ],
+        scratch_shapes=[
+            pltpu.VMEM((width, 2 * secs * side), bf16),
+            pltpu.VMEM((width, 2 * secs * side), bf16),
+            pltpu.VMEM((2 * n, width, lanes), f32),
+        ],
+        compiler_params=limit(8),
+        name="pressures",
+    )(cpl, *args)
+
+
+def core_sum_kernel(near_ref, got_ref, own_ref, *send):
+    groups = own_ref.shape[0]
+    own_ref[...] = near_ref[0:groups] + got_ref[0:groups].astype(f32)
+    for i, s in enumerate(send):
+        r = slice((i + 1) * groups, (i + 2) * groups)
+        s[...] = (near_ref[r] + got_ref[r].astype(f32)).astype(bf16)
+
+
+def core_sum(near, got, secs):
+    groups = near.shape[0] // secs
+    shape = (groups,) + near.shape[1:]
+    return pl.pallas_call(
+        core_sum_kernel,
+        in_specs=[VMEM] * 2,
+        out_specs=[VMEM] * secs,
+        out_shape=[jax.ShapeDtypeStruct(shape, f32)] + [jax.ShapeDtypeStruct(shape, bf16)] * (secs - 1),
+        compiler_params=limit(4),
+        name="core_sum",
+    )(near, got)
+
+
+def sec_sum_kernel(count, *refs):
+    own, got, pt, outs = refs[0], refs[1 : 1 + count], refs[1 + count], refs[2 + count :]
+    for j, out in enumerate(outs):
+        value = own[j]
+        for g in got:
+            value = value + g[j].astype(f32)
+        out[0] = value.astype(out.dtype)
+        out[1] = pt[j].astype(out.dtype)
+
+
+def sec_sum(own, got, pt):
+    shape = (2,) + own.shape[1:]
+    return pl.pallas_call(
+        functools.partial(sec_sum_kernel, len(got)),
+        in_specs=[VMEM] * (2 + len(got)),
+        out_specs=[VMEM] * 4,
+        out_shape=[jax.ShapeDtypeStruct(shape, f32)] + [jax.ShapeDtypeStruct(shape, bf16)] * 3,
+        compiler_params=limit(4),
+        name="sec_sum",
+    )(own, *got, pt)
+
+
+def output_kernel(r0, r1, r2, r3, loads_ref, press_ref, loads_t, press_t):
+    half = loads_t.shape[0] // 2
+    quarter = half // 4
+    x, y, _, _ = place()
+    for mask, r in enumerate((r0, r1, r2, r3)):
+        at = pl.multiple_of(((x + 2 * y) ^ mask) * quarter, quarter)
+        for part in range(2):
+            rows = pl.ds(part * half + at, quarter)
+            loads_t[rows, :] = r[0, part * quarter : (part + 1) * quarter, :].astype(f32)
+            press_t[rows, :] = r[1, part * quarter : (part + 1) * quarter, :].astype(f32)
+    loads_ref[...] = loads_t[...].T
+    press_ref[...] = press_t[...].T.astype(bf16)
+
+
+def outputs(parts):
+    _, width, lanes = parts[0].shape
+    cols = 4 * width
+    return pl.pallas_call(
+        output_kernel,
+        in_specs=[VMEM] * 4,
+        out_shape=[jax.ShapeDtypeStruct((lanes, cols), f32), jax.ShapeDtypeStruct((lanes, cols), bf16)],
+        scratch_shapes=[pltpu.VMEM((cols, lanes), f32)] * 2,
+        compiler_params=limit(4),
+        name="outputs",
+    )(*parts)
+
+
+def on_device_fast(modal_loads, receptance, shapes, coupling, panel_coords, panel_areas):
+    secs, tgts = lax.axis_size("sec"), lax.axis_size("tgt")
+    device_count = lax.axis_size("blk") * tgts * secs
+    pan_dev = panel_coords.shape[1]
+    panels = float(pan_dev * device_count)
+    width = modal_loads.shape[1] // 4
+    blocks = receptance.shape[1] // shapes.shape[2]
+
+    own, s1, s2, s3, geo = amplitude_parts(
+        panels, receptance, modal_loads, panel_coords, panel_areas[None, :], coupling
+    )
+    got = [exchange_plane(s, m) for m, s in ((1, s1), (2, s2), (3, s3))]
+    flat = shapes.reshape(pan_dev, -1)
+    modes = [flat] + [exchange_plane(flat, m) for m in (1, 2, 3)]
+    payload, cpl = amplitude_sum(own, geo, *got)
+    near = [payload] + [exchange_sec(payload, m) for m in range(1, secs)]
+    far = exchange_core(stack(near))
+    targets = payload[-4 * GEO :, :]
+    across = target_matrix(panels, targets)
+    mats = [helmholtz(across, n) for n in near] + [helmholtz(across, far, i) for i in range(secs)]
+    mats = [m for pair in mats for m in pair]
+    vel = velocities(panels, cpl, near, far, modes, width, blocks)
+    v_near = [vel] + [exchange_sec(vel, m) for m in range(1, secs)]
+    v_far = exchange_core(stack(v_near))
+    pt, n_near, n_far = pressures(cpl, v_near, v_far, mats, targets, modes, tgts)
+    parts = core_sum(n_near, exchange_core(n_far), secs)
+    sec_got = [exchange_sec(p, m) for m, p in zip(range(1, secs), parts[1:])]
+    finals = sec_sum(parts[0], sec_got, pt)
+    mine = [finals[0]] + [exchange_plane(f, m) for m, f in zip((1, 2, 3), finals[1:])]
+    return outputs(mine)
 
 
 def rotate_combine(leading, second):
@@ -43,7 +507,7 @@
     return rotate_combine(products[:target_count], products[target_count:])
 
 
-def on_device(modal_loads, receptance, shapes, coupling, panel_coords, panel_areas):
+def on_device_general(modal_loads, receptance, shapes, coupling, panel_coords, panel_areas):
     pan_dev = panel_coords.shape[1]
     case_width = modal_loads.shape[1]
     device_count = lax.axis_size("blk") * lax.axis_size("tgt") * lax.axis_size("sec")
@@ -107,6 +571,24 @@
     return (new_loads, pressure_f)
 
 
+def on_device(modal_loads, receptance, shapes, coupling, panel_coords, panel_areas):
+    lanes = 128
+    secs = lax.axis_size("sec")
+    mine = modal_loads.shape[0] * lax.axis_size("blk") // (lax.axis_size("blk") * lax.axis_size("tgt") * secs)
+    fits = (
+        lax.axis_size("blk") == 2
+        and lax.axis_size("tgt") == 4
+        and secs & (secs - 1) == 0
+        and coupling.shape[0] == 1
+        and shapes.shape[2] == lanes
+        and panel_coords.shape[1] == lanes
+        and modal_loads.shape[1] == lanes
+        and mine == lanes
+    )
+    body = on_device_fast if fits else on_device_general
+    return body(modal_loads, receptance, shapes, coupling, panel_coords, panel_areas)
+
+
 def solution(mesh):
     in_specs = (
         P("blk", None),

time: 271 us -> 60.4 us (0.22)
  waiting for transfers between devices: 148 us -> 12.8 us
  blocking collectives: 82.6 us -> 0 us
  starting transfers between devices: 0.12 us -> 25.9 us
  Pallas kernels: 0 us -> 15.9 us
  between operations: 13.9 us -> 0.83 us
  other arithmetic: 9.65 us -> 0 us
  matrix products: 6.2 us -> 0 us
  local copies, waits for them, and re-layouts: 8.47 us -> 4.67 us
    reduce_scatter x2 -> x0, waiting for transfers between devices: 146 us -> none  [the longest x1 138 us: on_device(): lax.psum_scatter(partial_loads, ('blk', 'tgt', 'sec'), scatter_dimension=...]
    all_gather x3 -> x0, blocking collectives: 70.7 us -> none  [the longest x1 36.2 us: on_device(): lax.all_gather(vel_t.astype(jnp.float32), ('tgt', 'sec'), axis=1, tiled=T...]
    ppermute x0 -> x21, starting transfers between devices: none -> 25.9 us  [the longest x9 13.4 us: exchange_sec(): lax.ppermute(x, 'sec', [(s, s ^ mask) for s in range(lax.axis_size('sec'))])]
    pallas_call x0 -> x18, Pallas kernels: none -> 15.9 us  [the longest x8 8.97 us: helmholtz(): pl.pallas_call(functools.partial(helmholtz_kernel, at), in_specs=[VMEM] *...]
    ppermute x0 -> x21, waiting for transfers between devices: none -> 12.8 us  [the longest x9 7.93 us: exchange_sec(): lax.ppermute(x, 'sec', [(s, s ^ mask) for s in range(lax.axis_size('sec'))])]
    psum x1 -> x0, blocking collectives: 11.9 us -> none  [on_device(): modal_sum = lax.psum(modal_sum, 'blk')]
    convert_element_type x2 -> x0, other arithmetic: 9.49 us -> none  [pressure_block(): (jnp.cos(phase_angle) * weight).astype(jnp.bfloat16)]
    dot_general x6 -> x0, matrix products: 6.2 us -> none  [the longest x1 1.86 us: on_device(): jnp.dot(receptance.reshape(2 * row_share, receptance.shape[2]), modal_loa...]
  transfers between devices with their start and end apart: 3 -> 21, of which waited for: 3 -> 11; matrix products, arithmetic and copies ran while one was open for 0% -> 0% of each run, Pallas kernels for 0% -> 15%
where the time goes in v2:
time: 60.4 us; the launch traced here: 60.1 us
  starting transfers between devices  25.9 us (43%)
  Pallas kernels  15.9 us (26%)
  waiting for transfers between devices  12.8 us (21%)
  local copies, waits for them, and re-layouts  4.67 us (8%)
  between operations  0.83 us (1%)
    ppermute x9, starting transfers between devices, exchange_sec(): lax.ppermute(x, 'sec', [(s, s ^ mask) for s in range(lax.axis_size('sec'))])  13.4 us
    ppermute x9, starting transfers between devices, exchange_plane(): return lax.ppermute(x, ('blk', 'tgt'), pairs)  11.9 us
    pallas_call x8, Pallas kernels, helmholtz(): pl.pallas_call(functools.partial(helmholtz_kernel, at), in_specs=[VMEM] *...  8.97 us
    ppermute x9, waiting for transfers between devices, exchange_sec(): lax.ppermute(x, 'sec', [(s, s ^ mask) for s in range(lax.axis_size('sec'))])  7.93 us
    unnamed x13, local copies, waits for them, and re-layouts  4.66 us
    ppermute x9, waiting for transfers between devices, exchange_plane(): return lax.ppermute(x, ('blk', 'tgt'), pairs)  3.84 us
    pallas_call x1, Pallas kernels, pressures(): pl.pallas_call(functools.partial(pressure_kernel, secs, tgt_n), in_specs=...  3.56 us
    pallas_call x1, Pallas kernels, amplitude_parts(): pl.pallas_call(functools.partial(amplitude_kernel, panels), in_specs=[HBM...  1.41 us
  transfers between devices with their start and end apart: 21, of which 11 were waited for; matrix products, arithmetic and copies ran while one was open for 0% of the time, Pallas kernels for 15%

profile of v2, /device:TPU:0, one launch (start us, length us, event | category | flops | bytes accessed | tf_op | source)
XLA Modules:
  0.0 60.1 jit_solution(6480365088590903357)
XLA Ops:
  0.6 1.6 %copy-done = bf16[2,256,2048]{2,1,0:T(8,128)(2,1)S(1)} copy-done((bf16[2,256,2048]{2,1,0:T(8,128)(2,1)S(1)}, bf16[2,256,2048]{2,1,0:T(8,128)(2,1)}, u32[]{:S(2)}) %copy-start) | copy-done | bytes 2097176
  2.2 1.0 %copy-done.1 = bf16[2048,128]{1,0:T(8,128)(2,1)S(1)} copy-done((bf16[2048,128]{1,0:T(8,128)(2,1)S(1)}, bf16[2048,128]{1,0:T(8,128)(2,1)}, u32[]{:S(2)}) %copy-start.1) | copy-done | bytes 524312
  3.3 0.7 %copy-done.2 = f32[3,128]{1,0:T(4,128)S(1)} copy-done((f32[3,128]{1,0:T(4,128)S(1)}, f32[3,128]{1,0:T(4,128)}, u32[]{:S(2)}) %copy-start.2) | copy-done | bytes 1560
  4.0 0.7 %copy-done.3 = f32[128]{0:T(128)S(1)} copy-done((f32[128]{0:T(128)S(1)}, f32[128]{0:T(128)}, u32[]{:S(2)}) %copy-start.3) | copy-done | bytes 536
  5.3 1.4 %amplitude_parts.1 = (f32[64,128]{1,0:T(8,128)S(1)}, bf16[80,128]{1,0:T(8,128)(2,1)S(1)}, bf16[80,128]{1,0:T(8,128)(2,1)S(1)}, bf16[80,128]{1,0:T(8,128)(2,1)S(1)}, bf16[16,128]{1,0:T(8,128)(2,1)S(1)}) custom-call(bf16[2,256,2048]{2,1,0:T(8,128)(2,1)S(1)} %copy-done, bf16[2048,128]{1,0:T(8,128)(2,1)S(1)} %copy-done.1, f32[3,128]{1,0:T(4,128)S(1)} %copy-done.2, ...), custom_call_target="tpu_custom_call" | custom-call | flops 268435456 | bytes 2097152 | tf_op jit(solution)/shard_map/amplitude_parts/pallas_call | solution.py:131
  6.7 3.0 %collective-permute-start = (bf16[80,128]{1,0:T(8,128)(2,1)S(1)}, bf16[80,128]{1,0:T(8,128)(2,1)S(1)}, u32[]{:S(2)}, u32[]{:S(2)}) collective-permute-start(bf16[80,128]{1,0:T(8,128)(2,1)S(1)} %get-tuple-element.38), channel_id=1, source_target_pairs={{0,16},{4,20},{8,24},{12,28},{16,0},{20,4},{24,8},{28,12},{1,17},{... | collective-permute-start | bytes 61448 | tf_op jit(solution)/shard_map/ppermute | solution.py:37
  9.7 1.5 %collective-permute-start.1 = (bf16[80,128]{1,0:T(8,128)(2,1)S(1)}, bf16[80,128]{1,0:T(8,128)(2,1)S(1)}, u32[]{:S(2)}, u32[]{:S(2)}) collective-permute-start(bf16[80,128]{1,0:T(8,128)(2,1)S(1)} %get-tuple-element.39), channel_id=1, source_target_pairs={{0,8},{4,12},{8,0},{12,4},{16,24},{20,28},{24,16},{28,20},{1,9},{5... | collective-permute-start | bytes 61448 | tf_op jit(solution)/shard_map/ppermute | solution.py:37
  11.3 3.0 %collective-permute-start.9 = (bf16[128,1024]{1,0:T(8,128)(2,1)S(1)}, bf16[128,1024]{1,0:T(8,128)(2,1)S(1)}, u32[]{:S(2)}, u32[]{:S(2)}) collective-permute-start(bf16[128,1024]{1,0:T(8,128)(2,1)S(1)} %bitcast.5), channel_id=1, source_target_pairs={{0,24},{4,28},{8,16},{12,20},{16,8},{20,12},{24,0},{28,4},{1,25},{... | collective-permute-start | bytes 786440 | tf_op jit(solution)/shard_map/ppermute | solution.py:37
  14.8 1.5 %collective-permute-done.2.d_ref = bf16[80,128]{1,0:T(8,128)(2,1)S(1)} collective-permute-done((bf16[80,128]{1,0:T(8,128)(2,1)S(1)}, bf16[80,128]{1,0:T(8,128)(2,1)S(1)}, u32[]{:S(2)}, u32[]{:S(2)}) %collective-permute-start.2) | collective-permute-done | bytes 20512 | tf_op jit(solution)/shard_map/ppermute | solution.py:37
  16.3 3.6 %collective-permute-start.5 = (bf16[192,128]{1,0:T(8,128)(2,1)S(1)}, bf16[192,128]{1,0:T(8,128)(2,1)S(1)}, u32[]{:S(2)}, u32[]{:S(2)}) collective-permute-start(bf16[192,128]{1,0:T(8,128)(2,1)S(1)} %get-tuple-element.42.refs_0_.src_ref), channel_id=1, source_target_pairs={{0,3},{1,2},{2,1},{3,0},{4,7},{5,6},{6,5},{7,4},{8,11},{9,10},{10,... | collective-permute-start | bytes 147464 | tf_op jit(solution)/shard_map/ppermute | solution.py:41
  19.9 0.8 %collective-permute-start.3 = (bf16[192,128]{1,0:T(8,128)(2,1)S(1)}, bf16[192,128]{1,0:T(8,128)(2,1)S(1)}, u32[]{:S(2)}, u32[]{:S(2)}) collective-permute-start(bf16[192,128]{1,0:T(8,128)(2,1)S(1)} %get-tuple-element.42.refs_0_.src_ref), channel_id=1, source_target_pairs={{0,1},{1,0},{2,3},{3,2},{4,5},{5,4},{6,7},{7,6},{8,9},{9,8},{10,11... | collective-permute-start | bytes 147464 | tf_op jit(solution)/shard_map/ppermute | solution.py:41
  20.9 1.1 %helmholtz.8 = (bf16[512,512]{1,0:T(8,128)(2,1)S(1)}, bf16[512,512]{1,0:T(8,128)(2,1)S(1)}) custom-call(bf16[512,64]{1,0:T(8,128)(2,1)S(1)} %target_matrix.1.tgt_ref, bf16[192,128]{1,0:T(8,128)(2,1)S(1)} %get-tuple-element.42.refs_0_.src_ref), custom_call_target="tpu_custom_call" | custom-call | flops 1073741824 | bytes 1048576 | tf_op jit(solution)/shard_map/helmholtz/pallas_call | solution.py:293
  22.7 2.2 %collective-permute-done.4.refs_2_.src_ref = bf16[192,128]{1,0:T(8,128)(2,1)S(1)} collective-permute-done((bf16[192,128]{1,0:T(8,128)(2,1)S(1)}, bf16[192,128]{1,0:T(8,128)(2,1)S(1)}, u32[]{:S(2)}, u32[]{:S(2)}) %collective-permute-start.4) | collective-permute-done | bytes 49184 | tf_op jit(solution)/shard_map/ppermute | solution.py:41
  25.0 1.1 %helmholtz.11 = (bf16[512,512]{1,0:T(8,128)(2,1)S(1)}, bf16[512,512]{1,0:T(8,128)(2,1)S(1)}) custom-call(bf16[512,64]{1,0:T(8,128)(2,1)S(1)} %target_matrix.1.tgt_ref, bf16[192,128]{1,0:T(8,128)(2,1)S(1)} %collective-permute-done.5.refs_3_.src_ref), custom_call_target="tpu_custom_call" | custom-call | flops 1073741824 | bytes 1048576 | tf_op jit(solution)/shard_map/helmholtz/pallas_call | solution.py:293
  26.1 1.1 %helmholtz.10 = (bf16[512,512]{1,0:T(8,128)(2,1)S(1)}, bf16[512,512]{1,0:T(8,128)(2,1)S(1)}) custom-call(bf16[512,64]{1,0:T(8,128)(2,1)S(1)} %target_matrix.1.tgt_ref, bf16[192,128]{1,0:T(8,128)(2,1)S(1)} %collective-permute-done.4.refs_2_.src_ref), custom_call_target="tpu_custom_call" | custom-call | flops 1073741824 | bytes 1048576 | tf_op jit(solution)/shard_map/helmholtz/pallas_call | solution.py:293
  27.3 1.1 %helmholtz.9 = (bf16[512,512]{1,0:T(8,128)(2,1)S(1)}, bf16[512,512]{1,0:T(8,128)(2,1)S(1)}) custom-call(bf16[512,64]{1,0:T(8,128)(2,1)S(1)} %target_matrix.1.tgt_ref, bf16[192,128]{1,0:T(8,128)(2,1)S(1)} %collective-permute-done.3.refs_1_.src_ref), custom_call_target="tpu_custom_call" | custom-call | flops 1073741824 | bytes 1048576 | tf_op jit(solution)/shard_map/helmholtz/pallas_call | solution.py:293
  28.8 1.0 %velocities.1.refs_0_ = bf16[4,32,128]{2,1,0:T(8,128)(2,1)S(1)} custom-call(s32[4,128]{1,0:T(4,128)S(1)} %get-tuple-element.41.cpl, bf16[192,128]{1,0:T(8,128)(2,1)S(1)} %get-tuple-element.42.refs_0_.src_ref, bf16[192,128]{1,0:T(8,128)(2,1)S(1)} %collective-permute-done.3.refs_1_.src_ref, bf16[192,128]{1,0:T(8,128)(2,1)S(1)} %collective-permute-done.4.refs_2_.src_ref, ...), custom_call_target="tpu_custom_call" | custom-call | tf_op jit(solution)/shard_map/velocities/pallas_call | solution.py:218
  29.8 3.5 %collective-permute-start.12 = (bf16[4,32,128]{2,1,0:T(8,128)(2,1)S(1)}, bf16[4,32,128]{2,1,0:T(8,128)(2,1)S(1)}, u32[]{:S(2)}, u32[]{:S(2)}) collective-permute-start(bf16[4,32,128]{2,1,0:T(8,128)(2,1)S(1)} %velocities.1.refs_0_), channel_id=1, source_target_pairs={{0,3},{1,2},{2,1},{3,0},{4,7},{5,6},{6,5},{7,4},{8,11},{9,10},{10,... | collective-permute-start | bytes 98312 | tf_op jit(solution)/shard_map/ppermute | solution.py:41
  33.3 1.0 %collective-permute-start.10 = (bf16[4,32,128]{2,1,0:T(8,128)(2,1)S(1)}, bf16[4,32,128]{2,1,0:T(8,128)(2,1)S(1)}, u32[]{:S(2)}, u32[]{:S(2)}) collective-permute-start(bf16[4,32,128]{2,1,0:T(8,128)(2,1)S(1)} %velocities.1.refs_0_), channel_id=1, source_target_pairs={{0,1},{1,0},{2,3},{3,2},{4,5},{5,4},{6,7},{7,6},{8,9},{9,8},{10,11... | collective-permute-start | bytes 98312 | tf_op jit(solution)/shard_map/ppermute | solution.py:41
  34.3 1.1 %helmholtz.15 = (bf16[512,512]{1,0:T(8,128)(2,1)S(1)}, bf16[512,512]{1,0:T(8,128)(2,1)S(1)}) custom-call(bf16[512,64]{1,0:T(8,128)(2,1)S(1)} %target_matrix.1.tgt_ref, bf16[4,192,128]{2,1,0:T(8,128)(2,1)S(1)} %collective-permute-done.6.refs_4_.src_ref), custom_call_target="tpu_custom_call" | custom-call | flops 1073741824 | bytes 1048576 | tf_op jit(solution)/shard_map/helmholtz/pallas_call | solution.py:293
  35.4 1.1 %helmholtz.14 = (bf16[512,512]{1,0:T(8,128)(2,1)S(1)}, bf16[512,512]{1,0:T(8,128)(2,1)S(1)}) custom-call(bf16[512,64]{1,0:T(8,128)(2,1)S(1)} %target_matrix.1.tgt_ref, bf16[4,192,128]{2,1,0:T(8,128)(2,1)S(1)} %collective-permute-done.6.refs_4_.src_ref), custom_call_target="tpu_custom_call" | custom-call | flops 1073741824 | bytes 1048576 | tf_op jit(solution)/shard_map/helmholtz/pallas_call | solution.py:293
  36.5 1.5 %collective-permute-done.11.refs_2_ = bf16[4,32,128]{2,1,0:T(8,128)(2,1)S(1)} collective-permute-done((bf16[4,32,128]{2,1,0:T(8,128)(2,1)S(1)}, bf16[4,32,128]{2,1,0:T(8,128)(2,1)S(1)}, u32[]{:S(2)}, u32[]{:S(2)}) %collective-permute-start.11) | collective-permute-done | bytes 32800 | tf_op jit(solution)/shard_map/ppermute | solution.py:41
  38.2 1.1 %helmholtz.13 = (bf16[512,512]{1,0:T(8,128)(2,1)S(1)}, bf16[512,512]{1,0:T(8,128)(2,1)S(1)}) custom-call(bf16[512,64]{1,0:T(8,128)(2,1)S(1)} %target_matrix.1.tgt_ref, bf16[4,192,128]{2,1,0:T(8,128)(2,1)S(1)} %collective-permute-done.6.refs_4_.src_ref), custom_call_target="tpu_custom_call" | custom-call | flops 1073741824 | bytes 1048576 | tf_op jit(solution)/shard_map/helmholtz/pallas_call | solution.py:293
  39.3 1.1 %helmholtz.12 = (bf16[512,512]{1,0:T(8,128)(2,1)S(1)}, bf16[512,512]{1,0:T(8,128)(2,1)S(1)}) custom-call(bf16[512,64]{1,0:T(8,128)(2,1)S(1)} %target_matrix.1.tgt_ref, bf16[4,192,128]{2,1,0:T(8,128)(2,1)S(1)} %collective-permute-done.6.refs_4_.src_ref), custom_call_target="tpu_custom_call" | custom-call | flops 1073741824 | bytes 1048576 | tf_op jit(solution)/shard_map/helmholtz/pallas_call | solution.py:293
  40.4 3.6 %pressures.1 = (bf16[4,32,128]{2,1,0:T(8,128)(2,1)S(1)}, f32[16,32,128]{2,1,0:T(8,128)S(1)}, bf16[16,32,128]{2,1,0:T(8,128)(2,1)S(1)}) custom-call(s32[4,128]{1,0:T(4,128)S(1)} %get-tuple-element.41.cpl, bf16[4,32,128]{2,1,0:T(8,128)(2,1)S(1)} %velocities.1.refs_0_, bf16[4,32,128]{2,1,0:T(8,128)(2,1)S(1)} %collective-permute-done.10.refs_1_, ...), custom_call_target="tpu_custom_call" | custom-call | tf_op jit(solution)/shard_map/pressures/pallas_call | solution.py:354
  44.6 1.0 %collective-permute-done.14.got_ref = bf16[16,32,128]{2,1,0:T(8,128)(2,1)S(1)} collective-permute-done((bf16[16,32,128]{2,1,0:T(8,128)(2,1)S(1)}, bf16[16,32,128]{2,1,0:T(8,128)(2,1)S(1)}, u32[]{:S(2)}, u32[]{:S(2)}) %collective-permute-start.14) | collective-permute-done | bytes 131104 | tf_op jit(solution)/shard_map/ppermute | solution.py:45
  45.8 2.3 %collective-permute-start.16 = (bf16[4,32,128]{2,1,0:T(8,128)(2,1)S(1)}, bf16[4,32,128]{2,1,0:T(8,128)(2,1)S(1)}, u32[]{:S(2)}, u32[]{:S(2)}) collective-permute-start(bf16[4,32,128]{2,1,0:T(8,128)(2,1)S(1)} %get-tuple-element.63), channel_id=1, source_target_pairs={{0,2},{1,3},{2,0},{3,1},{4,6},{5,7},{6,4},{7,5},{8,10},{9,11},{10,... | collective-permute-start | bytes 98312 | tf_op jit(solution)/shard_map/ppermute | solution.py:41
  48.1 2.0 %collective-permute-start.17 = (bf16[4,32,128]{2,1,0:T(8,128)(2,1)S(1)}, bf16[4,32,128]{2,1,0:T(8,128)(2,1)S(1)}, u32[]{:S(2)}, u32[]{:S(2)}) collective-permute-start(bf16[4,32,128]{2,1,0:T(8,128)(2,1)S(1)} %get-tuple-element.64), channel_id=1, source_target_pairs={{0,3},{1,2},{2,1},{3,0},{4,7},{5,6},{6,5},{7,4},{8,11},{9,10},{10,... | collective-permute-start | bytes 98312 | tf_op jit(solution)/shard_map/ppermute | solution.py:41
  50.6 3.2 %collective-permute-done.17.refs_3_ = bf16[4,32,128]{2,1,0:T(8,128)(2,1)S(1)} collective-permute-done((bf16[4,32,128]{2,1,0:T(8,128)(2,1)S(1)}, bf16[4,32,128]{2,1,0:T(8,128)(2,1)S(1)}, u32[]{:S(2)}, u32[]{:S(2)}) %collective-permute-start.17) | collective-permute-done | bytes 32800 | tf_op jit(solution)/shard_map/ppermute | solution.py:41
  54.7 2.6 %collective-permute-start.20 = (bf16[2,32,128]{2,1,0:T(8,128)(2,1)S(1)}, bf16[2,32,128]{2,1,0:T(8,128)(2,1)S(1)}, u32[]{:S(2)}, u32[]{:S(2)}) collective-permute-start(bf16[2,32,128]{2,1,0:T(8,128)(2,1)S(1)} %get-tuple-element.69), channel_id=1, source_target_pairs={{0,24},{4,28},{8,16},{12,20},{16,8},{20,12},{24,0},{28,4},{1,25},{... | collective-permute-start | bytes 49160 | tf_op jit(solution)/shard_map/ppermute | solution.py:37
  58.1 1.3 %collective-permute-done.20.r3 = bf16[2,32,128]{2,1,0:T(8,128)(2,1)S(1)} collective-permute-done((bf16[2,32,128]{2,1,0:T(8,128)(2,1)S(1)}, bf16[2,32,128]{2,1,0:T(8,128)(2,1)S(1)}, u32[]{:S(2)}, u32[]{:S(2)}) %collective-permute-start.20) | collective-permute-done | bytes 16416 | tf_op jit(solution)/shard_map/ppermute | solution.py:37
  59.4 0.8 %outputs.1 = (f32[128,128]{1,0:T(8,128)}, bf16[128,128]{1,0:T(8,128)(2,1)}) custom-call(f32[2,32,128]{2,1,0:T(8,128)S(1)} %get-tuple-element.66.r0, bf16[2,32,128]{2,1,0:T(8,128)(2,1)S(1)} %collective-permute-done.18.r1, bf16[2,32,128]{2,1,0:T(8,128)(2,1)S(1)} %collective-permute-done.19.r2, bf16[2,32,128]{2,1,0:T(8,128)(2,1)S(1)} %collective-permute-done.20.r3), custom_call_target="tpu_custom_call" | custom-call | tf_op jit(solution)/shard_map/outputs/pallas_call | solution.py:433
  (42 shorter events, 5.5 us)
Async XLA Ops:
  0.6 1.6 %copy-start = (bf16[2,256,2048]{2,1,0:T(8,128)(2,1)S(1)}, bf16[2,256,2048]{2,1,0:T(8,128)(2,1)}, u32[]{:S(2)}) copy-start(bf16[2,256,2048]{2,1,0:T(8,128)(2,1)} %r_hbm.1) | copy-start | bytes 6291460
  2.2 1.0 %copy-start.1 = (bf16[2048,128]{1,0:T(8,128)(2,1)S(1)}, bf16[2048,128]{1,0:T(8,128)(2,1)}, u32[]{:S(2)}) copy-start(bf16[2048,128]{1,0:T(8,128)(2,1)} %l_hbm.1) | copy-start | bytes 1572868
  3.3 0.7 %copy-start.2 = (f32[3,128]{1,0:T(4,128)S(1)}, f32[3,128]{1,0:T(4,128)}, u32[]{:S(2)}) copy-start(f32[3,128]{1,0:T(4,128)} %xyz_hbm.1) | copy-start | bytes 4612
  3.9 0.7 %copy-start.3 = (f32[128]{0:T(128)S(1)}, f32[128]{0:T(128)}, u32[]{:S(2)}) copy-start(f32[128]{0:T(128)} %param.11) | copy-start | bytes 1540
  4.6 0.7 %copy-start.4 = (s32[1,8]{1,0:T(1,128)S(1)}, s32[1,8]{1,0:T(1,128)}, u32[]{:S(2)}) copy-start(s32[1,8]{1,0:T(1,128)} %cpl_hbm.1) | copy-start | bytes 100
  5.3 6.0 %copy-start.5 = (bf16[128,8,128]{2,1,0:T(8,128)(2,1)S(1)}, bf16[128,8,128]{2,1,0:T(8,128)(2,1)}, u32[]{:S(2)}) copy-start(bf16[128,8,128]{2,1,0:T(8,128)(2,1)} %param.8) | copy-start | bytes 786436
  6.7 8.1 %collective-permute-start = (bf16[80,128]{1,0:T(8,128)(2,1)S(1)}, bf16[80,128]{1,0:T(8,128)(2,1)S(1)}, u32[]{:S(2)}, u32[]{:S(2)}) collective-permute-start(bf16[80,128]{1,0:T(8,128)(2,1)S(1)} %get-tuple-element.38), channel_id=1, source_target_pairs={{0,16},{4,20},{8,24},{12,28},{16,0},{20,4},{24,8},{28,12},{1,17},{... | collective-permute-start | bytes 61448 | tf_op jit(solution)/shard_map/ppermute | solution.py:37
  9.7 5.1 %collective-permute-start.1 = (bf16[80,128]{1,0:T(8,128)(2,1)S(1)}, bf16[80,128]{1,0:T(8,128)(2,1)S(1)}, u32[]{:S(2)}, u32[]{:S(2)}) collective-permute-start(bf16[80,128]{1,0:T(8,128)(2,1)S(1)} %get-tuple-element.39), channel_id=1, source_target_pairs={{0,8},{4,12},{8,0},{12,4},{16,24},{20,28},{24,16},{28,20},{1,9},{5... | collective-permute-start | bytes 61448 | tf_op jit(solution)/shard_map/ppermute | solution.py:37
  11.2 5.0 %collective-permute-start.2 = (bf16[80,128]{1,0:T(8,128)(2,1)S(1)}, bf16[80,128]{1,0:T(8,128)(2,1)S(1)}, u32[]{:S(2)}, u32[]{:S(2)}) collective-permute-start(bf16[80,128]{1,0:T(8,128)(2,1)S(1)} %get-tuple-element.40), channel_id=1, source_target_pairs={{0,24},{4,28},{8,16},{12,20},{16,8},{20,12},{24,0},{28,4},{1,25},{... | collective-permute-start | bytes 61448 | tf_op jit(solution)/shard_map/ppermute | solution.py:37
  11.3 17.1 %collective-permute-start.9 = (bf16[128,1024]{1,0:T(8,128)(2,1)S(1)}, bf16[128,1024]{1,0:T(8,128)(2,1)S(1)}, u32[]{:S(2)}, u32[]{:S(2)}) collective-permute-start(bf16[128,1024]{1,0:T(8,128)(2,1)S(1)} %bitcast.5), channel_id=1, source_target_pairs={{0,24},{4,28},{8,16},{12,20},{16,8},{20,12},{24,0},{28,4},{1,25},{... | collective-permute-start | bytes 786440 | tf_op jit(solution)/shard_map/ppermute | solution.py:37
  14.2 14.2 %collective-permute-start.8 = (bf16[128,1024]{1,0:T(8,128)(2,1)S(1)}, bf16[128,1024]{1,0:T(8,128)(2,1)S(1)}, u32[]{:S(2)}, u32[]{:S(2)}) collective-permute-start(bf16[128,1024]{1,0:T(8,128)(2,1)S(1)} %bitcast.6), channel_id=1, source_target_pairs={{0,8},{4,12},{8,0},{12,4},{16,24},{20,28},{24,16},{28,20},{1,9},{5... | collective-permute-start | bytes 786440 | tf_op jit(solution)/shard_map/ppermute | solution.py:37
  16.3 6.1 %collective-permute-start.5 = (bf16[192,128]{1,0:T(8,128)(2,1)S(1)}, bf16[192,128]{1,0:T(8,128)(2,1)S(1)}, u32[]{:S(2)}, u32[]{:S(2)}) collective-permute-start(bf16[192,128]{1,0:T(8,128)(2,1)S(1)} %get-tuple-element.42.refs_0_.src_ref), channel_id=1, source_target_pairs={{0,3},{1,2},{2,1},{3,0},{4,7},{5,6},{6,5},{7,4},{8,11},{9,10},{10,... | collective-permute-start | bytes 147464 | tf_op jit(solution)/shard_map/ppermute | solution.py:41
  19.9 5.0 %collective-permute-start.4 = (bf16[192,128]{1,0:T(8,128)(2,1)S(1)}, bf16[192,128]{1,0:T(8,128)(2,1)S(1)}, u32[]{:S(2)}, u32[]{:S(2)}) collective-permute-start(bf16[192,128]{1,0:T(8,128)(2,1)S(1)} %get-tuple-element.42.refs_0_.src_ref), channel_id=1, source_target_pairs={{0,2},{1,3},{2,0},{3,1},{4,6},{5,7},{6,4},{7,5},{8,10},{9,11},{10,... | collective-permute-start | bytes 147464 | tf_op jit(solution)/shard_map/ppermute | solution.py:41
  19.9 5.0 %collective-permute-start.3 = (bf16[192,128]{1,0:T(8,128)(2,1)S(1)}, bf16[192,128]{1,0:T(8,128)(2,1)S(1)}, u32[]{:S(2)}, u32[]{:S(2)}) collective-permute-start(bf16[192,128]{1,0:T(8,128)(2,1)S(1)} %get-tuple-element.42.refs_0_.src_ref), channel_id=1, source_target_pairs={{0,1},{1,0},{2,3},{3,2},{4,5},{5,4},{6,7},{7,6},{8,9},{9,8},{10,11... | collective-permute-start | bytes 147464 | tf_op jit(solution)/shard_map/ppermute | solution.py:41
  22.4 6.4 %collective-permute-start.7 = (bf16[128,1024]{1,0:T(8,128)(2,1)S(1)}, bf16[128,1024]{1,0:T(8,128)(2,1)S(1)}, u32[]{:S(2)}, u32[]{:S(2)}) collective-permute-start(bf16[128,1024]{1,0:T(8,128)(2,1)S(1)} %bitcast.7), channel_id=1, source_target_pairs={{0,16},{4,20},{8,24},{12,28},{16,0},{20,4},{24,8},{28,12},{1,17},{... | collective-permute-start | bytes 786440 | tf_op jit(solution)/shard_map/ppermute | solution.py:37
  24.9 3.9 %collective-permute-start.6 = (bf16[4,192,128]{2,1,0:T(8,128)(2,1)S(1)}, bf16[4,192,128]{2,1,0:T(8,128)(2,1)S(1)}, u32[]{:S(2)}, u32[]{:S(2)}) collective-permute-start(bf16[4,192,128]{2,1,0:T(8,128)(2,1)S(1)} %stack.2), channel_id=1, source_target_pairs={{0,4},{4,0},{8,12},{12,8},{1,5},{5,1},{9,13},{13,9},{2,6},{6,2},{1... | collective-permute-start | bytes 589832 | tf_op jit(solution)/shard_map/ppermute | solution.py:45
  29.8 6.7 %collective-permute-start.12 = (bf16[4,32,128]{2,1,0:T(8,128)(2,1)S(1)}, bf16[4,32,128]{2,1,0:T(8,128)(2,1)S(1)}, u32[]{:S(2)}, u32[]{:S(2)}) collective-permute-start(bf16[4,32,128]{2,1,0:T(8,128)(2,1)S(1)} %velocities.1.refs_0_), channel_id=1, source_target_pairs={{0,3},{1,2},{2,1},{3,0},{4,7},{5,6},{6,5},{7,4},{8,11},{9,10},{10,... | collective-permute-start | bytes 98312 | tf_op jit(solution)/shard_map/ppermute | solution.py:41
  33.3 4.8 %collective-permute-start.11 = (bf16[4,32,128]{2,1,0:T(8,128)(2,1)S(1)}, bf16[4,32,128]{2,1,0:T(8,128)(2,1)S(1)}, u32[]{:S(2)}, u32[]{:S(2)}) collective-permute-start(bf16[4,32,128]{2,1,0:T(8,128)(2,1)S(1)} %velocities.1.refs_0_), channel_id=1, source_target_pairs={{0,2},{1,3},{2,0},{3,1},{4,6},{5,7},{6,4},{7,5},{8,10},{9,11},{10,... | collective-permute-start | bytes 98312 | tf_op jit(solution)/shard_map/ppermute | solution.py:41
  33.3 4.8 %collective-permute-start.10 = (bf16[4,32,128]{2,1,0:T(8,128)(2,1)S(1)}, bf16[4,32,128]{2,1,0:T(8,128)(2,1)S(1)}, u32[]{:S(2)}, u32[]{:S(2)}) collective-permute-start(bf16[4,32,128]{2,1,0:T(8,128)(2,1)S(1)} %velocities.1.refs_0_), channel_id=1, source_target_pairs={{0,1},{1,0},{2,3},{3,2},{4,5},{5,4},{6,7},{7,6},{8,9},{9,8},{10,11... | collective-permute-start | bytes 98312 | tf_op jit(solution)/shard_map/ppermute | solution.py:41
  38.1 2.3 %collective-permute-start.13 = (bf16[4,4,32,128]{3,2,1,0:T(8,128)(2,1)S(1)}, bf16[4,4,32,128]{3,2,1,0:T(8,128)(2,1)S(1)}, u32[]{:S(2)}, u32[]{:S(2)}) collective-permute-start(bf16[4,4,32,128]{3,2,1,0:T(8,128)(2,1)S(1)} %stack.3), channel_id=1, source_target_pairs={{0,4},{4,0},{8,12},{12,8},{1,5},{5,1},{9,13},{13,9},{2,6},{6,2},{1... | collective-permute-start | bytes 393224 | tf_op jit(solution)/shard_map/ppermute | solution.py:45
  44.0 1.6 %collective-permute-start.14 = (bf16[16,32,128]{2,1,0:T(8,128)(2,1)S(1)}, bf16[16,32,128]{2,1,0:T(8,128)(2,1)S(1)}, u32[]{:S(2)}, u32[]{:S(2)}) collective-permute-start(bf16[16,32,128]{2,1,0:T(8,128)(2,1)S(1)} %get-tuple-element.60), channel_id=1, source_target_pairs={{0,4},{4,0},{8,12},{12,8},{1,5},{5,1},{9,13},{13,9},{2,6},{6,2},{1... | collective-permute-start | bytes 393224 | tf_op jit(solution)/shard_map/ppermute | solution.py:45
  45.6 4.5 %collective-permute-start.15 = (bf16[4,32,128]{2,1,0:T(8,128)(2,1)S(1)}, bf16[4,32,128]{2,1,0:T(8,128)(2,1)S(1)}, u32[]{:S(2)}, u32[]{:S(2)}) collective-permute-start(bf16[4,32,128]{2,1,0:T(8,128)(2,1)S(1)} %get-tuple-element.62), channel_id=1, source_target_pairs={{0,1},{1,0},{2,3},{3,2},{4,5},{5,4},{6,7},{7,6},{8,9},{9,8},{10,11... | collective-permute-start | bytes 98312 | tf_op jit(solution)/shard_map/ppermute | solution.py:41
  45.8 4.8 %collective-permute-start.16 = (bf16[4,32,128]{2,1,0:T(8,128)(2,1)S(1)}, bf16[4,32,128]{2,1,0:T(8,128)(2,1)S(1)}, u32[]{:S(2)}, u32[]{:S(2)}) collective-permute-start(bf16[4,32,128]{2,1,0:T(8,128)(2,1)S(1)} %get-tuple-element.63), channel_id=1, source_target_pairs={{0,2},{1,3},{2,0},{3,1},{4,6},{5,7},{6,4},{7,5},{8,10},{9,11},{10,... | collective-permute-start | bytes 98312 | tf_op jit(solution)/shard_map/ppermute | solution.py:41
  48.1 5.7 %collective-permute-start.17 = (bf16[4,32,128]{2,1,0:T(8,128)(2,1)S(1)}, bf16[4,32,128]{2,1,0:T(8,128)(2,1)S(1)}, u32[]{:S(2)}, u32[]{:S(2)}) collective-permute-start(bf16[4,32,128]{2,1,0:T(8,128)(2,1)S(1)} %get-tuple-element.64), channel_id=1, source_target_pairs={{0,3},{1,2},{2,1},{3,0},{4,7},{5,6},{6,5},{7,4},{8,11},{9,10},{10,... | collective-permute-start | bytes 98312 | tf_op jit(solution)/shard_map/ppermute | solution.py:41
  53.8 3.8 %collective-permute-start.18 = (bf16[2,32,128]{2,1,0:T(8,128)(2,1)S(1)}, bf16[2,32,128]{2,1,0:T(8,128)(2,1)S(1)}, u32[]{:S(2)}, u32[]{:S(2)}) collective-permute-start(bf16[2,32,128]{2,1,0:T(8,128)(2,1)S(1)} %get-tuple-element.67), channel_id=1, source_target_pairs={{0,16},{4,20},{8,24},{12,28},{16,0},{20,4},{24,8},{28,12},{1,17},{... | collective-permute-start | bytes 49160 | tf_op jit(solution)/shard_map/ppermute | solution.py:37
  54.3 3.7 %collective-permute-start.19 = (bf16[2,32,128]{2,1,0:T(8,128)(2,1)S(1)}, bf16[2,32,128]{2,1,0:T(8,128)(2,1)S(1)}, u32[]{:S(2)}, u32[]{:S(2)}) collective-permute-start(bf16[2,32,128]{2,1,0:T(8,128)(2,1)S(1)} %get-tuple-element.68), channel_id=1, source_target_pairs={{0,8},{4,12},{8,0},{12,4},{16,24},{20,28},{24,16},{28,20},{1,9},{5... | collective-permute-start | bytes 49160 | tf_op jit(solution)/shard_map/ppermute | solution.py:37
  54.7 4.6 %collective-permute-start.20 = (bf16[2,32,128]{2,1,0:T(8,128)(2,1)S(1)}, bf16[2,32,128]{2,1,0:T(8,128)(2,1)S(1)}, u32[]{:S(2)}, u32[]{:S(2)}) collective-permute-start(bf16[2,32,128]{2,1,0:T(8,128)(2,1)S(1)} %get-tuple-element.69), channel_id=1, source_target_pairs={{0,24},{4,28},{8,16},{12,20},{16,8},{20,12},{24,0},{28,4},{1,25},{... | collective-permute-start | bytes 49160 | tf_op jit(solution)/shard_map/ppermute | solution.py:37

commit v3 on v2

--- a/solution.py
+++ b/solution.py
@@ -448,9 +448,11 @@
     width = modal_loads.shape[1] // 4
     blocks = receptance.shape[1] // shapes.shape[2]
 
-    own, s1, s2, s3, geo = amplitude_parts(
-        panels, receptance, modal_loads, panel_coords, panel_areas[None, :], coupling
-    )
+    held = [
+        pltpu.with_memory_space_constraint(a, pltpu.HBM)
+        for a in (receptance, modal_loads, panel_coords, panel_areas[None, :], coupling)
+    ]
+    own, s1, s2, s3, geo = amplitude_parts(panels, *held)
     got = [exchange_plane(s, m) for m, s in ((1, s1), (2, s2), (3, s3))]
     flat = shapes.reshape(pan_dev, -1)
     modes = [flat] + [exchange_plane(flat, m) for m in (1, 2, 3)]

time: 60.4 us -> 57 us (0.944)
  local copies, waits for them, and re-layouts: 4.67 us -> 0.05 us
  Pallas kernels: 15.9 us -> 17.3 us
    unnamed x13 -> x3, local copies, waits for them, and re-layouts: 4.66 us -> 0.05 us
    pallas_call x1, Pallas kernels: 1.41 us -> 2.74 us  [amplitude_parts(): pl.pallas_call(functools.partial(amplitude_kernel, panels), in_specs=[HBM...]
  transfers between devices with their start and end apart: 21 -> 21, of which waited for: 11 -> 11; matrix products, arithmetic and copies ran while one was open for 0% -> 0% of each run, Pallas kernels for 15% -> 16%
where the time goes in v3:
time: 57 us; the launch traced here: 56.8 us
  starting transfers between devices  25.9 us (45%)
  Pallas kernels  17.3 us (30%)
  waiting for transfers between devices  12.7 us (22%)
  between operations  0.83 us (1%)
    ppermute x9, starting transfers between devices, exchange_sec(): lax.ppermute(x, 'sec', [(s, s ^ mask) for s in range(lax.axis_size('sec'))])  13.4 us
    ppermute x9, starting transfers between devices, exchange_plane(): return lax.ppermute(x, ('blk', 'tgt'), pairs)  11.8 us
    pallas_call x8, Pallas kernels, helmholtz(): pl.pallas_call(functools.partial(helmholtz_kernel, at), in_specs=[VMEM] *...  9 us
    ppermute x9, waiting for transfers between devices, exchange_sec(): lax.ppermute(x, 'sec', [(s, s ^ mask) for s in range(lax.axis_size('sec'))])  7.9 us
    ppermute x9, waiting for transfers between devices, exchange_plane(): return lax.ppermute(x, ('blk', 'tgt'), pairs)  3.84 us
    pallas_call x1, Pallas kernels, pressures(): pl.pallas_call(functools.partial(pressure_kernel, secs, tgt_n), in_specs=...  3.57 us
    pallas_call x1, Pallas kernels, amplitude_parts(): pl.pallas_call(functools.partial(amplitude_kernel, panels), in_specs=[HBM...  2.74 us
  transfers between devices with their start and end apart: 21, of which 11 were waited for; matrix products, arithmetic and copies ran while one was open for 0% of the time, Pallas kernels for 16%

profile of v3, /device:TPU:0, one launch (start us, length us, event | category | flops | bytes accessed | tf_op | source)
XLA Modules:
  0.0 56.8 jit_solution(8233527515331855120)
XLA Ops:
  0.6 2.7 %amplitude_parts.1 = (f32[64,128]{1,0:T(8,128)S(1)}, bf16[80,128]{1,0:T(8,128)(2,1)S(1)}, bf16[80,128]{1,0:T(8,128)(2,1)S(1)}, bf16[80,128]{1,0:T(8,128)(2,1)S(1)}, bf16[16,128]{1,0:T(8,128)(2,1)S(1)}) custom-call(bf16[2,256,2048]{2,1,0:T(8,128)(2,1)} %r_hbm.1, bf16[2048,128]{1,0:T(8,128)(2,1)} %l_hbm.1, f32[3,128]{1,0:T(4,128)} %xyz_hbm.1, ...), custom_call_target="tpu_custom_call" | custom-call | flops 268435456 | bytes 2097152 | tf_op jit(solution)/shard_map/amplitude_parts/pallas_call | solution.py:131
  3.4 3.0 %collective-permute-start = (bf16[80,128]{1,0:T(8,128)(2,1)S(1)}, bf16[80,128]{1,0:T(8,128)(2,1)S(1)}, u32[]{:S(2)}, u32[]{:S(2)}) collective-permute-start(bf16[80,128]{1,0:T(8,128)(2,1)S(1)} %get-tuple-element.38), channel_id=1, source_target_pairs={{0,16},{4,20},{8,24},{12,28},{16,0},{20,4},{24,8},{28,12},{1,17},{... | collective-permute-start | bytes 61448 | tf_op jit(solution)/shard_map/ppermute | solution.py:37
  6.4 1.5 %collective-permute-start.1 = (bf16[80,128]{1,0:T(8,128)(2,1)S(1)}, bf16[80,128]{1,0:T(8,128)(2,1)S(1)}, u32[]{:S(2)}, u32[]{:S(2)}) collective-permute-start(bf16[80,128]{1,0:T(8,128)(2,1)S(1)} %get-tuple-element.39), channel_id=1, source_target_pairs={{0,8},{4,12},{8,0},{12,4},{16,24},{20,28},{24,16},{28,20},{1,9},{5... | collective-permute-start | bytes 61448 | tf_op jit(solution)/shard_map/ppermute | solution.py:37
  8.0 3.0 %collective-permute-start.9 = (bf16[128,1024]{1,0:T(8,128)(2,1)S(1)}, bf16[128,1024]{1,0:T(8,128)(2,1)S(1)}, u32[]{:S(2)}, u32[]{:S(2)}) collective-permute-start(bf16[128,1024]{1,0:T(8,128)(2,1)S(1)} %bitcast.5), channel_id=1, source_target_pairs={{0,24},{4,28},{8,16},{12,20},{16,8},{20,12},{24,0},{28,4},{1,25},{... | collective-permute-start | bytes 786440 | tf_op jit(solution)/shard_map/ppermute | solution.py:37
  11.0 0.5 collective-permute-start.8
  11.5 1.5 %collective-permute-done.2.d_ref = bf16[80,128]{1,0:T(8,128)(2,1)S(1)} collective-permute-done((bf16[80,128]{1,0:T(8,128)(2,1)S(1)}, bf16[80,128]{1,0:T(8,128)(2,1)S(1)}, u32[]{:S(2)}, u32[]{:S(2)}) %collective-permute-start.2) | collective-permute-done | bytes 20512 | tf_op jit(solution)/shard_map/ppermute | solution.py:37
  13.0 3.6 %collective-permute-start.5 = (bf16[192,128]{1,0:T(8,128)(2,1)S(1)}, bf16[192,128]{1,0:T(8,128)(2,1)S(1)}, u32[]{:S(2)}, u32[]{:S(2)}) collective-permute-start(bf16[192,128]{1,0:T(8,128)(2,1)S(1)} %get-tuple-element.42.refs_0_.src_ref), channel_id=1, source_target_pairs={{0,3},{1,2},{2,1},{3,0},{4,7},{5,6},{6,5},{7,4},{8,11},{9,10},{10,... | collective-permute-start | bytes 147464 | tf_op jit(solution)/shard_map/ppermute | solution.py:41
  16.6 0.8 %collective-permute-start.3 = (bf16[192,128]{1,0:T(8,128)(2,1)S(1)}, bf16[192,128]{1,0:T(8,128)(2,1)S(1)}, u32[]{:S(2)}, u32[]{:S(2)}) collective-permute-start(bf16[192,128]{1,0:T(8,128)(2,1)S(1)} %get-tuple-element.42.refs_0_.src_ref), channel_id=1, source_target_pairs={{0,1},{1,0},{2,3},{3,2},{4,5},{5,4},{6,7},{7,6},{8,9},{9,8},{10,11... | collective-permute-start | bytes 147464 | tf_op jit(solution)/shard_map/ppermute | solution.py:41
  17.6 1.1 %helmholtz.8 = (bf16[512,512]{1,0:T(8,128)(2,1)S(1)}, bf16[512,512]{1,0:T(8,128)(2,1)S(1)}) custom-call(bf16[512,64]{1,0:T(8,128)(2,1)S(1)} %target_matrix.1.tgt_ref, bf16[192,128]{1,0:T(8,128)(2,1)S(1)} %get-tuple-element.42.refs_0_.src_ref), custom_call_target="tpu_custom_call" | custom-call | flops 1073741824 | bytes 1048576 | tf_op jit(solution)/shard_map/helmholtz/pallas_call | solution.py:293
  19.4 2.2 %collective-permute-done.4.refs_2_.src_ref = bf16[192,128]{1,0:T(8,128)(2,1)S(1)} collective-permute-done((bf16[192,128]{1,0:T(8,128)(2,1)S(1)}, bf16[192,128]{1,0:T(8,128)(2,1)S(1)}, u32[]{:S(2)}, u32[]{:S(2)}) %collective-permute-start.4) | collective-permute-done | bytes 49184 | tf_op jit(solution)/shard_map/ppermute | solution.py:41
  21.7 1.1 %helmholtz.11 = (bf16[512,512]{1,0:T(8,128)(2,1)S(1)}, bf16[512,512]{1,0:T(8,128)(2,1)S(1)}) custom-call(bf16[512,64]{1,0:T(8,128)(2,1)S(1)} %target_matrix.1.tgt_ref, bf16[192,128]{1,0:T(8,128)(2,1)S(1)} %collective-permute-done.5.refs_3_.src_ref), custom_call_target="tpu_custom_call" | custom-call | flops 1073741824 | bytes 1048576 | tf_op jit(solution)/shard_map/helmholtz/pallas_call | solution.py:293
  22.8 1.1 %helmholtz.10 = (bf16[512,512]{1,0:T(8,128)(2,1)S(1)}, bf16[512,512]{1,0:T(8,128)(2,1)S(1)}) custom-call(bf16[512,64]{1,0:T(8,128)(2,1)S(1)} %target_matrix.1.tgt_ref, bf16[192,128]{1,0:T(8,128)(2,1)S(1)} %collective-permute-done.4.refs_2_.src_ref), custom_call_target="tpu_custom_call" | custom-call | flops 1073741824 | bytes 1048576 | tf_op jit(solution)/shard_map/helmholtz/pallas_call | solution.py:293
  24.0 1.1 %helmholtz.9 = (bf16[512,512]{1,0:T(8,128)(2,1)S(1)}, bf16[512,512]{1,0:T(8,128)(2,1)S(1)}) custom-call(bf16[512,64]{1,0:T(8,128)(2,1)S(1)} %target_matrix.1.tgt_ref, bf16[192,128]{1,0:T(8,128)(2,1)S(1)} %collective-permute-done.3.refs_1_.src_ref), custom_call_target="tpu_custom_call" | custom-call | flops 1073741824 | bytes 1048576 | tf_op jit(solution)/shard_map/helmholtz/pallas_call | solution.py:293
  25.5 1.0 %velocities.1.refs_0_ = bf16[4,32,128]{2,1,0:T(8,128)(2,1)S(1)} custom-call(s32[4,128]{1,0:T(4,128)S(1)} %get-tuple-element.41.cpl, bf16[192,128]{1,0:T(8,128)(2,1)S(1)} %get-tuple-element.42.refs_0_.src_ref, bf16[192,128]{1,0:T(8,128)(2,1)S(1)} %collective-permute-done.3.refs_1_.src_ref, bf16[192,128]{1,0:T(8,128)(2,1)S(1)} %collective-permute-done.4.refs_2_.src_ref, ...), custom_call_target="tpu_custom_call" | custom-call | tf_op jit(solution)/shard_map/velocities/pallas_call | solution.py:218
  26.5 3.4 %collective-permute-start.12 = (bf16[4,32,128]{2,1,0:T(8,128)(2,1)S(1)}, bf16[4,32,128]{2,1,0:T(8,128)(2,1)S(1)}, u32[]{:S(2)}, u32[]{:S(2)}) collective-permute-start(bf16[4,32,128]{2,1,0:T(8,128)(2,1)S(1)} %velocities.1.refs_0_), channel_id=1, source_target_pairs={{0,3},{1,2},{2,1},{3,0},{4,7},{5,6},{6,5},{7,4},{8,11},{9,10},{10,... | collective-permute-start | bytes 98312 | tf_op jit(solution)/shard_map/ppermute | solution.py:41
  30.0 1.0 %collective-permute-start.10 = (bf16[4,32,128]{2,1,0:T(8,128)(2,1)S(1)}, bf16[4,32,128]{2,1,0:T(8,128)(2,1)S(1)}, u32[]{:S(2)}, u32[]{:S(2)}) collective-permute-start(bf16[4,32,128]{2,1,0:T(8,128)(2,1)S(1)} %velocities.1.refs_0_), channel_id=1, source_target_pairs={{0,1},{1,0},{2,3},{3,2},{4,5},{5,4},{6,7},{7,6},{8,9},{9,8},{10,11... | collective-permute-start | bytes 98312 | tf_op jit(solution)/shard_map/ppermute | solution.py:41
  31.0 1.1 %helmholtz.15 = (bf16[512,512]{1,0:T(8,128)(2,1)S(1)}, bf16[512,512]{1,0:T(8,128)(2,1)S(1)}) custom-call(bf16[512,64]{1,0:T(8,128)(2,1)S(1)} %target_matrix.1.tgt_ref, bf16[4,192,128]{2,1,0:T(8,128)(2,1)S(1)} %collective-permute-done.6.refs_4_.src_ref), custom_call_target="tpu_custom_call" | custom-call | flops 1073741824 | bytes 1048576 | tf_op jit(solution)/shard_map/helmholtz/pallas_call | solution.py:293
  32.1 1.1 %helmholtz.14 = (bf16[512,512]{1,0:T(8,128)(2,1)S(1)}, bf16[512,512]{1,0:T(8,128)(2,1)S(1)}) custom-call(bf16[512,64]{1,0:T(8,128)(2,1)S(1)} %target_matrix.1.tgt_ref, bf16[4,192,128]{2,1,0:T(8,128)(2,1)S(1)} %collective-permute-done.6.refs_4_.src_ref), custom_call_target="tpu_custom_call" | custom-call | flops 1073741824 | bytes 1048576 | tf_op jit(solution)/shard_map/helmholtz/pallas_call | solution.py:293
  33.3 1.5 %collective-permute-done.11.refs_2_ = bf16[4,32,128]{2,1,0:T(8,128)(2,1)S(1)} collective-permute-done((bf16[4,32,128]{2,1,0:T(8,128)(2,1)S(1)}, bf16[4,32,128]{2,1,0:T(8,128)(2,1)S(1)}, u32[]{:S(2)}, u32[]{:S(2)}) %collective-permute-start.11) | collective-permute-done | bytes 32800 | tf_op jit(solution)/shard_map/ppermute | solution.py:41
  34.9 1.1 %helmholtz.13 = (bf16[512,512]{1,0:T(8,128)(2,1)S(1)}, bf16[512,512]{1,0:T(8,128)(2,1)S(1)}) custom-call(bf16[512,64]{1,0:T(8,128)(2,1)S(1)} %target_matrix.1.tgt_ref, bf16[4,192,128]{2,1,0:T(8,128)(2,1)S(1)} %collective-permute-done.6.refs_4_.src_ref), custom_call_target="tpu_custom_call" | custom-call | flops 1073741824 | bytes 1048576 | tf_op jit(solution)/shard_map/helmholtz/pallas_call | solution.py:293
  36.0 1.1 %helmholtz.12 = (bf16[512,512]{1,0:T(8,128)(2,1)S(1)}, bf16[512,512]{1,0:T(8,128)(2,1)S(1)}) custom-call(bf16[512,64]{1,0:T(8,128)(2,1)S(1)} %target_matrix.1.tgt_ref, bf16[4,192,128]{2,1,0:T(8,128)(2,1)S(1)} %collective-permute-done.6.refs_4_.src_ref), custom_call_target="tpu_custom_call" | custom-call | flops 1073741824 | bytes 1048576 | tf_op jit(solution)/shard_map/helmholtz/pallas_call | solution.py:293
  37.2 3.6 %pressures.1 = (bf16[4,32,128]{2,1,0:T(8,128)(2,1)S(1)}, f32[16,32,128]{2,1,0:T(8,128)S(1)}, bf16[16,32,128]{2,1,0:T(8,128)(2,1)S(1)}) custom-call(s32[4,128]{1,0:T(4,128)S(1)} %get-tuple-element.41.cpl, bf16[4,32,128]{2,1,0:T(8,128)(2,1)S(1)} %velocities.1.refs_0_, bf16[4,32,128]{2,1,0:T(8,128)(2,1)S(1)} %collective-permute-done.10.refs_1_, ...), custom_call_target="tpu_custom_call" | custom-call | tf_op jit(solution)/shard_map/pressures/pallas_call | solution.py:354
  40.7 0.6 %collective-permute-start.14 = (bf16[16,32,128]{2,1,0:T(8,128)(2,1)S(1)}, bf16[16,32,128]{2,1,0:T(8,128)(2,1)S(1)}, u32[]{:S(2)}, u32[]{:S(2)}) collective-permute-start(bf16[16,32,128]{2,1,0:T(8,128)(2,1)S(1)} %get-tuple-element.60), channel_id=1, source_target_pairs={{0,4},{4,0},{8,12},{12,8},{1,5},{5,1},{9,13},{13,9},{2,6},{6,2},{1... | collective-permute-start | bytes 393224 | tf_op jit(solution)/shard_map/ppermute | solution.py:45
  41.3 1.0 %collective-permute-done.14.got_ref = bf16[16,32,128]{2,1,0:T(8,128)(2,1)S(1)} collective-permute-done((bf16[16,32,128]{2,1,0:T(8,128)(2,1)S(1)}, bf16[16,32,128]{2,1,0:T(8,128)(2,1)S(1)}, u32[]{:S(2)}, u32[]{:S(2)}) %collective-permute-start.14) | collective-permute-done | bytes 131104 | tf_op jit(solution)/shard_map/ppermute | solution.py:45
  42.5 2.3 %collective-permute-start.16 = (bf16[4,32,128]{2,1,0:T(8,128)(2,1)S(1)}, bf16[4,32,128]{2,1,0:T(8,128)(2,1)S(1)}, u32[]{:S(2)}, u32[]{:S(2)}) collective-permute-start(bf16[4,32,128]{2,1,0:T(8,128)(2,1)S(1)} %get-tuple-element.63), channel_id=1, source_target_pairs={{0,2},{1,3},{2,0},{3,1},{4,6},{5,7},{6,4},{7,5},{8,10},{9,11},{10,... | collective-permute-start | bytes 98312 | tf_op jit(solution)/shard_map/ppermute | solution.py:41
  44.8 2.0 %collective-permute-start.17 = (bf16[4,32,128]{2,1,0:T(8,128)(2,1)S(1)}, bf16[4,32,128]{2,1,0:T(8,128)(2,1)S(1)}, u32[]{:S(2)}, u32[]{:S(2)}) collective-permute-start(bf16[4,32,128]{2,1,0:T(8,128)(2,1)S(1)} %get-tuple-element.64), channel_id=1, source_target_pairs={{0,3},{1,2},{2,1},{3,0},{4,7},{5,6},{6,5},{7,4},{8,11},{9,10},{10,... | collective-permute-start | bytes 98312 | tf_op jit(solution)/shard_map/ppermute | solution.py:41
  46.8 0.5 collective-permute-done.16.refs_2_
  47.3 3.2 %collective-permute-done.17.refs_3_ = bf16[4,32,128]{2,1,0:T(8,128)(2,1)S(1)} collective-permute-done((bf16[4,32,128]{2,1,0:T(8,128)(2,1)S(1)}, bf16[4,32,128]{2,1,0:T(8,128)(2,1)S(1)}, u32[]{:S(2)}, u32[]{:S(2)}) %collective-permute-start.17) | collective-permute-done | bytes 32800 | tf_op jit(solution)/shard_map/ppermute | solution.py:41
  50.6 0.5 collective-permute-start.18
  51.4 2.7 %collective-permute-start.20 = (bf16[2,32,128]{2,1,0:T(8,128)(2,1)S(1)}, bf16[2,32,128]{2,1,0:T(8,128)(2,1)S(1)}, u32[]{:S(2)}, u32[]{:S(2)}) collective-permute-start(bf16[2,32,128]{2,1,0:T(8,128)(2,1)S(1)} %get-tuple-element.69), channel_id=1, source_target_pairs={{0,24},{4,28},{8,16},{12,20},{16,8},{20,12},{24,0},{28,4},{1,25},{... | collective-permute-start | bytes 49160 | tf_op jit(solution)/shard_map/ppermute | solution.py:37
  54.7 1.3 %collective-permute-done.20.r3 = bf16[2,32,128]{2,1,0:T(8,128)(2,1)S(1)} collective-permute-done((bf16[2,32,128]{2,1,0:T(8,128)(2,1)S(1)}, bf16[2,32,128]{2,1,0:T(8,128)(2,1)S(1)}, u32[]{:S(2)}, u32[]{:S(2)}) %collective-permute-start.20) | collective-permute-done | bytes 16416 | tf_op jit(solution)/shard_map/ppermute | solution.py:37
  56.1 0.8 %outputs.1 = (f32[128,128]{1,0:T(8,128)}, bf16[128,128]{1,0:T(8,128)(2,1)}) custom-call(f32[2,32,128]{2,1,0:T(8,128)S(1)} %get-tuple-element.66.r0, bf16[2,32,128]{2,1,0:T(8,128)(2,1)S(1)} %collective-permute-done.18.r1, bf16[2,32,128]{2,1,0:T(8,128)(2,1)S(1)} %collective-permute-done.19.r2, bf16[2,32,128]{2,1,0:T(8,128)(2,1)S(1)} %collective-permute-done.20.r3), custom_call_target="tpu_custom_call" | custom-call | tf_op jit(solution)/shard_map/outputs/pallas_call | solution.py:433
  (32 shorter events, 2.8 us)
Async XLA Ops:
  0.6 7.3 %copy-start = (bf16[128,8,128]{2,1,0:T(8,128)(2,1)S(1)}, bf16[128,8,128]{2,1,0:T(8,128)(2,1)}, u32[]{:S(2)}) copy-start(bf16[128,8,128]{2,1,0:T(8,128)(2,1)} %param.8) | copy-start | bytes 786436
  3.4 8.1 %collective-permute-start = (bf16[80,128]{1,0:T(8,128)(2,1)S(1)}, bf16[80,128]{1,0:T(8,128)(2,1)S(1)}, u32[]{:S(2)}, u32[]{:S(2)}) collective-permute-start(bf16[80,128]{1,0:T(8,128)(2,1)S(1)} %get-tuple-element.38), channel_id=1, source_target_pairs={{0,16},{4,20},{8,24},{12,28},{16,0},{20,4},{24,8},{28,12},{1,17},{... | collective-permute-start | bytes 61448 | tf_op jit(solution)/shard_map/ppermute | solution.py:37
  6.4 5.1 %collective-permute-start.1 = (bf16[80,128]{1,0:T(8,128)(2,1)S(1)}, bf16[80,128]{1,0:T(8,128)(2,1)S(1)}, u32[]{:S(2)}, u32[]{:S(2)}) collective-permute-start(bf16[80,128]{1,0:T(8,128)(2,1)S(1)} %get-tuple-element.39), channel_id=1, source_target_pairs={{0,8},{4,12},{8,0},{12,4},{16,24},{20,28},{24,16},{28,20},{1,9},{5... | collective-permute-start | bytes 61448 | tf_op jit(solution)/shard_map/ppermute | solution.py:37
  7.9 5.0 %collective-permute-start.2 = (bf16[80,128]{1,0:T(8,128)(2,1)S(1)}, bf16[80,128]{1,0:T(8,128)(2,1)S(1)}, u32[]{:S(2)}, u32[]{:S(2)}) collective-permute-start(bf16[80,128]{1,0:T(8,128)(2,1)S(1)} %get-tuple-element.40), channel_id=1, source_target_pairs={{0,24},{4,28},{8,16},{12,20},{16,8},{20,12},{24,0},{28,4},{1,25},{... | collective-permute-start | bytes 61448 | tf_op jit(solution)/shard_map/ppermute | solution.py:37
  8.0 17.1 %collective-permute-start.9 = (bf16[128,1024]{1,0:T(8,128)(2,1)S(1)}, bf16[128,1024]{1,0:T(8,128)(2,1)S(1)}, u32[]{:S(2)}, u32[]{:S(2)}) collective-permute-start(bf16[128,1024]{1,0:T(8,128)(2,1)S(1)} %bitcast.5), channel_id=1, source_target_pairs={{0,24},{4,28},{8,16},{12,20},{16,8},{20,12},{24,0},{28,4},{1,25},{... | collective-permute-start | bytes 786440 | tf_op jit(solution)/shard_map/ppermute | solution.py:37
  11.0 14.2 %collective-permute-start.8 = (bf16[128,1024]{1,0:T(8,128)(2,1)S(1)}, bf16[128,1024]{1,0:T(8,128)(2,1)S(1)}, u32[]{:S(2)}, u32[]{:S(2)}) collective-permute-start(bf16[128,1024]{1,0:T(8,128)(2,1)S(1)} %bitcast.6), channel_id=1, source_target_pairs={{0,8},{4,12},{8,0},{12,4},{16,24},{20,28},{24,16},{28,20},{1,9},{5... | collective-permute-start | bytes 786440 | tf_op jit(solution)/shard_map/ppermute | solution.py:37
  13.0 6.2 %collective-permute-start.5 = (bf16[192,128]{1,0:T(8,128)(2,1)S(1)}, bf16[192,128]{1,0:T(8,128)(2,1)S(1)}, u32[]{:S(2)}, u32[]{:S(2)}) collective-permute-start(bf16[192,128]{1,0:T(8,128)(2,1)S(1)} %get-tuple-element.42.refs_0_.src_ref), channel_id=1, source_target_pairs={{0,3},{1,2},{2,1},{3,0},{4,7},{5,6},{6,5},{7,4},{8,11},{9,10},{10,... | collective-permute-start | bytes 147464 | tf_op jit(solution)/shard_map/ppermute | solution.py:41
  16.6 5.0 %collective-permute-start.4 = (bf16[192,128]{1,0:T(8,128)(2,1)S(1)}, bf16[192,128]{1,0:T(8,128)(2,1)S(1)}, u32[]{:S(2)}, u32[]{:S(2)}) collective-permute-start(bf16[192,128]{1,0:T(8,128)(2,1)S(1)} %get-tuple-element.42.refs_0_.src_ref), channel_id=1, source_target_pairs={{0,2},{1,3},{2,0},{3,1},{4,6},{5,7},{6,4},{7,5},{8,10},{9,11},{10,... | collective-permute-start | bytes 147464 | tf_op jit(solution)/shard_map/ppermute | solution.py:41
  16.6 5.0 %collective-permute-start.3 = (bf16[192,128]{1,0:T(8,128)(2,1)S(1)}, bf16[192,128]{1,0:T(8,128)(2,1)S(1)}, u32[]{:S(2)}, u32[]{:S(2)}) collective-permute-start(bf16[192,128]{1,0:T(8,128)(2,1)S(1)} %get-tuple-element.42.refs_0_.src_ref), channel_id=1, source_target_pairs={{0,1},{1,0},{2,3},{3,2},{4,5},{5,4},{6,7},{7,6},{8,9},{9,8},{10,11... | collective-permute-start | bytes 147464 | tf_op jit(solution)/shard_map/ppermute | solution.py:41
  19.1 6.4 %collective-permute-start.7 = (bf16[128,1024]{1,0:T(8,128)(2,1)S(1)}, bf16[128,1024]{1,0:T(8,128)(2,1)S(1)}, u32[]{:S(2)}, u32[]{:S(2)}) collective-permute-start(bf16[128,1024]{1,0:T(8,128)(2,1)S(1)} %bitcast.7), channel_id=1, source_target_pairs={{0,16},{4,20},{8,24},{12,28},{16,0},{20,4},{24,8},{28,12},{1,17},{... | collective-permute-start | bytes 786440 | tf_op jit(solution)/shard_map/ppermute | solution.py:37
  21.6 3.9 %collective-permute-start.6 = (bf16[4,192,128]{2,1,0:T(8,128)(2,1)S(1)}, bf16[4,192,128]{2,1,0:T(8,128)(2,1)S(1)}, u32[]{:S(2)}, u32[]{:S(2)}) collective-permute-start(bf16[4,192,128]{2,1,0:T(8,128)(2,1)S(1)} %stack.2), channel_id=1, source_target_pairs={{0,4},{4,0},{8,12},{12,8},{1,5},{5,1},{9,13},{13,9},{2,6},{6,2},{1... | collective-permute-start | bytes 589832 | tf_op jit(solution)/shard_map/ppermute | solution.py:45
  26.5 6.7 %collective-permute-start.12 = (bf16[4,32,128]{2,1,0:T(8,128)(2,1)S(1)}, bf16[4,32,128]{2,1,0:T(8,128)(2,1)S(1)}, u32[]{:S(2)}, u32[]{:S(2)}) collective-permute-start(bf16[4,32,128]{2,1,0:T(8,128)(2,1)S(1)} %velocities.1.refs_0_), channel_id=1, source_target_pairs={{0,3},{1,2},{2,1},{3,0},{4,7},{5,6},{6,5},{7,4},{8,11},{9,10},{10,... | collective-permute-start | bytes 98312 | tf_op jit(solution)/shard_map/ppermute | solution.py:41
  30.0 4.8 %collective-permute-start.11 = (bf16[4,32,128]{2,1,0:T(8,128)(2,1)S(1)}, bf16[4,32,128]{2,1,0:T(8,128)(2,1)S(1)}, u32[]{:S(2)}, u32[]{:S(2)}) collective-permute-start(bf16[4,32,128]{2,1,0:T(8,128)(2,1)S(1)} %velocities.1.refs_0_), channel_id=1, source_target_pairs={{0,2},{1,3},{2,0},{3,1},{4,6},{5,7},{6,4},{7,5},{8,10},{9,11},{10,... | collective-permute-start | bytes 98312 | tf_op jit(solution)/shard_map/ppermute | solution.py:41
  30.0 4.8 %collective-permute-start.10 = (bf16[4,32,128]{2,1,0:T(8,128)(2,1)S(1)}, bf16[4,32,128]{2,1,0:T(8,128)(2,1)S(1)}, u32[]{:S(2)}, u32[]{:S(2)}) collective-permute-start(bf16[4,32,128]{2,1,0:T(8,128)(2,1)S(1)} %velocities.1.refs_0_), channel_id=1, source_target_pairs={{0,1},{1,0},{2,3},{3,2},{4,5},{5,4},{6,7},{7,6},{8,9},{9,8},{10,11... | collective-permute-start | bytes 98312 | tf_op jit(solution)/shard_map/ppermute | solution.py:41
  34.8 2.3 %collective-permute-start.13 = (bf16[4,4,32,128]{3,2,1,0:T(8,128)(2,1)S(1)}, bf16[4,4,32,128]{3,2,1,0:T(8,128)(2,1)S(1)}, u32[]{:S(2)}, u32[]{:S(2)}) collective-permute-start(bf16[4,4,32,128]{3,2,1,0:T(8,128)(2,1)S(1)} %stack.3), channel_id=1, source_target_pairs={{0,4},{4,0},{8,12},{12,8},{1,5},{5,1},{9,13},{13,9},{2,6},{6,2},{1... | collective-permute-start | bytes 393224 | tf_op jit(solution)/shard_map/ppermute | solution.py:45
  40.7 1.6 %collective-permute-start.14 = (bf16[16,32,128]{2,1,0:T(8,128)(2,1)S(1)}, bf16[16,32,128]{2,1,0:T(8,128)(2,1)S(1)}, u32[]{:S(2)}, u32[]{:S(2)}) collective-permute-start(bf16[16,32,128]{2,1,0:T(8,128)(2,1)S(1)} %get-tuple-element.60), channel_id=1, source_target_pairs={{0,4},{4,0},{8,12},{12,8},{1,5},{5,1},{9,13},{13,9},{2,6},{6,2},{1... | collective-permute-start | bytes 393224 | tf_op jit(solution)/shard_map/ppermute | solution.py:45
  42.3 4.5 %collective-permute-start.15 = (bf16[4,32,128]{2,1,0:T(8,128)(2,1)S(1)}, bf16[4,32,128]{2,1,0:T(8,128)(2,1)S(1)}, u32[]{:S(2)}, u32[]{:S(2)}) collective-permute-start(bf16[4,32,128]{2,1,0:T(8,128)(2,1)S(1)} %get-tuple-element.62), channel_id=1, source_target_pairs={{0,1},{1,0},{2,3},{3,2},{4,5},{5,4},{6,7},{7,6},{8,9},{9,8},{10,11... | collective-permute-start | bytes 98312 | tf_op jit(solution)/shard_map/ppermute | solution.py:41
  42.5 4.8 %collective-permute-start.16 = (bf16[4,32,128]{2,1,0:T(8,128)(2,1)S(1)}, bf16[4,32,128]{2,1,0:T(8,128)(2,1)S(1)}, u32[]{:S(2)}, u32[]{:S(2)}) collective-permute-start(bf16[4,32,128]{2,1,0:T(8,128)(2,1)S(1)} %get-tuple-element.63), channel_id=1, source_target_pairs={{0,2},{1,3},{2,0},{3,1},{4,6},{5,7},{6,4},{7,5},{8,10},{9,11},{10,... | collective-permute-start | bytes 98312 | tf_op jit(solution)/shard_map/ppermute | solution.py:41
  44.8 5.7 %collective-permute-start.17 = (bf16[4,32,128]{2,1,0:T(8,128)(2,1)S(1)}, bf16[4,32,128]{2,1,0:T(8,128)(2,1)S(1)}, u32[]{:S(2)}, u32[]{:S(2)}) collective-permute-start(bf16[4,32,128]{2,1,0:T(8,128)(2,1)S(1)} %get-tuple-element.64), channel_id=1, source_target_pairs={{0,3},{1,2},{2,1},{3,0},{4,7},{5,6},{6,5},{7,4},{8,11},{9,10},{10,... | collective-permute-start | bytes 98312 | tf_op jit(solution)/shard_map/ppermute | solution.py:41
  50.6 3.8 %collective-permute-start.18 = (bf16[2,32,128]{2,1,0:T(8,128)(2,1)S(1)}, bf16[2,32,128]{2,1,0:T(8,128)(2,1)S(1)}, u32[]{:S(2)}, u32[]{:S(2)}) collective-permute-start(bf16[2,32,128]{2,1,0:T(8,128)(2,1)S(1)} %get-tuple-element.67), channel_id=1, source_target_pairs={{0,16},{4,20},{8,24},{12,28},{16,0},{20,4},{24,8},{28,12},{1,17},{... | collective-permute-start | bytes 49160 | tf_op jit(solution)/shard_map/ppermute | solution.py:37
  51.0 3.7 %collective-permute-start.19 = (bf16[2,32,128]{2,1,0:T(8,128)(2,1)S(1)}, bf16[2,32,128]{2,1,0:T(8,128)(2,1)S(1)}, u32[]{:S(2)}, u32[]{:S(2)}) collective-permute-start(bf16[2,32,128]{2,1,0:T(8,128)(2,1)S(1)} %get-tuple-element.68), channel_id=1, source_target_pairs={{0,8},{4,12},{8,0},{12,4},{16,24},{20,28},{24,16},{28,20},{1,9},{5... | collective-permute-start | bytes 49160 | tf_op jit(solution)/shard_map/ppermute | solution.py:37
  51.4 4.6 %collective-permute-start.20 = (bf16[2,32,128]{2,1,0:T(8,128)(2,1)S(1)}, bf16[2,32,128]{2,1,0:T(8,128)(2,1)S(1)}, u32[]{:S(2)}, u32[]{:S(2)}) collective-permute-start(bf16[2,32,128]{2,1,0:T(8,128)(2,1)S(1)} %get-tuple-element.69), channel_id=1, source_target_pairs={{0,24},{4,28},{8,16},{12,20},{16,8},{20,12},{24,0},{28,4},{1,25},{... | collective-permute-start | bytes 49160 | tf_op jit(solution)/shard_map/ppermute | solution.py:37

commit v4 on v3

--- a/solution.py
+++ b/solution.py
@@ -144,12 +144,13 @@
             pltpu.SemaphoreType.DMA((4 + blocks,)),
         ],
         compiler_params=limit(12),
-        cost_estimate=pl.CostEstimate(flops=4 * rows * depth * width, bytes_accessed=4 * rows * depth, transcendentals=0),
+        cost_estimate=pl.CostEstimate(flops=4 * rows * depth * width, bytes_accessed=1, transcendentals=0),
         name="amplitude_parts",
     )(receptance, loads, xyz, area, coupling)
 
 
-def amplitude_sum_kernel(own_ref, geo_ref, x_ref, y_ref, d_ref, out_ref, cpl_ref):
+def amplitude_sum_kernel(count, *refs):
+    own_ref, geo_ref, d_ref, x_ref, y_ref, out_ref, cpl_ref = refs[count:]
     n = own_ref.shape[0]
     out_ref[0:n, :] = (own_ref[...] + x_ref[0:n, :].astype(f32)).astype(bf16)
     out_ref[n : 2 * n, :] = (y_ref[0:n, :].astype(f32) + d_ref[0:n, :].astype(f32)).astype(bf16)
@@ -159,16 +160,16 @@
         cpl_ref[i : i + 1, :] = g.astype(f32)[GEO - 1 :, :].astype(jnp.int32)
 
 
-def amplitude_sum(own, geo, x, y, d):
+def amplitude_sum(early, own, geo, x, y, d):
     n = own.shape[0]
     return pl.pallas_call(
-        amplitude_sum_kernel,
-        in_specs=[VMEM] * 5,
+        functools.partial(amplitude_sum_kernel, len(early)),
+        in_specs=[pl.BlockSpec(memory_space=pl.ANY)] * len(early) + [VMEM] * 5,
         out_specs=[VMEM] * 2,
         out_shape=[jax.ShapeDtypeStruct((2 * n + 4 * GEO, 128), bf16), jax.ShapeDtypeStruct((4, 128), jnp.int32)],
         compiler_params=limit(4),
         name="amplitude_sum",
-    )(own, geo, x, y, d)
+    )(*early, own, geo, d, x, y)
 
 
 def stack_kernel(*refs):
@@ -243,7 +244,7 @@
         mat[9:12, col] = jnp.ones((3, lanes), f32)
         for i, part in enumerate(three_parts(norm)):
             mat[3 * GEO + i : 3 * GEO + i + 1, col] = part
-    out_ref[...] = mat[...].T.astype(bf16)
+    out_ref[...] = mat[...].astype(bf16)
 
 
 def target_matrix(panels, geo):
@@ -252,54 +253,47 @@
         functools.partial(target_kernel, panels),
         in_specs=[VMEM],
         out_specs=VMEM,
-        out_shape=jax.ShapeDtypeStruct((side, 4 * GEO), bf16),
+        out_shape=jax.ShapeDtypeStruct((4 * GEO, side), bf16),
         scratch_shapes=[pltpu.VMEM((4 * GEO, side), f32)],
         compiler_params=limit(4),
         name="target_matrix",
     )(geo)
 
 
-def helmholtz_kernel(at, tgt_ref, src_ref, re_ref, im_ref, dist):
+def helmholtz_kernel(at, tgt_ref, src_ref, *refs):
+    re_ref, im_ref = refs[-2:]
     src = src_ref if at is None else src_ref.at[at]
-    side = tgt_ref.shape[0]
+    side = tgt_ref.shape[1]
     first = src.shape[0] - side // 128 * GEO
-    wide = jnp.concatenate([src[first + j * GEO : first + (j + 1) * GEO, :] for j in range(side // 128)], axis=1)
-    full = jnp.concatenate([wide, wide, wide, jnp.ones_like(wide)], axis=0)
-    dist[...] = jnp.dot(tgt_ref[...], full, preferred_element_type=f32)
-    strip, span = 16, 256
     c0, c1, c2 = (c / cos_terms[3] for c in cos_terms[:3])
-
-    def step(i, _):
-        rows = pl.ds(pl.multiple_of(i * strip, strip), strip)
-        for n in range(side // span):
-            cols = slice(n * span, (n + 1) * span)
-            square = dist[rows, cols]
-            inverse = lax.rsqrt(square)
-            t = square * inverse
-            f = t - jnp.round(t)
-            u = f * f
-            s = (((sin_terms[3] * u + sin_terms[2]) * u + sin_terms[1]) * u + sin_terms[0]) * f
-            c = ((u + c2) * u + c1) * u + c0
-            part = s * inverse
-            re_ref[rows, cols] = (inverse - s * part).astype(bf16)
-            im_ref[rows, cols] = (c * part).astype(bf16)
-        return 0
-
-    lax.fori_loop(0, side // strip, step, 0, unroll=4)
-
-
-def helmholtz(targets, payload, at=None):
-    side = targets.shape[0]
+    strip = 128
+    for r in range(0, side, strip):
+        at_row = first + r // 128 * GEO
+        one = src[at_row : at_row + GEO, :]
+        full = jnp.concatenate([one, one, one, jnp.ones_like(one)], axis=0)
+        square = lax.dot_general(full, tgt_ref[...], (((0,), (0,)), ((), ())), preferred_element_type=f32)
+        inverse = lax.rsqrt(square)
+        t = square * inverse
+        f = t - jnp.round(t)
+        u = f * f
+        s = (((sin_terms[3] * u + sin_terms[2]) * u + sin_terms[1]) * u + sin_terms[0]) * f
+        c = ((u + c2) * u + c1) * u + c0
+        part = s * inverse
+        re_ref[r : r + strip, :] = (inverse - s * part).astype(bf16)
+        im_ref[r : r + strip, :] = (c * part).astype(bf16)
+
+
+def helmholtz(targets, payload, at=None, after=(), cost=1.0):
+    side = targets.shape[1]
     return pl.pallas_call(
         functools.partial(helmholtz_kernel, at),
-        in_specs=[VMEM] * 2,
+        in_specs=[VMEM] * 2 + [pl.BlockSpec(memory_space=pl.ANY)] * len(after),
         out_specs=[VMEM] * 2,
         out_shape=[jax.ShapeDtypeStruct((side, side), bf16)] * 2,
-        scratch_shapes=[pltpu.VMEM((side, side), f32)],
         compiler_params=limit(4),
-        cost_estimate=pl.CostEstimate(flops=4096 * side * side, bytes_accessed=4 * side * side, transcendentals=side * side),
+        cost_estimate=pl.CostEstimate(flops=int(cost * 4000 * side * side), bytes_accessed=1, transcendentals=0),
         name="helmholtz",
-    )(targets, payload)
+    )(targets, payload, *after)
 
 
 def pressure_kernel(secs, tgt_n, cpl, *refs):
@@ -317,13 +311,12 @@
             lead[:, col] = v
             turned[0:half, col] = -v[half:]
             turned[half:, col] = v[0:half]
-    dims = (((1,), (1,)), ((), ()))
     re = im = 0.0
     for i in range(2 * secs):
         col = slice(i * side, (i + 1) * side)
-        re += lax.dot_general(mats[2 * i][...], lead[:, col], dims, preferred_element_type=f32)
-        im += lax.dot_general(mats[2 * i + 1][...], turned[:, col], dims, preferred_element_type=f32)
-    p = (re + im * cos_terms[3]).T.astype(bf16)
+        re += jnp.dot(lead[:, col], mats[2 * i][...], preferred_element_type=f32)
+        im += jnp.dot(turned[:, col], mats[2 * i + 1][...], preferred_element_type=f32)
+    p = (re + im * cos_terms[3]).astype(bf16)
     total[...] = jnp.zeros_like(total)
     x, y, c, z = place()
     sec_bits, tgt_bits = bits_of(secs), bits_of(tgt_n)
@@ -392,7 +385,7 @@
 
 
 def sec_sum_kernel(count, *refs):
-    own, got, pt, outs = refs[0], refs[1 : 1 + count], refs[1 + count], refs[2 + count :]
+    own, got, pt, outs = refs[0], refs[count:0:-1], refs[1 + count], refs[2 + count :]
     for j, out in enumerate(outs):
         value = own[j]
         for g in got:
@@ -410,10 +403,10 @@
         out_shape=[jax.ShapeDtypeStruct(shape, f32)] + [jax.ShapeDtypeStruct(shape, bf16)] * 3,
         compiler_params=limit(4),
         name="sec_sum",
-    )(own, *got, pt)
-
-
-def output_kernel(r0, r1, r2, r3, loads_ref, press_ref, loads_t, press_t):
+    )(own, *got[::-1], pt)
+
+
+def output_kernel(r0, r3, r1, r2, loads_ref, press_ref, loads_t, press_t):
     half = loads_t.shape[0] // 2
     quarter = half // 4
     x, y, _, _ = place()
@@ -437,7 +430,7 @@
         scratch_shapes=[pltpu.VMEM((cols, lanes), f32)] * 2,
         compiler_params=limit(4),
         name="outputs",
-    )(*parts)
+    )(parts[0], parts[3], parts[1], parts[2])
 
 
 def on_device_fast(modal_loads, receptance, shapes, coupling, panel_coords, panel_areas):
@@ -454,16 +447,18 @@
     ]
     own, s1, s2, s3, geo = amplitude_parts(panels, *held)
     got = [exchange_plane(s, m) for m, s in ((1, s1), (2, s2), (3, s3))]
-    flat = shapes.reshape(pan_dev, -1)
-    modes = [flat] + [exchange_plane(flat, m) for m in (1, 2, 3)]
-    payload, cpl = amplitude_sum(own, geo, *got)
+    modes = [shapes] + [exchange_plane(shapes, m) for m in (1, 2)]
+    modes.append(exchange_plane(modes[1], 2))
+    early = modes[1:3]
+    modes = [m.reshape(pan_dev, -1) for m in modes]
+    payload, cpl = amplitude_sum(early, own, geo, *got)
     near = [payload] + [exchange_sec(payload, m) for m in range(1, secs)]
     far = exchange_core(stack(near))
     targets = payload[-4 * GEO :, :]
     across = target_matrix(panels, targets)
-    mats = [helmholtz(across, n) for n in near] + [helmholtz(across, far, i) for i in range(secs)]
+    vel = velocities(panels, cpl, near, far, modes, width, blocks)
+    mats = [helmholtz(across, n) for n in near] + [helmholtz(across, far, i, (vel,), 1.4) for i in range(secs)]
     mats = [m for pair in mats for m in pair]
-    vel = velocities(panels, cpl, near, far, modes, width, blocks)
     v_near = [vel] + [exchange_sec(vel, m) for m in range(1, secs)]
     v_far = exchange_core(stack(v_near))
     pt, n_near, n_far = pressures(cpl, v_near, v_far, mats, targets, modes, tgts)

time: 57 us -> 55.8 us (0.979)
  Pallas kernels: 17.3 us -> 14.7 us
  starting transfers between devices: 25.9 us -> 26.9 us
    ppermute x9, waiting for transfers between devices: 7.9 us -> 5.59 us  [exchange_sec(): lax.ppermute(x, 'sec', [(s, s ^ mask) for s in range(lax.axis_size('sec'))])]
    ppermute x9, waiting for transfers between devices: 3.84 us -> 5.84 us  [exchange_plane(): return lax.ppermute(x, ('blk', 'tgt'), pairs)]
    pallas_call x8, Pallas kernels: 9 us -> 7.55 us  [helmholtz(): pl.pallas_call(functools.partial(helmholtz_kernel, at), in_specs=[VMEM] *...]
    ppermute x9, starting transfers between devices: 11.8 us -> 13.2 us  [exchange_plane(): return lax.ppermute(x, ('blk', 'tgt'), pairs)]
    pallas_call x1, Pallas kernels: 3.57 us -> 2.53 us  [pressures(): pl.pallas_call(functools.partial(pressure_kernel, secs, tgt_n), in_specs=...]
    ppermute x3, waiting for transfers between devices: 0.99 us -> 1.58 us  [exchange_core(): lax.ppermute(x, 'tgt', [(t, t ^ 1) for t in range(lax.axis_size('tgt'))])]
  transfers between devices with their start and end apart: 21 -> 21, of which waited for: 11 -> 12; matrix products, arithmetic and copies ran while one was open for 0% -> 0% of each run, Pallas kernels for 16% -> 19%
where the time goes in v4:
time: 55.8 us; the launch traced here: 55.6 us
  starting transfers between devices  26.9 us (48%)
  Pallas kernels  14.7 us (26%)
  waiting for transfers between devices  13 us (23%)
  between operations  0.81 us (1%)
    ppermute x9, starting transfers between devices, exchange_sec(): lax.ppermute(x, 'sec', [(s, s ^ mask) for s in range(lax.axis_size('sec'))])  13.4 us
    ppermute x9, starting transfers between devices, exchange_plane(): return lax.ppermute(x, ('blk', 'tgt'), pairs)  13.2 us
    pallas_call x8, Pallas kernels, helmholtz(): pl.pallas_call(functools.partial(helmholtz_kernel, at), in_specs=[VMEM] *...  7.55 us
    ppermute x9, waiting for transfers between devices, exchange_plane(): return lax.ppermute(x, ('blk', 'tgt'), pairs)  5.84 us
    ppermute x9, waiting for transfers between devices, exchange_sec(): lax.ppermute(x, 'sec', [(s, s ^ mask) for s in range(lax.axis_size('sec'))])  5.59 us
    pallas_call x1, Pallas kernels, amplitude_parts(): pl.pallas_call(functools.partial(amplitude_kernel, panels), in_specs=[HBM...  2.7 us
    pallas_call x1, Pallas kernels, pressures(): pl.pallas_call(functools.partial(pressure_kernel, secs, tgt_n), in_specs=...  2.53 us
    ppermute x3, waiting for transfers between devices, exchange_core(): lax.ppermute(x, 'tgt', [(t, t ^ 1) for t in range(lax.axis_size('tgt'))])  1.58 us
  transfers between devices with their start and end apart: 21, of which 12 were waited for; matrix products, arithmetic and copies ran while one was open for 0% of the time, Pallas kernels for 19%

profile of v4, /device:TPU:0, one launch (start us, length us, event | category | flops | bytes accessed | tf_op | source)
XLA Modules:
  0.0 55.6 jit_solution(2289800829634707702)
XLA Ops:
  0.6 3.0 %collective-permute-start = (bf16[128,8,128]{2,1,0:T(8,128)(2,1)}, bf16[128,8,128]{2,1,0:T(8,128)(2,1)S(1)}, u32[]{:S(2)}, u32[]{:S(2)}) collective-permute-start(bf16[128,8,128]{2,1,0:T(8,128)(2,1)} %param.8), channel_id=1, source_target_pairs={{0,16},{4,20},{8,24},{12,28},{16,0},{20,4},{24,8},{28,12},{1,17},{... | collective-permute-start | bytes 786440 | tf_op jit(solution)/shard_map/ppermute | solution.py:37
  3.6 1.5 %collective-permute-start.1 = (bf16[128,8,128]{2,1,0:T(8,128)(2,1)}, bf16[128,8,128]{2,1,0:T(8,128)(2,1)S(1)}, u32[]{:S(2)}, u32[]{:S(2)}) collective-permute-start(bf16[128,8,128]{2,1,0:T(8,128)(2,1)} %param.8), channel_id=1, source_target_pairs={{0,8},{4,12},{8,0},{12,4},{16,24},{20,28},{24,16},{28,20},{1,9},{5... | collective-permute-start | bytes 786440 | tf_op jit(solution)/shard_map/ppermute | solution.py:37
  5.2 2.7 %amplitude_parts.1 = (f32[64,128]{1,0:T(8,128)S(1)}, bf16[80,128]{1,0:T(8,128)(2,1)S(1)}, bf16[80,128]{1,0:T(8,128)(2,1)S(1)}, bf16[80,128]{1,0:T(8,128)(2,1)S(1)}, bf16[16,128]{1,0:T(8,128)(2,1)S(1)}) custom-call(bf16[2,256,2048]{2,1,0:T(8,128)(2,1)} %r_hbm.1, bf16[2048,128]{1,0:T(8,128)(2,1)} %l_hbm.1, f32[3,128]{1,0:T(4,128)} %xyz_hbm.1, ...), custom_call_target="tpu_custom_call" | custom-call | flops 268435456 | bytes 1 | tf_op jit(solution)/shard_map/amplitude_parts/pallas_call | solution.py:131
  8.0 1.9 %collective-permute-start.3 = (bf16[80,128]{1,0:T(8,128)(2,1)S(1)}, bf16[80,128]{1,0:T(8,128)(2,1)S(1)}, u32[]{:S(2)}, u32[]{:S(2)}) collective-permute-start(bf16[80,128]{1,0:T(8,128)(2,1)S(1)} %get-tuple-element.39), channel_id=1, source_target_pairs={{0,16},{4,20},{8,24},{12,28},{16,0},{20,4},{24,8},{28,12},{1,17},{... | collective-permute-start | bytes 61448 | tf_op jit(solution)/shard_map/ppermute | solution.py:37
  9.9 1.5 %collective-permute-start.4 = (bf16[80,128]{1,0:T(8,128)(2,1)S(1)}, bf16[80,128]{1,0:T(8,128)(2,1)S(1)}, u32[]{:S(2)}, u32[]{:S(2)}) collective-permute-start(bf16[80,128]{1,0:T(8,128)(2,1)S(1)} %get-tuple-element.40), channel_id=1, source_target_pairs={{0,8},{4,12},{8,0},{12,4},{16,24},{20,28},{24,16},{28,20},{1,9},{5... | collective-permute-start | bytes 61448 | tf_op jit(solution)/shard_map/ppermute | solution.py:37
  11.5 1.1 %collective-permute-done.2.refs_4_ = bf16[80,128]{1,0:T(8,128)(2,1)S(1)} collective-permute-done((bf16[80,128]{1,0:T(8,128)(2,1)S(1)}, bf16[80,128]{1,0:T(8,128)(2,1)S(1)}, u32[]{:S(2)}, u32[]{:S(2)}) %collective-permute-start.2) | collective-permute-done | bytes 20512 | tf_op jit(solution)/shard_map/ppermute | solution.py:37
  12.6 1.1 %collective-permute-done.4.refs_6_ = bf16[80,128]{1,0:T(8,128)(2,1)S(1)} collective-permute-done((bf16[80,128]{1,0:T(8,128)(2,1)S(1)}, bf16[80,128]{1,0:T(8,128)(2,1)S(1)}, u32[]{:S(2)}, u32[]{:S(2)}) %collective-permute-start.4) | collective-permute-done | bytes 20512 | tf_op jit(solution)/shard_map/ppermute | solution.py:37
  13.7 3.7 %collective-permute-start.7 = (bf16[192,128]{1,0:T(8,128)(2,1)S(1)}, bf16[192,128]{1,0:T(8,128)(2,1)S(1)}, u32[]{:S(2)}, u32[]{:S(2)}) collective-permute-start(bf16[192,128]{1,0:T(8,128)(2,1)S(1)} %get-tuple-element.42.refs_0_.src_ref), channel_id=1, source_target_pairs={{0,3},{1,2},{2,1},{3,0},{4,7},{5,6},{6,5},{7,4},{8,11},{9,10},{10,... | collective-permute-start | bytes 147464 | tf_op jit(solution)/shard_map/ppermute | solution.py:41
  17.4 0.8 %collective-permute-start.5 = (bf16[192,128]{1,0:T(8,128)(2,1)S(1)}, bf16[192,128]{1,0:T(8,128)(2,1)S(1)}, u32[]{:S(2)}, u32[]{:S(2)}) collective-permute-start(bf16[192,128]{1,0:T(8,128)(2,1)S(1)} %get-tuple-element.42.refs_0_.src_ref), channel_id=1, source_target_pairs={{0,1},{1,0},{2,3},{3,2},{4,5},{5,4},{6,7},{7,6},{8,9},{9,8},{10,11... | collective-permute-start | bytes 147464 | tf_op jit(solution)/shard_map/ppermute | solution.py:41
  18.2 0.9 %helmholtz.8 = (bf16[512,512]{1,0:T(8,128)(2,1)S(1)}, bf16[512,512]{1,0:T(8,128)(2,1)S(1)}) custom-call(bf16[64,512]{1,0:T(8,128)(2,1)S(1)} %target_matrix.1.tgt_ref, bf16[192,128]{1,0:T(8,128)(2,1)S(1)} %get-tuple-element.42.refs_0_.src_ref), custom_call_target="tpu_custom_call" | custom-call | flops 1048576000 | bytes 1 | tf_op jit(solution)/shard_map/helmholtz/pallas_call | solution.py:288
  19.3 1.6 %collective-permute-start.9 = (bf16[128,8,128]{2,1,0:T(8,128)(2,1)S(1)}, bf16[128,8,128]{2,1,0:T(8,128)(2,1)S(1)}, u32[]{:S(2)}, u32[]{:S(2)}) collective-permute-start(bf16[128,8,128]{2,1,0:T(8,128)(2,1)S(1)} %collective-permute-done.refs_0_), channel_id=1, source_target_pairs={{0,8},{4,12},{8,0},{12,4},{16,24},{20,28},{24,16},{28,20},{1,9},{5... | collective-permute-start | bytes 786440 | tf_op jit(solution)/shard_map/ppermute | solution.py:37
  20.9 1.5 %collective-permute-done.6.refs_2_.src_ref = bf16[192,128]{1,0:T(8,128)(2,1)S(1)} collective-permute-done((bf16[192,128]{1,0:T(8,128)(2,1)S(1)}, bf16[192,128]{1,0:T(8,128)(2,1)S(1)}, u32[]{:S(2)}, u32[]{:S(2)}) %collective-permute-start.6) | collective-permute-done | bytes 49184 | tf_op jit(solution)/shard_map/ppermute | solution.py:41
  22.5 0.9 %helmholtz.11 = (bf16[512,512]{1,0:T(8,128)(2,1)S(1)}, bf16[512,512]{1,0:T(8,128)(2,1)S(1)}) custom-call(bf16[64,512]{1,0:T(8,128)(2,1)S(1)} %target_matrix.1.tgt_ref, bf16[192,128]{1,0:T(8,128)(2,1)S(1)} %collective-permute-done.7.refs_3_.src_ref), custom_call_target="tpu_custom_call" | custom-call | flops 1048576000 | bytes 1 | tf_op jit(solution)/shard_map/helmholtz/pallas_call | solution.py:288
  23.4 0.9 %helmholtz.10 = (bf16[512,512]{1,0:T(8,128)(2,1)S(1)}, bf16[512,512]{1,0:T(8,128)(2,1)S(1)}) custom-call(bf16[64,512]{1,0:T(8,128)(2,1)S(1)} %target_matrix.1.tgt_ref, bf16[192,128]{1,0:T(8,128)(2,1)S(1)} %collective-permute-done.6.refs_2_.src_ref), custom_call_target="tpu_custom_call" | custom-call | flops 1048576000 | bytes 1 | tf_op jit(solution)/shard_map/helmholtz/pallas_call | solution.py:288
  24.4 0.9 %helmholtz.9 = (bf16[512,512]{1,0:T(8,128)(2,1)S(1)}, bf16[512,512]{1,0:T(8,128)(2,1)S(1)}) custom-call(bf16[64,512]{1,0:T(8,128)(2,1)S(1)} %target_matrix.1.tgt_ref, bf16[192,128]{1,0:T(8,128)(2,1)S(1)} %collective-permute-done.5.refs_1_.src_ref), custom_call_target="tpu_custom_call" | custom-call | flops 1048576000 | bytes 1 | tf_op jit(solution)/shard_map/helmholtz/pallas_call | solution.py:288
  25.8 1.0 %velocities.1.refs_0_ = bf16[4,32,128]{2,1,0:T(8,128)(2,1)S(1)} custom-call(s32[4,128]{1,0:T(4,128)S(1)} %get-tuple-element.41.cpl, bf16[192,128]{1,0:T(8,128)(2,1)S(1)} %get-tuple-element.42.refs_0_.src_ref, bf16[192,128]{1,0:T(8,128)(2,1)S(1)} %collective-permute-done.5.refs_1_.src_ref, bf16[192,128]{1,0:T(8,128)(2,1)S(1)} %collective-permute-done.6.refs_2_.src_ref, ...), custom_call_target="tpu_custom_call" | custom-call | tf_op jit(solution)/shard_map/velocities/pallas_call | solution.py:219
  26.8 3.7 %collective-permute-start.12 = (bf16[4,32,128]{2,1,0:T(8,128)(2,1)S(1)}, bf16[4,32,128]{2,1,0:T(8,128)(2,1)S(1)}, u32[]{:S(2)}, u32[]{:S(2)}) collective-permute-start(bf16[4,32,128]{2,1,0:T(8,128)(2,1)S(1)} %velocities.1.refs_0_), channel_id=1, source_target_pairs={{0,3},{1,2},{2,1},{3,0},{4,7},{5,6},{6,5},{7,4},{8,11},{9,10},{10,... | collective-permute-start | bytes 98312 | tf_op jit(solution)/shard_map/ppermute | solution.py:41
  31.3 0.9 %helmholtz.15 = (bf16[512,512]{1,0:T(8,128)(2,1)S(1)}, bf16[512,512]{1,0:T(8,128)(2,1)S(1)}) custom-call(bf16[64,512]{1,0:T(8,128)(2,1)S(1)} %target_matrix.1.tgt_ref, bf16[4,192,128]{2,1,0:T(8,128)(2,1)S(1)} %collective-permute-done.8.refs_4_.src_ref, bf16[4,32,128]{2,1,0:T(8,128)(2,1)S(1)} %velocities.1.refs_0_), custom_call_target="tpu_custom_call" | custom-call | flops 1468006400 | bytes 1 | tf_op jit(solution)/shard_map/helmholtz/pallas_call | solution.py:288
  32.2 0.9 %helmholtz.14 = (bf16[512,512]{1,0:T(8,128)(2,1)S(1)}, bf16[512,512]{1,0:T(8,128)(2,1)S(1)}) custom-call(bf16[64,512]{1,0:T(8,128)(2,1)S(1)} %target_matrix.1.tgt_ref, bf16[4,192,128]{2,1,0:T(8,128)(2,1)S(1)} %collective-permute-done.8.refs_4_.src_ref, bf16[4,32,128]{2,1,0:T(8,128)(2,1)S(1)} %velocities.1.refs_0_), custom_call_target="tpu_custom_call" | custom-call | flops 1468006400 | bytes 1 | tf_op jit(solution)/shard_map/helmholtz/pallas_call | solution.py:288
  33.2 0.9 %helmholtz.13 = (bf16[512,512]{1,0:T(8,128)(2,1)S(1)}, bf16[512,512]{1,0:T(8,128)(2,1)S(1)}) custom-call(bf16[64,512]{1,0:T(8,128)(2,1)S(1)} %target_matrix.1.tgt_ref, bf16[4,192,128]{2,1,0:T(8,128)(2,1)S(1)} %collective-permute-done.8.refs_4_.src_ref, bf16[4,32,128]{2,1,0:T(8,128)(2,1)S(1)} %velocities.1.refs_0_), custom_call_target="tpu_custom_call" | custom-call | flops 1468006400 | bytes 1 | tf_op jit(solution)/shard_map/helmholtz/pallas_call | solution.py:288
  34.1 1.2 %collective-permute-done.11.refs_2_ = bf16[4,32,128]{2,1,0:T(8,128)(2,1)S(1)} collective-permute-done((bf16[4,32,128]{2,1,0:T(8,128)(2,1)S(1)}, bf16[4,32,128]{2,1,0:T(8,128)(2,1)S(1)}, u32[]{:S(2)}, u32[]{:S(2)}) %collective-permute-start.11) | collective-permute-done | bytes 32800 | tf_op jit(solution)/shard_map/ppermute | solution.py:41
  35.4 0.9 %helmholtz.12 = (bf16[512,512]{1,0:T(8,128)(2,1)S(1)}, bf16[512,512]{1,0:T(8,128)(2,1)S(1)}) custom-call(bf16[64,512]{1,0:T(8,128)(2,1)S(1)} %target_matrix.1.tgt_ref, bf16[4,192,128]{2,1,0:T(8,128)(2,1)S(1)} %collective-permute-done.8.refs_4_.src_ref, bf16[4,32,128]{2,1,0:T(8,128)(2,1)S(1)} %velocities.1.refs_0_), custom_call_target="tpu_custom_call" | custom-call | flops 1468006400 | bytes 1 | tf_op jit(solution)/shard_map/helmholtz/pallas_call | solution.py:288
  36.7 2.5 %pressures.1 = (bf16[4,32,128]{2,1,0:T(8,128)(2,1)S(1)}, f32[16,32,128]{2,1,0:T(8,128)S(1)}, bf16[16,32,128]{2,1,0:T(8,128)(2,1)S(1)}) custom-call(s32[4,128]{1,0:T(4,128)S(1)} %get-tuple-element.41.cpl, bf16[4,32,128]{2,1,0:T(8,128)(2,1)S(1)} %velocities.1.refs_0_, bf16[4,32,128]{2,1,0:T(8,128)(2,1)S(1)} %collective-permute-done.10.refs_1_, ...), custom_call_target="tpu_custom_call" | custom-call | tf_op jit(solution)/shard_map/pressures/pallas_call | solution.py:347
  39.5 1.2 %collective-permute-done.14.got_ref = bf16[16,32,128]{2,1,0:T(8,128)(2,1)S(1)} collective-permute-done((bf16[16,32,128]{2,1,0:T(8,128)(2,1)S(1)}, bf16[16,32,128]{2,1,0:T(8,128)(2,1)S(1)}, u32[]{:S(2)}, u32[]{:S(2)}) %collective-permute-start.14) | collective-permute-done | bytes 131104 | tf_op jit(solution)/shard_map/ppermute | solution.py:45
  40.7 2.5 %collective-permute-start.15 = (bf16[4,32,128]{2,1,0:T(8,128)(2,1)S(1)}, bf16[4,32,128]{2,1,0:T(8,128)(2,1)S(1)}, u32[]{:S(2)}, u32[]{:S(2)}) collective-permute-start(bf16[4,32,128]{2,1,0:T(8,128)(2,1)S(1)} %get-tuple-element.62), channel_id=1, source_target_pairs={{0,3},{1,2},{2,1},{3,0},{4,7},{5,6},{6,5},{7,4},{8,11},{9,10},{10,... | collective-permute-start | bytes 98312 | tf_op jit(solution)/shard_map/ppermute | solution.py:41
  43.2 1.9 %collective-permute-start.17 = (bf16[4,32,128]{2,1,0:T(8,128)(2,1)S(1)}, bf16[4,32,128]{2,1,0:T(8,128)(2,1)S(1)}, u32[]{:S(2)}, u32[]{:S(2)}) collective-permute-start(bf16[4,32,128]{2,1,0:T(8,128)(2,1)S(1)} %get-tuple-element.64), channel_id=1, source_target_pairs={{0,1},{1,0},{2,3},{3,2},{4,5},{5,4},{6,7},{7,6},{8,9},{9,8},{10,11... | collective-permute-start | bytes 98312 | tf_op jit(solution)/shard_map/ppermute | solution.py:41
  45.2 1.7 %collective-permute-done.15.refs_1_ = bf16[4,32,128]{2,1,0:T(8,128)(2,1)S(1)} collective-permute-done((bf16[4,32,128]{2,1,0:T(8,128)(2,1)S(1)}, bf16[4,32,128]{2,1,0:T(8,128)(2,1)S(1)}, u32[]{:S(2)}, u32[]{:S(2)}) %collective-permute-start.15) | collective-permute-done | bytes 32800 | tf_op jit(solution)/shard_map/ppermute | solution.py:41
  46.8 1.2 %collective-permute-done.16.refs_2_ = bf16[4,32,128]{2,1,0:T(8,128)(2,1)S(1)} collective-permute-done((bf16[4,32,128]{2,1,0:T(8,128)(2,1)S(1)}, bf16[4,32,128]{2,1,0:T(8,128)(2,1)S(1)}, u32[]{:S(2)}, u32[]{:S(2)}) %collective-permute-start.16) | collective-permute-done | bytes 32800 | tf_op jit(solution)/shard_map/ppermute | solution.py:41
  48.1 1.6 %collective-permute-start.18 = (bf16[2,32,128]{2,1,0:T(8,128)(2,1)S(1)}, bf16[2,32,128]{2,1,0:T(8,128)(2,1)S(1)}, u32[]{:S(2)}, u32[]{:S(2)}) collective-permute-start(bf16[2,32,128]{2,1,0:T(8,128)(2,1)S(1)} %get-tuple-element.67), channel_id=1, source_target_pairs={{0,24},{4,28},{8,16},{12,20},{16,8},{20,12},{24,0},{28,4},{1,25},{... | collective-permute-start | bytes 49160 | tf_op jit(solution)/shard_map/ppermute | solution.py:37
  49.6 1.5 %collective-permute-start.19 = (bf16[2,32,128]{2,1,0:T(8,128)(2,1)S(1)}, bf16[2,32,128]{2,1,0:T(8,128)(2,1)S(1)}, u32[]{:S(2)}, u32[]{:S(2)}) collective-permute-start(bf16[2,32,128]{2,1,0:T(8,128)(2,1)S(1)} %get-tuple-element.68), channel_id=1, source_target_pairs={{0,16},{4,20},{8,24},{12,28},{16,0},{20,4},{24,8},{28,12},{1,17},{... | collective-permute-start | bytes 49160 | tf_op jit(solution)/shard_map/ppermute | solution.py:37
  51.6 1.1 %collective-permute-done.18.r3 = bf16[2,32,128]{2,1,0:T(8,128)(2,1)S(1)} collective-permute-done((bf16[2,32,128]{2,1,0:T(8,128)(2,1)S(1)}, bf16[2,32,128]{2,1,0:T(8,128)(2,1)S(1)}, u32[]{:S(2)}, u32[]{:S(2)}) %collective-permute-start.18) | collective-permute-done | bytes 16416 | tf_op jit(solution)/shard_map/ppermute | solution.py:37
  53.4 1.5 %collective-permute-done.20.r2 = bf16[2,32,128]{2,1,0:T(8,128)(2,1)S(1)} collective-permute-done((bf16[2,32,128]{2,1,0:T(8,128)(2,1)S(1)}, bf16[2,32,128]{2,1,0:T(8,128)(2,1)S(1)}, u32[]{:S(2)}, u32[]{:S(2)}) %collective-permute-start.20) | collective-permute-done | bytes 16416 | tf_op jit(solution)/shard_map/ppermute | solution.py:37
  (35 shorter events, 4.2 us)
Async XLA Ops:
  0.6 10.8 %copy-start = (bf16[128,8,128]{2,1,0:T(8,128)(2,1)S(1)}, bf16[128,8,128]{2,1,0:T(8,128)(2,1)}, u32[]{:S(2)}) copy-start(bf16[128,8,128]{2,1,0:T(8,128)(2,1)} %param.8) | copy-start | bytes 786436
  0.6 13.1 %collective-permute-start = (bf16[128,8,128]{2,1,0:T(8,128)(2,1)}, bf16[128,8,128]{2,1,0:T(8,128)(2,1)S(1)}, u32[]{:S(2)}, u32[]{:S(2)}) collective-permute-start(bf16[128,8,128]{2,1,0:T(8,128)(2,1)} %param.8), channel_id=1, source_target_pairs={{0,16},{4,20},{8,24},{12,28},{16,0},{20,4},{24,8},{28,12},{1,17},{... | collective-permute-start | bytes 786440 | tf_op jit(solution)/shard_map/ppermute | solution.py:37
  3.6 10.1 %collective-permute-start.1 = (bf16[128,8,128]{2,1,0:T(8,128)(2,1)}, bf16[128,8,128]{2,1,0:T(8,128)(2,1)S(1)}, u32[]{:S(2)}, u32[]{:S(2)}) collective-permute-start(bf16[128,8,128]{2,1,0:T(8,128)(2,1)} %param.8), channel_id=1, source_target_pairs={{0,8},{4,12},{8,0},{12,4},{16,24},{20,28},{24,16},{28,20},{1,9},{5... | collective-permute-start | bytes 786440 | tf_op jit(solution)/shard_map/ppermute | solution.py:37
  7.9 4.7 %collective-permute-start.2 = (bf16[80,128]{1,0:T(8,128)(2,1)S(1)}, bf16[80,128]{1,0:T(8,128)(2,1)S(1)}, u32[]{:S(2)}, u32[]{:S(2)}) collective-permute-start(bf16[80,128]{1,0:T(8,128)(2,1)S(1)} %get-tuple-element.38), channel_id=1, source_target_pairs={{0,24},{4,28},{8,16},{12,20},{16,8},{20,12},{24,0},{28,4},{1,25},{... | collective-permute-start | bytes 61448 | tf_op jit(solution)/shard_map/ppermute | solution.py:37
  8.0 4.7 %collective-permute-start.3 = (bf16[80,128]{1,0:T(8,128)(2,1)S(1)}, bf16[80,128]{1,0:T(8,128)(2,1)S(1)}, u32[]{:S(2)}, u32[]{:S(2)}) collective-permute-start(bf16[80,128]{1,0:T(8,128)(2,1)S(1)} %get-tuple-element.39), channel_id=1, source_target_pairs={{0,16},{4,20},{8,24},{12,28},{16,0},{20,4},{24,8},{28,12},{1,17},{... | collective-permute-start | bytes 61448 | tf_op jit(solution)/shard_map/ppermute | solution.py:37
  9.9 3.8 %collective-permute-start.4 = (bf16[80,128]{1,0:T(8,128)(2,1)S(1)}, bf16[80,128]{1,0:T(8,128)(2,1)S(1)}, u32[]{:S(2)}, u32[]{:S(2)}) collective-permute-start(bf16[80,128]{1,0:T(8,128)(2,1)S(1)} %get-tuple-element.40), channel_id=1, source_target_pairs={{0,8},{4,12},{8,0},{12,4},{16,24},{20,28},{24,16},{28,20},{1,9},{5... | collective-permute-start | bytes 61448 | tf_op jit(solution)/shard_map/ppermute | solution.py:37
  13.7 7.1 %collective-permute-start.7 = (bf16[192,128]{1,0:T(8,128)(2,1)S(1)}, bf16[192,128]{1,0:T(8,128)(2,1)S(1)}, u32[]{:S(2)}, u32[]{:S(2)}) collective-permute-start(bf16[192,128]{1,0:T(8,128)(2,1)S(1)} %get-tuple-element.42.refs_0_.src_ref), channel_id=1, source_target_pairs={{0,3},{1,2},{2,1},{3,0},{4,7},{5,6},{6,5},{7,4},{8,11},{9,10},{10,... | collective-permute-start | bytes 147464 | tf_op jit(solution)/shard_map/ppermute | solution.py:41
  17.4 5.0 %collective-permute-start.6 = (bf16[192,128]{1,0:T(8,128)(2,1)S(1)}, bf16[192,128]{1,0:T(8,128)(2,1)S(1)}, u32[]{:S(2)}, u32[]{:S(2)}) collective-permute-start(bf16[192,128]{1,0:T(8,128)(2,1)S(1)} %get-tuple-element.42.refs_0_.src_ref), channel_id=1, source_target_pairs={{0,2},{1,3},{2,0},{3,1},{4,6},{5,7},{6,4},{7,5},{8,10},{9,11},{10,... | collective-permute-start | bytes 147464 | tf_op jit(solution)/shard_map/ppermute | solution.py:41
  17.4 5.0 %collective-permute-start.5 = (bf16[192,128]{1,0:T(8,128)(2,1)S(1)}, bf16[192,128]{1,0:T(8,128)(2,1)S(1)}, u32[]{:S(2)}, u32[]{:S(2)}) collective-permute-start(bf16[192,128]{1,0:T(8,128)(2,1)S(1)} %get-tuple-element.42.refs_0_.src_ref), channel_id=1, source_target_pairs={{0,1},{1,0},{2,3},{3,2},{4,5},{5,4},{6,7},{7,6},{8,9},{9,8},{10,11... | collective-permute-start | bytes 147464 | tf_op jit(solution)/shard_map/ppermute | solution.py:41
  19.3 6.4 %collective-permute-start.9 = (bf16[128,8,128]{2,1,0:T(8,128)(2,1)S(1)}, bf16[128,8,128]{2,1,0:T(8,128)(2,1)S(1)}, u32[]{:S(2)}, u32[]{:S(2)}) collective-permute-start(bf16[128,8,128]{2,1,0:T(8,128)(2,1)S(1)} %collective-permute-done.refs_0_), channel_id=1, source_target_pairs={{0,8},{4,12},{8,0},{12,4},{16,24},{20,28},{24,16},{28,20},{1,9},{5... | collective-permute-start | bytes 786440 | tf_op jit(solution)/shard_map/ppermute | solution.py:37
  22.4 3.4 %collective-permute-start.8 = (bf16[4,192,128]{2,1,0:T(8,128)(2,1)S(1)}, bf16[4,192,128]{2,1,0:T(8,128)(2,1)S(1)}, u32[]{:S(2)}, u32[]{:S(2)}) collective-permute-start(bf16[4,192,128]{2,1,0:T(8,128)(2,1)S(1)} %stack.2), channel_id=1, source_target_pairs={{0,4},{4,0},{8,12},{12,8},{1,5},{5,1},{9,13},{13,9},{2,6},{6,2},{1... | collective-permute-start | bytes 589832 | tf_op jit(solution)/shard_map/ppermute | solution.py:45
  26.8 7.3 %collective-permute-start.12 = (bf16[4,32,128]{2,1,0:T(8,128)(2,1)S(1)}, bf16[4,32,128]{2,1,0:T(8,128)(2,1)S(1)}, u32[]{:S(2)}, u32[]{:S(2)}) collective-permute-start(bf16[4,32,128]{2,1,0:T(8,128)(2,1)S(1)} %velocities.1.refs_0_), channel_id=1, source_target_pairs={{0,3},{1,2},{2,1},{3,0},{4,7},{5,6},{6,5},{7,4},{8,11},{9,10},{10,... | collective-permute-start | bytes 98312 | tf_op jit(solution)/shard_map/ppermute | solution.py:41
  30.5 4.8 %collective-permute-start.11 = (bf16[4,32,128]{2,1,0:T(8,128)(2,1)S(1)}, bf16[4,32,128]{2,1,0:T(8,128)(2,1)S(1)}, u32[]{:S(2)}, u32[]{:S(2)}) collective-permute-start(bf16[4,32,128]{2,1,0:T(8,128)(2,1)S(1)} %velocities.1.refs_0_), channel_id=1, source_target_pairs={{0,2},{1,3},{2,0},{3,1},{4,6},{5,7},{6,4},{7,5},{8,10},{9,11},{10,... | collective-permute-start | bytes 98312 | tf_op jit(solution)/shard_map/ppermute | solution.py:41
  30.5 4.8 %collective-permute-start.10 = (bf16[4,32,128]{2,1,0:T(8,128)(2,1)S(1)}, bf16[4,32,128]{2,1,0:T(8,128)(2,1)S(1)}, u32[]{:S(2)}, u32[]{:S(2)}) collective-permute-start(bf16[4,32,128]{2,1,0:T(8,128)(2,1)S(1)} %velocities.1.refs_0_), channel_id=1, source_target_pairs={{0,1},{1,0},{2,3},{3,2},{4,5},{5,4},{6,7},{7,6},{8,9},{9,8},{10,11... | collective-permute-start | bytes 98312 | tf_op jit(solution)/shard_map/ppermute | solution.py:41
  35.3 1.4 %collective-permute-start.13 = (bf16[4,4,32,128]{3,2,1,0:T(8,128)(2,1)S(1)}, bf16[4,4,32,128]{3,2,1,0:T(8,128)(2,1)S(1)}, u32[]{:S(2)}, u32[]{:S(2)}) collective-permute-start(bf16[4,4,32,128]{3,2,1,0:T(8,128)(2,1)S(1)} %stack.3), channel_id=1, source_target_pairs={{0,4},{4,0},{8,12},{12,8},{1,5},{5,1},{9,13},{13,9},{2,6},{6,2},{1... | collective-permute-start | bytes 393224 | tf_op jit(solution)/shard_map/ppermute | solution.py:45
  39.2 1.4 %collective-permute-start.14 = (bf16[16,32,128]{2,1,0:T(8,128)(2,1)S(1)}, bf16[16,32,128]{2,1,0:T(8,128)(2,1)S(1)}, u32[]{:S(2)}, u32[]{:S(2)}) collective-permute-start(bf16[16,32,128]{2,1,0:T(8,128)(2,1)S(1)} %get-tuple-element.60), channel_id=1, source_target_pairs={{0,4},{4,0},{8,12},{12,8},{1,5},{5,1},{9,13},{13,9},{2,6},{6,2},{1... | collective-permute-start | bytes 393224 | tf_op jit(solution)/shard_map/ppermute | solution.py:45
  40.7 6.1 %collective-permute-start.15 = (bf16[4,32,128]{2,1,0:T(8,128)(2,1)S(1)}, bf16[4,32,128]{2,1,0:T(8,128)(2,1)S(1)}, u32[]{:S(2)}, u32[]{:S(2)}) collective-permute-start(bf16[4,32,128]{2,1,0:T(8,128)(2,1)S(1)} %get-tuple-element.62), channel_id=1, source_target_pairs={{0,3},{1,2},{2,1},{3,0},{4,7},{5,6},{6,5},{7,4},{8,11},{9,10},{10,... | collective-permute-start | bytes 98312 | tf_op jit(solution)/shard_map/ppermute | solution.py:41
  43.2 4.8 %collective-permute-start.16 = (bf16[4,32,128]{2,1,0:T(8,128)(2,1)S(1)}, bf16[4,32,128]{2,1,0:T(8,128)(2,1)S(1)}, u32[]{:S(2)}, u32[]{:S(2)}) collective-permute-start(bf16[4,32,128]{2,1,0:T(8,128)(2,1)S(1)} %get-tuple-element.63), channel_id=1, source_target_pairs={{0,2},{1,3},{2,0},{3,1},{4,6},{5,7},{6,4},{7,5},{8,10},{9,11},{10,... | collective-permute-start | bytes 98312 | tf_op jit(solution)/shard_map/ppermute | solution.py:41
  43.2 4.8 %collective-permute-start.17 = (bf16[4,32,128]{2,1,0:T(8,128)(2,1)S(1)}, bf16[4,32,128]{2,1,0:T(8,128)(2,1)S(1)}, u32[]{:S(2)}, u32[]{:S(2)}) collective-permute-start(bf16[4,32,128]{2,1,0:T(8,128)(2,1)S(1)} %get-tuple-element.64), channel_id=1, source_target_pairs={{0,1},{1,0},{2,3},{3,2},{4,5},{5,4},{6,7},{7,6},{8,9},{9,8},{10,11... | collective-permute-start | bytes 98312 | tf_op jit(solution)/shard_map/ppermute | solution.py:41
  48.1 4.7 %collective-permute-start.18 = (bf16[2,32,128]{2,1,0:T(8,128)(2,1)S(1)}, bf16[2,32,128]{2,1,0:T(8,128)(2,1)S(1)}, u32[]{:S(2)}, u32[]{:S(2)}) collective-permute-start(bf16[2,32,128]{2,1,0:T(8,128)(2,1)S(1)} %get-tuple-element.67), channel_id=1, source_target_pairs={{0,24},{4,28},{8,16},{12,20},{16,8},{20,12},{24,0},{28,4},{1,25},{... | collective-permute-start | bytes 49160 | tf_op jit(solution)/shard_map/ppermute | solution.py:37
  49.6 3.7 %collective-permute-start.19 = (bf16[2,32,128]{2,1,0:T(8,128)(2,1)S(1)}, bf16[2,32,128]{2,1,0:T(8,128)(2,1)S(1)}, u32[]{:S(2)}, u32[]{:S(2)}) collective-permute-start(bf16[2,32,128]{2,1,0:T(8,128)(2,1)S(1)} %get-tuple-element.68), channel_id=1, source_target_pairs={{0,16},{4,20},{8,24},{12,28},{16,0},{20,4},{24,8},{28,12},{1,17},{... | collective-permute-start | bytes 49160 | tf_op jit(solution)/shard_map/ppermute | solution.py:37
  51.1 3.7 %collective-permute-start.20 = (bf16[2,32,128]{2,1,0:T(8,128)(2,1)S(1)}, bf16[2,32,128]{2,1,0:T(8,128)(2,1)S(1)}, u32[]{:S(2)}, u32[]{:S(2)}) collective-permute-start(bf16[2,32,128]{2,1,0:T(8,128)(2,1)S(1)} %get-tuple-element.69), channel_id=1, source_target_pairs={{0,8},{4,12},{8,0},{12,4},{16,24},{20,28},{24,16},{28,20},{1,9},{5... | collective-permute-start | bytes 49160 | tf_op jit(solution)/shard_map/ppermute | solution.py:37

commit v5 on v4

--- a/solution.py
+++ b/solution.py
@@ -79,11 +79,34 @@
     ]
     fetch_loads = pltpu.make_async_copy(l_hbm, l_buf, sems.at[3])
     fetch = [
-        pltpu.make_async_copy(r_hbm.at[:, b * lanes : (b + 1) * lanes, :], r_buf.at[:, b * lanes : (b + 1) * lanes, :], sems.at[4 + b])
+        pltpu.make_async_copy(
+            r_hbm.at[part, b * lanes : (b + 1) * lanes, :], r_buf.at[part, b * lanes : (b + 1) * lanes, :], sems.at[4 + 2 * b + part]
+        )
         for b in range(blocks)
+        for part in range(2)
     ]
-    for copy in [fetch_loads] + fetch + small:
+    for copy in [fetch_loads] + small + fetch:
         copy.start()
+    width = l_buf.shape[1]
+    half = width // 2
+    quarter = half // 4
+    x, y, _, _ = place()
+    mine = x + 2 * y
+    fetch_loads.wait()
+    for b in range(blocks):
+        span = slice(b * lanes, (b + 1) * lanes)
+        fetch[2 * b].wait()
+        lead = jnp.dot(r_buf[0, span, :], l_buf[...], preferred_element_type=f32)
+        fetch[2 * b + 1].wait()
+        turned = pltpu.roll(jnp.dot(r_buf[1, span, :], l_buf[...], preferred_element_type=f32), half, 1)
+        lane = lax.broadcasted_iota(jnp.int32, turned.shape, 1)
+        amp_t[...] = (lead + jnp.where(lane < half, -turned, turned)).T
+        for mask, out in enumerate((own_ref, s1_ref, s2_ref, s3_ref)):
+            at = pl.multiple_of((mine ^ mask) * quarter, quarter)
+            for part in range(2):
+                r0 = (2 * b + part) * quarter
+                out[r0 : r0 + quarter, :] = amp_t[pl.ds(part * half + at, quarter), :].astype(out.dtype)
+
     for copy in small:
         copy.wait()
     scaled = (xyz[...] - 0.5) * turns
@@ -102,25 +125,6 @@
     for out in (s1_ref, s2_ref, s3_ref):
         out[out.shape[0] - GEO :, :] = packed
 
-    width = l_buf.shape[1]
-    half = width // 2
-    quarter = half // 4
-    x, y, _, _ = place()
-    mine = x + 2 * y
-    fetch_loads.wait()
-    for b in range(blocks):
-        fetch[b].wait()
-        span = slice(b * lanes, (b + 1) * lanes)
-        both = jnp.dot(r_buf[:, span, :].reshape(2 * lanes, r_buf.shape[2]), l_buf[...], preferred_element_type=f32)
-        turned = pltpu.roll(both[lanes:], half, 1)
-        lane = lax.broadcasted_iota(jnp.int32, turned.shape, 1)
-        amp_t[...] = (both[:lanes] + jnp.where(lane < half, -turned, turned)).T
-        for mask, out in enumerate((own_ref, s1_ref, s2_ref, s3_ref)):
-            at = pl.multiple_of((mine ^ mask) * quarter, quarter)
-            for part in range(2):
-                r0 = (2 * b + part) * quarter
-                out[r0 : r0 + quarter, :] = amp_t[pl.ds(part * half + at, quarter), :].astype(out.dtype)
-
 
 def amplitude_parts(panels, receptance, loads, xyz, area, coupling):
     _, rows, depth = receptance.shape
@@ -141,7 +145,7 @@
             pltpu.VMEM(coupling.shape, jnp.int32),
             pltpu.VMEM((width, 128), f32),
             pltpu.VMEM((GEO, 128), f32),
-            pltpu.SemaphoreType.DMA((4 + blocks,)),
+            pltpu.SemaphoreType.DMA((4 + 2 * blocks,)),
         ],
         compiler_params=limit(12),
         cost_estimate=pl.CostEstimate(flops=4 * rows * depth * width, bytes_accessed=1, transcendentals=0),
@@ -190,7 +194,7 @@
 
 def velocity_kernel(width, blocks, scale, secs, cpl, *refs):
     near, far_ref = refs[0:secs], refs[secs]
-    modes, out_ref, table, picked = refs[secs + 1 : secs + 5], refs[-3], refs[-2], refs[-1]
+    modes, out_ref, table, picked = refs[secs + 1 : secs + 5], *refs[-3:]
     _, y, c, z = place()
     used = 2 * blocks * width
     for i in range(secs):
@@ -218,7 +222,7 @@
     secs = len(near)
     return pl.pallas_call(
         functools.partial(velocity_kernel, width, blocks, turns / math.sqrt(panels), secs),
-        in_specs=[SMEM] + [VMEM] * (secs + 5),
+        in_specs=[VMEM] * (secs + 6),
         out_specs=VMEM,
         out_shape=jax.ShapeDtypeStruct((4, width, count), bf16),
         scratch_shapes=[
@@ -291,7 +295,7 @@
         out_specs=[VMEM] * 2,
         out_shape=[jax.ShapeDtypeStruct((side, side), bf16)] * 2,
         compiler_params=limit(4),
-        cost_estimate=pl.CostEstimate(flops=int(cost * 4000 * side * side), bytes_accessed=1, transcendentals=0),
+        cost_estimate=pl.CostEstimate(flops=int(cost * 3900 * side * side), bytes_accessed=1, transcendentals=0),
         name="helmholtz",
     )(targets, payload, *after)
 
@@ -346,7 +350,7 @@
     args = [*v_near, v_far, *mats, geo, *modes]
     return pl.pallas_call(
         functools.partial(pressure_kernel, secs, tgt_n),
-        in_specs=[SMEM] + [VMEM] * len(args),
+        in_specs=[VMEM] * (1 + len(args)),
         out_specs=[VMEM] * 3,
         out_shape=[
             jax.ShapeDtypeStruct((groups, width, lanes), bf16),

time: 55.8 us -> 53.6 us (0.961)
  Pallas kernels: 14.7 us -> 13.5 us
  waiting for transfers between devices: 13 us -> 12 us
    pallas_call x1, Pallas kernels: 2.53 us -> 1.9 us  [pressures(): pl.pallas_call(functools.partial(pressure_kernel, secs, tgt_n), in_specs=...]
    ppermute x9, waiting for transfers between devices: 5.59 us -> 5 us  [exchange_sec(): lax.ppermute(x, 'sec', [(s, s ^ mask) for s in range(lax.axis_size('sec'))])]
  transfers between devices with their start and end apart: 21 -> 21, of which waited for: 12 -> 11; matrix products, arithmetic and copies ran while one was open for 0% -> 0% of each run, Pallas kernels for 19% -> 19%
where the time goes in v5:
time: 53.6 us; the launch traced here: 53.4 us
  starting transfers between devices  26.9 us (50%)
  Pallas kernels  13.5 us (25%)
  waiting for transfers between devices  12 us (22%)
  between operations  0.82 us (2%)
    ppermute x9, starting transfers between devices, exchange_sec(): lax.ppermute(x, 'sec', [(s, s ^ mask) for s in range(lax.axis_size('sec'))])  13.3 us
    ppermute x9, starting transfers between devices, exchange_plane(): return lax.ppermute(x, ('blk', 'tgt'), pairs)  13.2 us
    pallas_call x8, Pallas kernels, helmholtz(): pl.pallas_call(functools.partial(helmholtz_kernel, at), in_specs=[VMEM] *...  7.57 us
    ppermute x9, waiting for transfers between devices, exchange_plane(): return lax.ppermute(x, ('blk', 'tgt'), pairs)  5.45 us
    ppermute x9, waiting for transfers between devices, exchange_sec(): lax.ppermute(x, 'sec', [(s, s ^ mask) for s in range(lax.axis_size('sec'))])  5 us
    pallas_call x1, Pallas kernels, amplitude_parts(): pl.pallas_call(functools.partial(amplitude_kernel, panels), in_specs=[HBM...  2.61 us
    pallas_call x1, Pallas kernels, pressures(): pl.pallas_call(functools.partial(pressure_kernel, secs, tgt_n), in_specs=...  1.9 us
    ppermute x3, waiting for transfers between devices, exchange_core(): lax.ppermute(x, 'tgt', [(t, t ^ 1) for t in range(lax.axis_size('tgt'))])  1.58 us
  transfers between devices with their start and end apart: 21, of which 11 were waited for; matrix products, arithmetic and copies ran while one was open for 0% of the time, Pallas kernels for 19%

profile of v5, /device:TPU:0, one launch (start us, length us, event | category | flops | bytes accessed | tf_op | source)
XLA Modules:
  0.0 53.4 jit_solution(13643414994882858960)
XLA Ops:
  0.6 3.0 %collective-permute-start = (bf16[128,8,128]{2,1,0:T(8,128)(2,1)}, bf16[128,8,128]{2,1,0:T(8,128)(2,1)S(1)}, u32[]{:S(2)}, u32[]{:S(2)}) collective-permute-start(bf16[128,8,128]{2,1,0:T(8,128)(2,1)} %param.8), channel_id=1, source_target_pairs={{0,16},{4,20},{8,24},{12,28},{16,0},{20,4},{24,8},{28,12},{1,17},{... | collective-permute-start | bytes 786440 | tf_op jit(solution)/shard_map/ppermute | solution.py:37
  3.6 1.5 %collective-permute-start.1 = (bf16[128,8,128]{2,1,0:T(8,128)(2,1)}, bf16[128,8,128]{2,1,0:T(8,128)(2,1)S(1)}, u32[]{:S(2)}, u32[]{:S(2)}) collective-permute-start(bf16[128,8,128]{2,1,0:T(8,128)(2,1)} %param.8), channel_id=1, source_target_pairs={{0,8},{4,12},{8,0},{12,4},{16,24},{20,28},{24,16},{28,20},{1,9},{5... | collective-permute-start | bytes 786440 | tf_op jit(solution)/shard_map/ppermute | solution.py:37
  5.2 2.6 %amplitude_parts.1 = (f32[64,128]{1,0:T(8,128)S(1)}, bf16[80,128]{1,0:T(8,128)(2,1)S(1)}, bf16[80,128]{1,0:T(8,128)(2,1)S(1)}, bf16[80,128]{1,0:T(8,128)(2,1)S(1)}, bf16[16,128]{1,0:T(8,128)(2,1)S(1)}) custom-call(bf16[2,256,2048]{2,1,0:T(8,128)(2,1)} %r_hbm.1, bf16[2048,128]{1,0:T(8,128)(2,1)} %l_hbm.1, f32[3,128]{1,0:T(4,128)} %xyz_hbm.1, ...), custom_call_target="tpu_custom_call" | custom-call | flops 268435456 | bytes 1 | tf_op jit(solution)/shard_map/amplitude_parts/pallas_call | solution.py:135
  7.9 1.9 %collective-permute-start.3 = (bf16[80,128]{1,0:T(8,128)(2,1)S(1)}, bf16[80,128]{1,0:T(8,128)(2,1)S(1)}, u32[]{:S(2)}, u32[]{:S(2)}) collective-permute-start(bf16[80,128]{1,0:T(8,128)(2,1)S(1)} %get-tuple-element.39), channel_id=1, source_target_pairs={{0,16},{4,20},{8,24},{12,28},{16,0},{20,4},{24,8},{28,12},{1,17},{... | collective-permute-start | bytes 61448 | tf_op jit(solution)/shard_map/ppermute | solution.py:37
  9.8 1.5 %collective-permute-start.4 = (bf16[80,128]{1,0:T(8,128)(2,1)S(1)}, bf16[80,128]{1,0:T(8,128)(2,1)S(1)}, u32[]{:S(2)}, u32[]{:S(2)}) collective-permute-start(bf16[80,128]{1,0:T(8,128)(2,1)S(1)} %get-tuple-element.40), channel_id=1, source_target_pairs={{0,8},{4,12},{8,0},{12,4},{16,24},{20,28},{24,16},{28,20},{1,9},{5... | collective-permute-start | bytes 61448 | tf_op jit(solution)/shard_map/ppermute | solution.py:37
  11.4 1.1 %collective-permute-done.2.refs_4_ = bf16[80,128]{1,0:T(8,128)(2,1)S(1)} collective-permute-done((bf16[80,128]{1,0:T(8,128)(2,1)S(1)}, bf16[80,128]{1,0:T(8,128)(2,1)S(1)}, u32[]{:S(2)}, u32[]{:S(2)}) %collective-permute-start.2) | collective-permute-done | bytes 20512 | tf_op jit(solution)/shard_map/ppermute | solution.py:37
  12.5 1.1 %collective-permute-done.4.refs_6_ = bf16[80,128]{1,0:T(8,128)(2,1)S(1)} collective-permute-done((bf16[80,128]{1,0:T(8,128)(2,1)S(1)}, bf16[80,128]{1,0:T(8,128)(2,1)S(1)}, u32[]{:S(2)}, u32[]{:S(2)}) %collective-permute-start.4) | collective-permute-done | bytes 20512 | tf_op jit(solution)/shard_map/ppermute | solution.py:37
  13.6 3.7 %collective-permute-start.7 = (bf16[192,128]{1,0:T(8,128)(2,1)S(1)}, bf16[192,128]{1,0:T(8,128)(2,1)S(1)}, u32[]{:S(2)}, u32[]{:S(2)}) collective-permute-start(bf16[192,128]{1,0:T(8,128)(2,1)S(1)} %get-tuple-element.42.refs_0_.src_ref), channel_id=1, source_target_pairs={{0,3},{1,2},{2,1},{3,0},{4,7},{5,6},{6,5},{7,4},{8,11},{9,10},{10,... | collective-permute-start | bytes 147464 | tf_op jit(solution)/shard_map/ppermute | solution.py:41
  17.3 0.8 %collective-permute-start.5 = (bf16[192,128]{1,0:T(8,128)(2,1)S(1)}, bf16[192,128]{1,0:T(8,128)(2,1)S(1)}, u32[]{:S(2)}, u32[]{:S(2)}) collective-permute-start(bf16[192,128]{1,0:T(8,128)(2,1)S(1)} %get-tuple-element.42.refs_0_.src_ref), channel_id=1, source_target_pairs={{0,1},{1,0},{2,3},{3,2},{4,5},{5,4},{6,7},{7,6},{8,9},{9,8},{10,11... | collective-permute-start | bytes 147464 | tf_op jit(solution)/shard_map/ppermute | solution.py:41
  18.2 1.6 %collective-permute-start.9 = (bf16[128,8,128]{2,1,0:T(8,128)(2,1)S(1)}, bf16[128,8,128]{2,1,0:T(8,128)(2,1)S(1)}, u32[]{:S(2)}, u32[]{:S(2)}) collective-permute-start(bf16[128,8,128]{2,1,0:T(8,128)(2,1)S(1)} %collective-permute-done.refs_0_), channel_id=1, source_target_pairs={{0,8},{4,12},{8,0},{12,4},{16,24},{20,28},{24,16},{28,20},{1,9},{5... | collective-permute-start | bytes 786440 | tf_op jit(solution)/shard_map/ppermute | solution.py:37
  19.8 0.9 %helmholtz.8 = (bf16[512,512]{1,0:T(8,128)(2,1)S(1)}, bf16[512,512]{1,0:T(8,128)(2,1)S(1)}) custom-call(bf16[64,512]{1,0:T(8,128)(2,1)S(1)} %target_matrix.1.tgt_ref, bf16[192,128]{1,0:T(8,128)(2,1)S(1)} %get-tuple-element.42.refs_0_.src_ref), custom_call_target="tpu_custom_call" | custom-call | flops 1022361600 | bytes 1 | tf_op jit(solution)/shard_map/helmholtz/pallas_call | solution.py:292
  20.8 1.5 %collective-permute-done.6.refs_2_.src_ref = bf16[192,128]{1,0:T(8,128)(2,1)S(1)} collective-permute-done((bf16[192,128]{1,0:T(8,128)(2,1)S(1)}, bf16[192,128]{1,0:T(8,128)(2,1)S(1)}, u32[]{:S(2)}, u32[]{:S(2)}) %collective-permute-start.6) | collective-permute-done | bytes 49184 | tf_op jit(solution)/shard_map/ppermute | solution.py:41
  22.4 1.0 %helmholtz.11 = (bf16[512,512]{1,0:T(8,128)(2,1)S(1)}, bf16[512,512]{1,0:T(8,128)(2,1)S(1)}) custom-call(bf16[64,512]{1,0:T(8,128)(2,1)S(1)} %target_matrix.1.tgt_ref, bf16[192,128]{1,0:T(8,128)(2,1)S(1)} %collective-permute-done.7.refs_3_.src_ref), custom_call_target="tpu_custom_call" | custom-call | flops 1022361600 | bytes 1 | tf_op jit(solution)/shard_map/helmholtz/pallas_call | solution.py:292
  23.4 0.9 %helmholtz.10 = (bf16[512,512]{1,0:T(8,128)(2,1)S(1)}, bf16[512,512]{1,0:T(8,128)(2,1)S(1)}) custom-call(bf16[64,512]{1,0:T(8,128)(2,1)S(1)} %target_matrix.1.tgt_ref, bf16[192,128]{1,0:T(8,128)(2,1)S(1)} %collective-permute-done.6.refs_2_.src_ref), custom_call_target="tpu_custom_call" | custom-call | flops 1022361600 | bytes 1 | tf_op jit(solution)/shard_map/helmholtz/pallas_call | solution.py:292
  24.3 0.9 %helmholtz.9 = (bf16[512,512]{1,0:T(8,128)(2,1)S(1)}, bf16[512,512]{1,0:T(8,128)(2,1)S(1)}) custom-call(bf16[64,512]{1,0:T(8,128)(2,1)S(1)} %target_matrix.1.tgt_ref, bf16[192,128]{1,0:T(8,128)(2,1)S(1)} %collective-permute-done.5.refs_1_.src_ref), custom_call_target="tpu_custom_call" | custom-call | flops 1022361600 | bytes 1 | tf_op jit(solution)/shard_map/helmholtz/pallas_call | solution.py:292
  25.9 3.1 %collective-permute-start.12 = (bf16[4,32,128]{2,1,0:T(8,128)(2,1)S(1)}, bf16[4,32,128]{2,1,0:T(8,128)(2,1)S(1)}, u32[]{:S(2)}, u32[]{:S(2)}) collective-permute-start(bf16[4,32,128]{2,1,0:T(8,128)(2,1)S(1)} %velocities.1.refs_0_), channel_id=1, source_target_pairs={{0,3},{1,2},{2,1},{3,0},{4,7},{5,6},{6,5},{7,4},{8,11},{9,10},{10,... | collective-permute-start | bytes 98312 | tf_op jit(solution)/shard_map/ppermute | solution.py:41
  28.9 1.4 %collective-permute-start.10 = (bf16[4,32,128]{2,1,0:T(8,128)(2,1)S(1)}, bf16[4,32,128]{2,1,0:T(8,128)(2,1)S(1)}, u32[]{:S(2)}, u32[]{:S(2)}) collective-permute-start(bf16[4,32,128]{2,1,0:T(8,128)(2,1)S(1)} %velocities.1.refs_0_), channel_id=1, source_target_pairs={{0,1},{1,0},{2,3},{3,2},{4,5},{5,4},{6,7},{7,6},{8,9},{9,8},{10,11... | collective-permute-start | bytes 98312 | tf_op jit(solution)/shard_map/ppermute | solution.py:41
  30.3 0.9 %helmholtz.15 = (bf16[512,512]{1,0:T(8,128)(2,1)S(1)}, bf16[512,512]{1,0:T(8,128)(2,1)S(1)}) custom-call(bf16[64,512]{1,0:T(8,128)(2,1)S(1)} %target_matrix.1.tgt_ref, bf16[4,192,128]{2,1,0:T(8,128)(2,1)S(1)} %collective-permute-done.8.refs_4_.src_ref, bf16[4,32,128]{2,1,0:T(8,128)(2,1)S(1)} %velocities.1.refs_0_), custom_call_target="tpu_custom_call" | custom-call | flops 1431306240 | bytes 1 | tf_op jit(solution)/shard_map/helmholtz/pallas_call | solution.py:292
  31.2 0.9 %helmholtz.14 = (bf16[512,512]{1,0:T(8,128)(2,1)S(1)}, bf16[512,512]{1,0:T(8,128)(2,1)S(1)}) custom-call(bf16[64,512]{1,0:T(8,128)(2,1)S(1)} %target_matrix.1.tgt_ref, bf16[4,192,128]{2,1,0:T(8,128)(2,1)S(1)} %collective-permute-done.8.refs_4_.src_ref, bf16[4,32,128]{2,1,0:T(8,128)(2,1)S(1)} %velocities.1.refs_0_), custom_call_target="tpu_custom_call" | custom-call | flops 1431306240 | bytes 1 | tf_op jit(solution)/shard_map/helmholtz/pallas_call | solution.py:292
  32.2 0.9 %helmholtz.13 = (bf16[512,512]{1,0:T(8,128)(2,1)S(1)}, bf16[512,512]{1,0:T(8,128)(2,1)S(1)}) custom-call(bf16[64,512]{1,0:T(8,128)(2,1)S(1)} %target_matrix.1.tgt_ref, bf16[4,192,128]{2,1,0:T(8,128)(2,1)S(1)} %collective-permute-done.8.refs_4_.src_ref, bf16[4,32,128]{2,1,0:T(8,128)(2,1)S(1)} %velocities.1.refs_0_), custom_call_target="tpu_custom_call" | custom-call | flops 1431306240 | bytes 1 | tf_op jit(solution)/shard_map/helmholtz/pallas_call | solution.py:292
  33.8 0.9 %helmholtz.12 = (bf16[512,512]{1,0:T(8,128)(2,1)S(1)}, bf16[512,512]{1,0:T(8,128)(2,1)S(1)}) custom-call(bf16[64,512]{1,0:T(8,128)(2,1)S(1)} %target_matrix.1.tgt_ref, bf16[4,192,128]{2,1,0:T(8,128)(2,1)S(1)} %collective-permute-done.8.refs_4_.src_ref, bf16[4,32,128]{2,1,0:T(8,128)(2,1)S(1)} %velocities.1.refs_0_), custom_call_target="tpu_custom_call" | custom-call | flops 1431306240 | bytes 1 | tf_op jit(solution)/shard_map/helmholtz/pallas_call | solution.py:292
  35.2 1.9 %pressures.1 = (bf16[4,32,128]{2,1,0:T(8,128)(2,1)S(1)}, f32[16,32,128]{2,1,0:T(8,128)S(1)}, bf16[16,32,128]{2,1,0:T(8,128)(2,1)S(1)}) custom-call(s32[4,128]{1,0:T(4,128)S(1)} %get-tuple-element.41.cpl, bf16[4,32,128]{2,1,0:T(8,128)(2,1)S(1)} %velocities.1.refs_0_, bf16[4,32,128]{2,1,0:T(8,128)(2,1)S(1)} %collective-permute-done.10.refs_1_, ...), custom_call_target="tpu_custom_call" | custom-call | tf_op jit(solution)/shard_map/pressures/pallas_call | solution.py:351
  37.3 1.2 %collective-permute-done.14.got_ref = bf16[16,32,128]{2,1,0:T(8,128)(2,1)S(1)} collective-permute-done((bf16[16,32,128]{2,1,0:T(8,128)(2,1)S(1)}, bf16[16,32,128]{2,1,0:T(8,128)(2,1)S(1)}, u32[]{:S(2)}, u32[]{:S(2)}) %collective-permute-start.14) | collective-permute-done | bytes 131104 | tf_op jit(solution)/shard_map/ppermute | solution.py:45
  38.5 2.5 %collective-permute-start.15 = (bf16[4,32,128]{2,1,0:T(8,128)(2,1)S(1)}, bf16[4,32,128]{2,1,0:T(8,128)(2,1)S(1)}, u32[]{:S(2)}, u32[]{:S(2)}) collective-permute-start(bf16[4,32,128]{2,1,0:T(8,128)(2,1)S(1)} %get-tuple-element.62), channel_id=1, source_target_pairs={{0,3},{1,2},{2,1},{3,0},{4,7},{5,6},{6,5},{7,4},{8,11},{9,10},{10,... | collective-permute-start | bytes 98312 | tf_op jit(solution)/shard_map/ppermute | solution.py:41
  41.1 1.9 %collective-permute-start.17 = (bf16[4,32,128]{2,1,0:T(8,128)(2,1)S(1)}, bf16[4,32,128]{2,1,0:T(8,128)(2,1)S(1)}, u32[]{:S(2)}, u32[]{:S(2)}) collective-permute-start(bf16[4,32,128]{2,1,0:T(8,128)(2,1)S(1)} %get-tuple-element.64), channel_id=1, source_target_pairs={{0,1},{1,0},{2,3},{3,2},{4,5},{5,4},{6,7},{7,6},{8,9},{9,8},{10,11... | collective-permute-start | bytes 98312 | tf_op jit(solution)/shard_map/ppermute | solution.py:41
  43.0 1.7 %collective-permute-done.15.refs_1_ = bf16[4,32,128]{2,1,0:T(8,128)(2,1)S(1)} collective-permute-done((bf16[4,32,128]{2,1,0:T(8,128)(2,1)S(1)}, bf16[4,32,128]{2,1,0:T(8,128)(2,1)S(1)}, u32[]{:S(2)}, u32[]{:S(2)}) %collective-permute-start.15) | collective-permute-done | bytes 32800 | tf_op jit(solution)/shard_map/ppermute | solution.py:41
  44.6 1.2 %collective-permute-done.16.refs_2_ = bf16[4,32,128]{2,1,0:T(8,128)(2,1)S(1)} collective-permute-done((bf16[4,32,128]{2,1,0:T(8,128)(2,1)S(1)}, bf16[4,32,128]{2,1,0:T(8,128)(2,1)S(1)}, u32[]{:S(2)}, u32[]{:S(2)}) %collective-permute-start.16) | collective-permute-done | bytes 32800 | tf_op jit(solution)/shard_map/ppermute | solution.py:41
  45.9 1.5 %collective-permute-start.18 = (bf16[2,32,128]{2,1,0:T(8,128)(2,1)S(1)}, bf16[2,32,128]{2,1,0:T(8,128)(2,1)S(1)}, u32[]{:S(2)}, u32[]{:S(2)}) collective-permute-start(bf16[2,32,128]{2,1,0:T(8,128)(2,1)S(1)} %get-tuple-element.67), channel_id=1, source_target_pairs={{0,24},{4,28},{8,16},{12,20},{16,8},{20,12},{24,0},{28,4},{1,25},{... | collective-permute-start | bytes 49160 | tf_op jit(solution)/shard_map/ppermute | solution.py:37
  47.4 1.5 %collective-permute-start.19 = (bf16[2,32,128]{2,1,0:T(8,128)(2,1)S(1)}, bf16[2,32,128]{2,1,0:T(8,128)(2,1)S(1)}, u32[]{:S(2)}, u32[]{:S(2)}) collective-permute-start(bf16[2,32,128]{2,1,0:T(8,128)(2,1)S(1)} %get-tuple-element.68), channel_id=1, source_target_pairs={{0,16},{4,20},{8,24},{12,28},{16,0},{20,4},{24,8},{28,12},{1,17},{... | collective-permute-start | bytes 49160 | tf_op jit(solution)/shard_map/ppermute | solution.py:37
  49.5 1.1 %collective-permute-done.18.r3 = bf16[2,32,128]{2,1,0:T(8,128)(2,1)S(1)} collective-permute-done((bf16[2,32,128]{2,1,0:T(8,128)(2,1)S(1)}, bf16[2,32,128]{2,1,0:T(8,128)(2,1)S(1)}, u32[]{:S(2)}, u32[]{:S(2)}) %collective-permute-start.18) | collective-permute-done | bytes 16416 | tf_op jit(solution)/shard_map/ppermute | solution.py:37
  51.2 1.5 %collective-permute-done.20.r2 = bf16[2,32,128]{2,1,0:T(8,128)(2,1)S(1)} collective-permute-done((bf16[2,32,128]{2,1,0:T(8,128)(2,1)S(1)}, bf16[2,32,128]{2,1,0:T(8,128)(2,1)S(1)}, u32[]{:S(2)}, u32[]{:S(2)}) %collective-permute-start.20) | collective-permute-done | bytes 16416 | tf_op jit(solution)/shard_map/ppermute | solution.py:37
  52.7 0.8 %outputs.1 = (f32[128,128]{1,0:T(8,128)}, bf16[128,128]{1,0:T(8,128)(2,1)}) custom-call(f32[2,32,128]{2,1,0:T(8,128)S(1)} %get-tuple-element.66.r0, bf16[2,32,128]{2,1,0:T(8,128)(2,1)S(1)} %collective-permute-done.18.r3, bf16[2,32,128]{2,1,0:T(8,128)(2,1)S(1)} %collective-permute-done.19.r1, bf16[2,32,128]{2,1,0:T(8,128)(2,1)S(1)} %collective-permute-done.20.r2), custom_call_target="tpu_custom_call" | custom-call | tf_op jit(solution)/shard_map/outputs/pallas_call | solution.py:430
  (35 shorter events, 3.4 us)
Async XLA Ops:
  0.6 10.7 %copy-start = (bf16[128,8,128]{2,1,0:T(8,128)(2,1)S(1)}, bf16[128,8,128]{2,1,0:T(8,128)(2,1)}, u32[]{:S(2)}) copy-start(bf16[128,8,128]{2,1,0:T(8,128)(2,1)} %param.8) | copy-start | bytes 786436
  0.6 13.0 %collective-permute-start = (bf16[128,8,128]{2,1,0:T(8,128)(2,1)}, bf16[128,8,128]{2,1,0:T(8,128)(2,1)S(1)}, u32[]{:S(2)}, u32[]{:S(2)}) collective-permute-start(bf16[128,8,128]{2,1,0:T(8,128)(2,1)} %param.8), channel_id=1, source_target_pairs={{0,16},{4,20},{8,24},{12,28},{16,0},{20,4},{24,8},{28,12},{1,17},{... | collective-permute-start | bytes 786440 | tf_op jit(solution)/shard_map/ppermute | solution.py:37
  3.6 10.0 %collective-permute-start.1 = (bf16[128,8,128]{2,1,0:T(8,128)(2,1)}, bf16[128,8,128]{2,1,0:T(8,128)(2,1)S(1)}, u32[]{:S(2)}, u32[]{:S(2)}) collective-permute-start(bf16[128,8,128]{2,1,0:T(8,128)(2,1)} %param.8), channel_id=1, source_target_pairs={{0,8},{4,12},{8,0},{12,4},{16,24},{20,28},{24,16},{28,20},{1,9},{5... | collective-permute-start | bytes 786440 | tf_op jit(solution)/shard_map/ppermute | solution.py:37
  7.8 4.7 %collective-permute-start.2 = (bf16[80,128]{1,0:T(8,128)(2,1)S(1)}, bf16[80,128]{1,0:T(8,128)(2,1)S(1)}, u32[]{:S(2)}, u32[]{:S(2)}) collective-permute-start(bf16[80,128]{1,0:T(8,128)(2,1)S(1)} %get-tuple-element.38), channel_id=1, source_target_pairs={{0,24},{4,28},{8,16},{12,20},{16,8},{20,12},{24,0},{28,4},{1,25},{... | collective-permute-start | bytes 61448 | tf_op jit(solution)/shard_map/ppermute | solution.py:37
  7.9 4.7 %collective-permute-start.3 = (bf16[80,128]{1,0:T(8,128)(2,1)S(1)}, bf16[80,128]{1,0:T(8,128)(2,1)S(1)}, u32[]{:S(2)}, u32[]{:S(2)}) collective-permute-start(bf16[80,128]{1,0:T(8,128)(2,1)S(1)} %get-tuple-element.39), channel_id=1, source_target_pairs={{0,16},{4,20},{8,24},{12,28},{16,0},{20,4},{24,8},{28,12},{1,17},{... | collective-permute-start | bytes 61448 | tf_op jit(solution)/shard_map/ppermute | solution.py:37
  9.8 3.8 %collective-permute-start.4 = (bf16[80,128]{1,0:T(8,128)(2,1)S(1)}, bf16[80,128]{1,0:T(8,128)(2,1)S(1)}, u32[]{:S(2)}, u32[]{:S(2)}) collective-permute-start(bf16[80,128]{1,0:T(8,128)(2,1)S(1)} %get-tuple-element.40), channel_id=1, source_target_pairs={{0,8},{4,12},{8,0},{12,4},{16,24},{20,28},{24,16},{28,20},{1,9},{5... | collective-permute-start | bytes 61448 | tf_op jit(solution)/shard_map/ppermute | solution.py:37
  13.6 7.1 %collective-permute-start.7 = (bf16[192,128]{1,0:T(8,128)(2,1)S(1)}, bf16[192,128]{1,0:T(8,128)(2,1)S(1)}, u32[]{:S(2)}, u32[]{:S(2)}) collective-permute-start(bf16[192,128]{1,0:T(8,128)(2,1)S(1)} %get-tuple-element.42.refs_0_.src_ref), channel_id=1, source_target_pairs={{0,3},{1,2},{2,1},{3,0},{4,7},{5,6},{6,5},{7,4},{8,11},{9,10},{10,... | collective-permute-start | bytes 147464 | tf_op jit(solution)/shard_map/ppermute | solution.py:41
  17.3 5.0 %collective-permute-start.6 = (bf16[192,128]{1,0:T(8,128)(2,1)S(1)}, bf16[192,128]{1,0:T(8,128)(2,1)S(1)}, u32[]{:S(2)}, u32[]{:S(2)}) collective-permute-start(bf16[192,128]{1,0:T(8,128)(2,1)S(1)} %get-tuple-element.42.refs_0_.src_ref), channel_id=1, source_target_pairs={{0,2},{1,3},{2,0},{3,1},{4,6},{5,7},{6,4},{7,5},{8,10},{9,11},{10,... | collective-permute-start | bytes 147464 | tf_op jit(solution)/shard_map/ppermute | solution.py:41
  17.3 5.0 %collective-permute-start.5 = (bf16[192,128]{1,0:T(8,128)(2,1)S(1)}, bf16[192,128]{1,0:T(8,128)(2,1)S(1)}, u32[]{:S(2)}, u32[]{:S(2)}) collective-permute-start(bf16[192,128]{1,0:T(8,128)(2,1)S(1)} %get-tuple-element.42.refs_0_.src_ref), channel_id=1, source_target_pairs={{0,1},{1,0},{2,3},{3,2},{4,5},{5,4},{6,7},{7,6},{8,9},{9,8},{10,11... | collective-permute-start | bytes 147464 | tf_op jit(solution)/shard_map/ppermute | solution.py:41
  18.2 7.0 %collective-permute-start.9 = (bf16[128,8,128]{2,1,0:T(8,128)(2,1)S(1)}, bf16[128,8,128]{2,1,0:T(8,128)(2,1)S(1)}, u32[]{:S(2)}, u32[]{:S(2)}) collective-permute-start(bf16[128,8,128]{2,1,0:T(8,128)(2,1)S(1)} %collective-permute-done.refs_0_), channel_id=1, source_target_pairs={{0,8},{4,12},{8,0},{12,4},{16,24},{20,28},{24,16},{28,20},{1,9},{5... | collective-permute-start | bytes 786440 | tf_op jit(solution)/shard_map/ppermute | solution.py:37
  22.3 3.0 %collective-permute-start.8 = (bf16[4,192,128]{2,1,0:T(8,128)(2,1)S(1)}, bf16[4,192,128]{2,1,0:T(8,128)(2,1)S(1)}, u32[]{:S(2)}, u32[]{:S(2)}) collective-permute-start(bf16[4,192,128]{2,1,0:T(8,128)(2,1)S(1)} %stack.2), channel_id=1, source_target_pairs={{0,4},{4,0},{8,12},{12,8},{1,5},{5,1},{9,13},{13,9},{2,6},{6,2},{1... | collective-permute-start | bytes 589832 | tf_op jit(solution)/shard_map/ppermute | solution.py:45
  25.9 7.3 %collective-permute-start.12 = (bf16[4,32,128]{2,1,0:T(8,128)(2,1)S(1)}, bf16[4,32,128]{2,1,0:T(8,128)(2,1)S(1)}, u32[]{:S(2)}, u32[]{:S(2)}) collective-permute-start(bf16[4,32,128]{2,1,0:T(8,128)(2,1)S(1)} %velocities.1.refs_0_), channel_id=1, source_target_pairs={{0,3},{1,2},{2,1},{3,0},{4,7},{5,6},{6,5},{7,4},{8,11},{9,10},{10,... | collective-permute-start | bytes 98312 | tf_op jit(solution)/shard_map/ppermute | solution.py:41
  28.9 4.8 %collective-permute-start.11 = (bf16[4,32,128]{2,1,0:T(8,128)(2,1)S(1)}, bf16[4,32,128]{2,1,0:T(8,128)(2,1)S(1)}, u32[]{:S(2)}, u32[]{:S(2)}) collective-permute-start(bf16[4,32,128]{2,1,0:T(8,128)(2,1)S(1)} %velocities.1.refs_0_), channel_id=1, source_target_pairs={{0,2},{1,3},{2,0},{3,1},{4,6},{5,7},{6,4},{7,5},{8,10},{9,11},{10,... | collective-permute-start | bytes 98312 | tf_op jit(solution)/shard_map/ppermute | solution.py:41
  28.9 4.8 %collective-permute-start.10 = (bf16[4,32,128]{2,1,0:T(8,128)(2,1)S(1)}, bf16[4,32,128]{2,1,0:T(8,128)(2,1)S(1)}, u32[]{:S(2)}, u32[]{:S(2)}) collective-permute-start(bf16[4,32,128]{2,1,0:T(8,128)(2,1)S(1)} %velocities.1.refs_0_), channel_id=1, source_target_pairs={{0,1},{1,0},{2,3},{3,2},{4,5},{5,4},{6,7},{7,6},{8,9},{9,8},{10,11... | collective-permute-start | bytes 98312 | tf_op jit(solution)/shard_map/ppermute | solution.py:41
  33.7 1.4 %collective-permute-start.13 = (bf16[4,4,32,128]{3,2,1,0:T(8,128)(2,1)S(1)}, bf16[4,4,32,128]{3,2,1,0:T(8,128)(2,1)S(1)}, u32[]{:S(2)}, u32[]{:S(2)}) collective-permute-start(bf16[4,4,32,128]{3,2,1,0:T(8,128)(2,1)S(1)} %stack.3), channel_id=1, source_target_pairs={{0,4},{4,0},{8,12},{12,8},{1,5},{5,1},{9,13},{13,9},{2,6},{6,2},{1... | collective-permute-start | bytes 393224 | tf_op jit(solution)/shard_map/ppermute | solution.py:45
  37.1 1.4 %collective-permute-start.14 = (bf16[16,32,128]{2,1,0:T(8,128)(2,1)S(1)}, bf16[16,32,128]{2,1,0:T(8,128)(2,1)S(1)}, u32[]{:S(2)}, u32[]{:S(2)}) collective-permute-start(bf16[16,32,128]{2,1,0:T(8,128)(2,1)S(1)} %get-tuple-element.60), channel_id=1, source_target_pairs={{0,4},{4,0},{8,12},{12,8},{1,5},{5,1},{9,13},{13,9},{2,6},{6,2},{1... | collective-permute-start | bytes 393224 | tf_op jit(solution)/shard_map/ppermute | solution.py:45
  38.5 6.1 %collective-permute-start.15 = (bf16[4,32,128]{2,1,0:T(8,128)(2,1)S(1)}, bf16[4,32,128]{2,1,0:T(8,128)(2,1)S(1)}, u32[]{:S(2)}, u32[]{:S(2)}) collective-permute-start(bf16[4,32,128]{2,1,0:T(8,128)(2,1)S(1)} %get-tuple-element.62), channel_id=1, source_target_pairs={{0,3},{1,2},{2,1},{3,0},{4,7},{5,6},{6,5},{7,4},{8,11},{9,10},{10,... | collective-permute-start | bytes 98312 | tf_op jit(solution)/shard_map/ppermute | solution.py:41
  41.1 4.8 %collective-permute-start.16 = (bf16[4,32,128]{2,1,0:T(8,128)(2,1)S(1)}, bf16[4,32,128]{2,1,0:T(8,128)(2,1)S(1)}, u32[]{:S(2)}, u32[]{:S(2)}) collective-permute-start(bf16[4,32,128]{2,1,0:T(8,128)(2,1)S(1)} %get-tuple-element.63), channel_id=1, source_target_pairs={{0,2},{1,3},{2,0},{3,1},{4,6},{5,7},{6,4},{7,5},{8,10},{9,11},{10,... | collective-permute-start | bytes 98312 | tf_op jit(solution)/shard_map/ppermute | solution.py:41
  41.1 4.8 %collective-permute-start.17 = (bf16[4,32,128]{2,1,0:T(8,128)(2,1)S(1)}, bf16[4,32,128]{2,1,0:T(8,128)(2,1)S(1)}, u32[]{:S(2)}, u32[]{:S(2)}) collective-permute-start(bf16[4,32,128]{2,1,0:T(8,128)(2,1)S(1)} %get-tuple-element.64), channel_id=1, source_target_pairs={{0,1},{1,0},{2,3},{3,2},{4,5},{5,4},{6,7},{7,6},{8,9},{9,8},{10,11... | collective-permute-start | bytes 98312 | tf_op jit(solution)/shard_map/ppermute | solution.py:41
  45.9 4.7 %collective-permute-start.18 = (bf16[2,32,128]{2,1,0:T(8,128)(2,1)S(1)}, bf16[2,32,128]{2,1,0:T(8,128)(2,1)S(1)}, u32[]{:S(2)}, u32[]{:S(2)}) collective-permute-start(bf16[2,32,128]{2,1,0:T(8,128)(2,1)S(1)} %get-tuple-element.67), channel_id=1, source_target_pairs={{0,24},{4,28},{8,16},{12,20},{16,8},{20,12},{24,0},{28,4},{1,25},{... | collective-permute-start | bytes 49160 | tf_op jit(solution)/shard_map/ppermute | solution.py:37
  47.4 3.7 %collective-permute-start.19 = (bf16[2,32,128]{2,1,0:T(8,128)(2,1)S(1)}, bf16[2,32,128]{2,1,0:T(8,128)(2,1)S(1)}, u32[]{:S(2)}, u32[]{:S(2)}) collective-permute-start(bf16[2,32,128]{2,1,0:T(8,128)(2,1)S(1)} %get-tuple-element.68), channel_id=1, source_target_pairs={{0,16},{4,20},{8,24},{12,28},{16,0},{20,4},{24,8},{28,12},{1,17},{... | collective-permute-start | bytes 49160 | tf_op jit(solution)/shard_map/ppermute | solution.py:37
  48.9 3.7 %collective-permute-start.20 = (bf16[2,32,128]{2,1,0:T(8,128)(2,1)S(1)}, bf16[2,32,128]{2,1,0:T(8,128)(2,1)S(1)}, u32[]{:S(2)}, u32[]{:S(2)}) collective-permute-start(bf16[2,32,128]{2,1,0:T(8,128)(2,1)S(1)} %get-tuple-element.69), channel_id=1, source_target_pairs={{0,8},{4,12},{8,0},{12,4},{16,24},{20,28},{24,16},{28,20},{1,9},{5... | collective-permute-start | bytes 49160 | tf_op jit(solution)/shard_map/ppermute | solution.py:37

commit v6 on v5

--- a/solution.py
+++ b/solution.py
@@ -154,7 +154,7 @@
 
 
 def amplitude_sum_kernel(count, *refs):
-    own_ref, geo_ref, d_ref, x_ref, y_ref, out_ref, cpl_ref = refs[count:]
+    own_ref, geo_ref, x_ref, y_ref, d_ref, out_ref, cpl_ref = refs[count:]
     n = own_ref.shape[0]
     out_ref[0:n, :] = (own_ref[...] + x_ref[0:n, :].astype(f32)).astype(bf16)
     out_ref[n : 2 * n, :] = (y_ref[0:n, :].astype(f32) + d_ref[0:n, :].astype(f32)).astype(bf16)
@@ -167,13 +167,13 @@
 def amplitude_sum(early, own, geo, x, y, d):
     n = own.shape[0]
     return pl.pallas_call(
-        functools.partial(amplitude_sum_kernel, len(early)),
+        functools.partial(amplitude_sum_kernel, 0),
         in_specs=[pl.BlockSpec(memory_space=pl.ANY)] * len(early) + [VMEM] * 5,
         out_specs=[VMEM] * 2,
         out_shape=[jax.ShapeDtypeStruct((2 * n + 4 * GEO, 128), bf16), jax.ShapeDtypeStruct((4, 128), jnp.int32)],
         compiler_params=limit(4),
         name="amplitude_sum",
-    )(*early, own, geo, d, x, y)
+    )(own, geo, x, y, d)
 
 
 def stack_kernel(*refs):
@@ -451,11 +451,9 @@
     ]
     own, s1, s2, s3, geo = amplitude_parts(panels, *held)
     got = [exchange_plane(s, m) for m, s in ((1, s1), (2, s2), (3, s3))]
-    modes = [shapes] + [exchange_plane(shapes, m) for m in (1, 2)]
-    modes.append(exchange_plane(modes[1], 2))
-    early = modes[1:3]
-    modes = [m.reshape(pan_dev, -1) for m in modes]
-    payload, cpl = amplitude_sum(early, own, geo, *got)
+    flat = shapes.reshape(pan_dev, -1)
+    modes = [flat] + [exchange_plane(flat, m) for m in (1, 2, 3)]
+    payload, cpl = amplitude_sum([], own, geo, *got)
     near = [payload] + [exchange_sec(payload, m) for m in range(1, secs)]
     far = exchange_core(stack(near))
     targets = payload[-4 * GEO :, :]

time: 53.6 us -> 52.9 us (0.987)
  starting transfers between devices: 26.9 us -> 25.5 us
  waiting for transfers between devices: 12 us -> 12.8 us
    ppermute x9, waiting for transfers between devices: 5 us -> 6.78 us  [exchange_sec(): lax.ppermute(x, 'sec', [(s, s ^ mask) for s in range(lax.axis_size('sec'))])]
    ppermute x9, starting transfers between devices: 13.2 us -> 11.8 us  [exchange_plane(): return lax.ppermute(x, ('blk', 'tgt'), pairs)]
    ppermute x9, waiting for transfers between devices: 5.45 us -> 4.46 us  [exchange_plane(): return lax.ppermute(x, ('blk', 'tgt'), pairs)]
  transfers between devices with their start and end apart: 21 -> 21, of which waited for: 11 -> 11; matrix products, arithmetic and copies ran while one was open for 0% -> 0% of each run, Pallas kernels for 19% -> 14%
where the time goes in v6:
time: 52.9 us; the launch traced here: 52.7 us
  starting transfers between devices  25.5 us (48%)
  Pallas kernels  13.5 us (26%)
  waiting for transfers between devices  12.8 us (24%)
  between operations  0.79 us (1%)
    ppermute x9, starting transfers between devices, exchange_sec(): lax.ppermute(x, 'sec', [(s, s ^ mask) for s in range(lax.axis_size('sec'))])  13.3 us
    ppermute x9, starting transfers between devices, exchange_plane(): return lax.ppermute(x, ('blk', 'tgt'), pairs)  11.8 us
    pallas_call x8, Pallas kernels, helmholtz(): pl.pallas_call(functools.partial(helmholtz_kernel, at), in_specs=[VMEM] *...  7.56 us
    ppermute x9, waiting for transfers between devices, exchange_sec(): lax.ppermute(x, 'sec', [(s, s ^ mask) for s in range(lax.axis_size('sec'))])  6.78 us
    ppermute x9, waiting for transfers between devices, exchange_plane(): return lax.ppermute(x, ('blk', 'tgt'), pairs)  4.46 us
    pallas_call x1, Pallas kernels, amplitude_parts(): pl.pallas_call(functools.partial(amplitude_kernel, panels), in_specs=[HBM...  2.65 us
    pallas_call x1, Pallas kernels, pressures(): pl.pallas_call(functools.partial(pressure_kernel, secs, tgt_n), in_specs=...  1.9 us
    ppermute x3, waiting for transfers between devices, exchange_core(): lax.ppermute(x, 'tgt', [(t, t ^ 1) for t in range(lax.axis_size('tgt'))])  1.59 us
  transfers between devices with their start and end apart: 21, of which 11 were waited for; matrix products, arithmetic and copies ran while one was open for 0% of the time, Pallas kernels for 14%

profile of v6, /device:TPU:0, one launch (start us, length us, event | category | flops | bytes accessed | tf_op | source)
XLA Modules:
  0.0 52.7 jit_solution(10480816470003394108)
XLA Ops:
  0.6 2.7 %amplitude_parts.1 = (f32[64,128]{1,0:T(8,128)S(1)}, bf16[80,128]{1,0:T(8,128)(2,1)S(1)}, bf16[80,128]{1,0:T(8,128)(2,1)S(1)}, bf16[80,128]{1,0:T(8,128)(2,1)S(1)}, bf16[16,128]{1,0:T(8,128)(2,1)S(1)}) custom-call(bf16[2,256,2048]{2,1,0:T(8,128)(2,1)} %r_hbm.1, bf16[2048,128]{1,0:T(8,128)(2,1)} %l_hbm.1, f32[3,128]{1,0:T(4,128)} %xyz_hbm.1, ...), custom_call_target="tpu_custom_call" | custom-call | flops 268435456 | bytes 1 | tf_op jit(solution)/shard_map/amplitude_parts/pallas_call | solution.py:135
  3.3 3.0 %collective-permute-start = (bf16[80,128]{1,0:T(8,128)(2,1)S(1)}, bf16[80,128]{1,0:T(8,128)(2,1)S(1)}, u32[]{:S(2)}, u32[]{:S(2)}) collective-permute-start(bf16[80,128]{1,0:T(8,128)(2,1)S(1)} %get-tuple-element.38), channel_id=1, source_target_pairs={{0,16},{4,20},{8,24},{12,28},{16,0},{20,4},{24,8},{28,12},{1,17},{... | collective-permute-start | bytes 61448 | tf_op jit(solution)/shard_map/ppermute | solution.py:37
  6.3 1.5 %collective-permute-start.1 = (bf16[80,128]{1,0:T(8,128)(2,1)S(1)}, bf16[80,128]{1,0:T(8,128)(2,1)S(1)}, u32[]{:S(2)}, u32[]{:S(2)}) collective-permute-start(bf16[80,128]{1,0:T(8,128)(2,1)S(1)} %get-tuple-element.39), channel_id=1, source_target_pairs={{0,8},{4,12},{8,0},{12,4},{16,24},{20,28},{24,16},{28,20},{1,9},{5... | collective-permute-start | bytes 61448 | tf_op jit(solution)/shard_map/ppermute | solution.py:37
  7.9 3.0 %collective-permute-start.9 = (bf16[128,1024]{1,0:T(8,128)(2,1)S(1)}, bf16[128,1024]{1,0:T(8,128)(2,1)S(1)}, u32[]{:S(2)}, u32[]{:S(2)}) collective-permute-start(bf16[128,1024]{1,0:T(8,128)(2,1)S(1)} %bitcast.5), channel_id=1, source_target_pairs={{0,24},{4,28},{8,16},{12,20},{16,8},{20,12},{24,0},{28,4},{1,25},{... | collective-permute-start | bytes 786440 | tf_op jit(solution)/shard_map/ppermute | solution.py:37
  11.4 1.5 %collective-permute-done.2.refs_4_ = bf16[80,128]{1,0:T(8,128)(2,1)S(1)} collective-permute-done((bf16[80,128]{1,0:T(8,128)(2,1)S(1)}, bf16[80,128]{1,0:T(8,128)(2,1)S(1)}, u32[]{:S(2)}, u32[]{:S(2)}) %collective-permute-start.2) | collective-permute-done | bytes 20512 | tf_op jit(solution)/shard_map/ppermute | solution.py:37
  12.9 3.6 %collective-permute-start.5 = (bf16[192,128]{1,0:T(8,128)(2,1)S(1)}, bf16[192,128]{1,0:T(8,128)(2,1)S(1)}, u32[]{:S(2)}, u32[]{:S(2)}) collective-permute-start(bf16[192,128]{1,0:T(8,128)(2,1)S(1)} %get-tuple-element.42.refs_0_.src_ref), channel_id=1, source_target_pairs={{0,3},{1,2},{2,1},{3,0},{4,7},{5,6},{6,5},{7,4},{8,11},{9,10},{10,... | collective-permute-start | bytes 147464 | tf_op jit(solution)/shard_map/ppermute | solution.py:41
  16.5 0.8 %collective-permute-start.3 = (bf16[192,128]{1,0:T(8,128)(2,1)S(1)}, bf16[192,128]{1,0:T(8,128)(2,1)S(1)}, u32[]{:S(2)}, u32[]{:S(2)}) collective-permute-start(bf16[192,128]{1,0:T(8,128)(2,1)S(1)} %get-tuple-element.42.refs_0_.src_ref), channel_id=1, source_target_pairs={{0,1},{1,0},{2,3},{3,2},{4,5},{5,4},{6,7},{7,6},{8,9},{9,8},{10,11... | collective-permute-start | bytes 147464 | tf_op jit(solution)/shard_map/ppermute | solution.py:41
  17.4 0.9 %helmholtz.8 = (bf16[512,512]{1,0:T(8,128)(2,1)S(1)}, bf16[512,512]{1,0:T(8,128)(2,1)S(1)}) custom-call(bf16[64,512]{1,0:T(8,128)(2,1)S(1)} %target_matrix.1.tgt_ref, bf16[192,128]{1,0:T(8,128)(2,1)S(1)} %get-tuple-element.42.refs_0_.src_ref), custom_call_target="tpu_custom_call" | custom-call | flops 1022361600 | bytes 1 | tf_op jit(solution)/shard_map/helmholtz/pallas_call | solution.py:292
  18.3 0.7 %collective-permute-done.5.refs_3_.src_ref = bf16[192,128]{1,0:T(8,128)(2,1)S(1)} collective-permute-done((bf16[192,128]{1,0:T(8,128)(2,1)S(1)}, bf16[192,128]{1,0:T(8,128)(2,1)S(1)}, u32[]{:S(2)}, u32[]{:S(2)}) %collective-permute-start.5) | collective-permute-done | bytes 49184 | tf_op jit(solution)/shard_map/ppermute | solution.py:41
  19.3 2.2 %collective-permute-done.4.refs_2_.src_ref = bf16[192,128]{1,0:T(8,128)(2,1)S(1)} collective-permute-done((bf16[192,128]{1,0:T(8,128)(2,1)S(1)}, bf16[192,128]{1,0:T(8,128)(2,1)S(1)}, u32[]{:S(2)}, u32[]{:S(2)}) %collective-permute-start.4) | collective-permute-done | bytes 49184 | tf_op jit(solution)/shard_map/ppermute | solution.py:41
  21.6 0.9 %helmholtz.11 = (bf16[512,512]{1,0:T(8,128)(2,1)S(1)}, bf16[512,512]{1,0:T(8,128)(2,1)S(1)}) custom-call(bf16[64,512]{1,0:T(8,128)(2,1)S(1)} %target_matrix.1.tgt_ref, bf16[192,128]{1,0:T(8,128)(2,1)S(1)} %collective-permute-done.5.refs_3_.src_ref), custom_call_target="tpu_custom_call" | custom-call | flops 1022361600 | bytes 1 | tf_op jit(solution)/shard_map/helmholtz/pallas_call | solution.py:292
  22.6 0.9 %helmholtz.10 = (bf16[512,512]{1,0:T(8,128)(2,1)S(1)}, bf16[512,512]{1,0:T(8,128)(2,1)S(1)}) custom-call(bf16[64,512]{1,0:T(8,128)(2,1)S(1)} %target_matrix.1.tgt_ref, bf16[192,128]{1,0:T(8,128)(2,1)S(1)} %collective-permute-done.4.refs_2_.src_ref), custom_call_target="tpu_custom_call" | custom-call | flops 1022361600 | bytes 1 | tf_op jit(solution)/shard_map/helmholtz/pallas_call | solution.py:292
  23.5 0.9 %helmholtz.9 = (bf16[512,512]{1,0:T(8,128)(2,1)S(1)}, bf16[512,512]{1,0:T(8,128)(2,1)S(1)}) custom-call(bf16[64,512]{1,0:T(8,128)(2,1)S(1)} %target_matrix.1.tgt_ref, bf16[192,128]{1,0:T(8,128)(2,1)S(1)} %collective-permute-done.3.refs_1_.src_ref), custom_call_target="tpu_custom_call" | custom-call | flops 1022361600 | bytes 1 | tf_op jit(solution)/shard_map/helmholtz/pallas_call | solution.py:292
  24.5 0.9 %collective-permute-done.7.refs_6_.refs_23_ = bf16[128,1024]{1,0:T(8,128)(2,1)S(1)} collective-permute-done((bf16[128,1024]{1,0:T(8,128)(2,1)S(1)}, bf16[128,1024]{1,0:T(8,128)(2,1)S(1)}, u32[]{:S(2)}, u32[]{:S(2)}) %collective-permute-start.7) | collective-permute-done | bytes 262176 | tf_op jit(solution)/shard_map/ppermute | solution.py:37
  25.9 3.4 %collective-permute-start.12 = (bf16[4,32,128]{2,1,0:T(8,128)(2,1)S(1)}, bf16[4,32,128]{2,1,0:T(8,128)(2,1)S(1)}, u32[]{:S(2)}, u32[]{:S(2)}) collective-permute-start(bf16[4,32,128]{2,1,0:T(8,128)(2,1)S(1)} %velocities.1.refs_0_), channel_id=1, source_target_pairs={{0,3},{1,2},{2,1},{3,0},{4,7},{5,6},{6,5},{7,4},{8,11},{9,10},{10,... | collective-permute-start | bytes 98312 | tf_op jit(solution)/shard_map/ppermute | solution.py:41
  29.4 1.0 %collective-permute-start.10 = (bf16[4,32,128]{2,1,0:T(8,128)(2,1)S(1)}, bf16[4,32,128]{2,1,0:T(8,128)(2,1)S(1)}, u32[]{:S(2)}, u32[]{:S(2)}) collective-permute-start(bf16[4,32,128]{2,1,0:T(8,128)(2,1)S(1)} %velocities.1.refs_0_), channel_id=1, source_target_pairs={{0,1},{1,0},{2,3},{3,2},{4,5},{5,4},{6,7},{7,6},{8,9},{9,8},{10,11... | collective-permute-start | bytes 98312 | tf_op jit(solution)/shard_map/ppermute | solution.py:41
  30.4 0.9 %helmholtz.15 = (bf16[512,512]{1,0:T(8,128)(2,1)S(1)}, bf16[512,512]{1,0:T(8,128)(2,1)S(1)}) custom-call(bf16[64,512]{1,0:T(8,128)(2,1)S(1)} %target_matrix.1.tgt_ref, bf16[4,192,128]{2,1,0:T(8,128)(2,1)S(1)} %collective-permute-done.6.refs_4_.src_ref, bf16[4,32,128]{2,1,0:T(8,128)(2,1)S(1)} %velocities.1.refs_0_), custom_call_target="tpu_custom_call" | custom-call | flops 1431306240 | bytes 1 | tf_op jit(solution)/shard_map/helmholtz/pallas_call | solution.py:292
  31.3 0.9 %helmholtz.14 = (bf16[512,512]{1,0:T(8,128)(2,1)S(1)}, bf16[512,512]{1,0:T(8,128)(2,1)S(1)}) custom-call(bf16[64,512]{1,0:T(8,128)(2,1)S(1)} %target_matrix.1.tgt_ref, bf16[4,192,128]{2,1,0:T(8,128)(2,1)S(1)} %collective-permute-done.6.refs_4_.src_ref, bf16[4,32,128]{2,1,0:T(8,128)(2,1)S(1)} %velocities.1.refs_0_), custom_call_target="tpu_custom_call" | custom-call | flops 1431306240 | bytes 1 | tf_op jit(solution)/shard_map/helmholtz/pallas_call | solution.py:292
  32.3 0.9 %helmholtz.13 = (bf16[512,512]{1,0:T(8,128)(2,1)S(1)}, bf16[512,512]{1,0:T(8,128)(2,1)S(1)}) custom-call(bf16[64,512]{1,0:T(8,128)(2,1)S(1)} %target_matrix.1.tgt_ref, bf16[4,192,128]{2,1,0:T(8,128)(2,1)S(1)} %collective-permute-done.6.refs_4_.src_ref, bf16[4,32,128]{2,1,0:T(8,128)(2,1)S(1)} %velocities.1.refs_0_), custom_call_target="tpu_custom_call" | custom-call | flops 1431306240 | bytes 1 | tf_op jit(solution)/shard_map/helmholtz/pallas_call | solution.py:292
  33.2 0.9 %collective-permute-done.11.refs_2_ = bf16[4,32,128]{2,1,0:T(8,128)(2,1)S(1)} collective-permute-done((bf16[4,32,128]{2,1,0:T(8,128)(2,1)S(1)}, bf16[4,32,128]{2,1,0:T(8,128)(2,1)S(1)}, u32[]{:S(2)}, u32[]{:S(2)}) %collective-permute-start.11) | collective-permute-done | bytes 32800 | tf_op jit(solution)/shard_map/ppermute | solution.py:41
  34.3 0.9 %helmholtz.12 = (bf16[512,512]{1,0:T(8,128)(2,1)S(1)}, bf16[512,512]{1,0:T(8,128)(2,1)S(1)}) custom-call(bf16[64,512]{1,0:T(8,128)(2,1)S(1)} %target_matrix.1.tgt_ref, bf16[4,192,128]{2,1,0:T(8,128)(2,1)S(1)} %collective-permute-done.6.refs_4_.src_ref, bf16[4,32,128]{2,1,0:T(8,128)(2,1)S(1)} %velocities.1.refs_0_), custom_call_target="tpu_custom_call" | custom-call | flops 1431306240 | bytes 1 | tf_op jit(solution)/shard_map/helmholtz/pallas_call | solution.py:292
  35.6 1.9 %pressures.1 = (bf16[4,32,128]{2,1,0:T(8,128)(2,1)S(1)}, f32[16,32,128]{2,1,0:T(8,128)S(1)}, bf16[16,32,128]{2,1,0:T(8,128)(2,1)S(1)}) custom-call(s32[4,128]{1,0:T(4,128)S(1)} %get-tuple-element.41.cpl, bf16[4,32,128]{2,1,0:T(8,128)(2,1)S(1)} %velocities.1.refs_0_, bf16[4,32,128]{2,1,0:T(8,128)(2,1)S(1)} %collective-permute-done.10.refs_1_, ...), custom_call_target="tpu_custom_call" | custom-call | tf_op jit(solution)/shard_map/pressures/pallas_call | solution.py:351
  37.7 1.2 %collective-permute-done.14.got_ref = bf16[16,32,128]{2,1,0:T(8,128)(2,1)S(1)} collective-permute-done((bf16[16,32,128]{2,1,0:T(8,128)(2,1)S(1)}, bf16[16,32,128]{2,1,0:T(8,128)(2,1)S(1)}, u32[]{:S(2)}, u32[]{:S(2)}) %collective-permute-start.14) | collective-permute-done | bytes 131104 | tf_op jit(solution)/shard_map/ppermute | solution.py:45
  39.0 2.5 %collective-permute-start.15 = (bf16[4,32,128]{2,1,0:T(8,128)(2,1)S(1)}, bf16[4,32,128]{2,1,0:T(8,128)(2,1)S(1)}, u32[]{:S(2)}, u32[]{:S(2)}) collective-permute-start(bf16[4,32,128]{2,1,0:T(8,128)(2,1)S(1)} %get-tuple-element.62), channel_id=1, source_target_pairs={{0,3},{1,2},{2,1},{3,0},{4,7},{5,6},{6,5},{7,4},{8,11},{9,10},{10,... | collective-permute-start | bytes 98312 | tf_op jit(solution)/shard_map/ppermute | solution.py:41
  41.5 1.9 %collective-permute-start.17 = (bf16[4,32,128]{2,1,0:T(8,128)(2,1)S(1)}, bf16[4,32,128]{2,1,0:T(8,128)(2,1)S(1)}, u32[]{:S(2)}, u32[]{:S(2)}) collective-permute-start(bf16[4,32,128]{2,1,0:T(8,128)(2,1)S(1)} %get-tuple-element.64), channel_id=1, source_target_pairs={{0,1},{1,0},{2,3},{3,2},{4,5},{5,4},{6,7},{7,6},{8,9},{9,8},{10,11... | collective-permute-start | bytes 98312 | tf_op jit(solution)/shard_map/ppermute | solution.py:41
  43.4 1.7 %collective-permute-done.15.refs_1_ = bf16[4,32,128]{2,1,0:T(8,128)(2,1)S(1)} collective-permute-done((bf16[4,32,128]{2,1,0:T(8,128)(2,1)S(1)}, bf16[4,32,128]{2,1,0:T(8,128)(2,1)S(1)}, u32[]{:S(2)}, u32[]{:S(2)}) %collective-permute-start.15) | collective-permute-done | bytes 32800 | tf_op jit(solution)/shard_map/ppermute | solution.py:41
  45.1 1.2 %collective-permute-done.16.refs_2_ = bf16[4,32,128]{2,1,0:T(8,128)(2,1)S(1)} collective-permute-done((bf16[4,32,128]{2,1,0:T(8,128)(2,1)S(1)}, bf16[4,32,128]{2,1,0:T(8,128)(2,1)S(1)}, u32[]{:S(2)}, u32[]{:S(2)}) %collective-permute-start.16) | collective-permute-done | bytes 32800 | tf_op jit(solution)/shard_map/ppermute | solution.py:41
  46.6 1.6 %collective-permute-start.19 = (bf16[2,32,128]{2,1,0:T(8,128)(2,1)S(1)}, bf16[2,32,128]{2,1,0:T(8,128)(2,1)S(1)}, u32[]{:S(2)}, u32[]{:S(2)}) collective-permute-start(bf16[2,32,128]{2,1,0:T(8,128)(2,1)S(1)} %get-tuple-element.68), channel_id=1, source_target_pairs={{0,16},{4,20},{8,24},{12,28},{16,0},{20,4},{24,8},{28,12},{1,17},{... | collective-permute-start | bytes 49160 | tf_op jit(solution)/shard_map/ppermute | solution.py:37
  48.2 1.7 %collective-permute-start.20 = (bf16[2,32,128]{2,1,0:T(8,128)(2,1)S(1)}, bf16[2,32,128]{2,1,0:T(8,128)(2,1)S(1)}, u32[]{:S(2)}, u32[]{:S(2)}) collective-permute-start(bf16[2,32,128]{2,1,0:T(8,128)(2,1)S(1)} %get-tuple-element.69), channel_id=1, source_target_pairs={{0,8},{4,12},{8,0},{12,4},{16,24},{20,28},{24,16},{28,20},{1,9},{5... | collective-permute-start | bytes 49160 | tf_op jit(solution)/shard_map/ppermute | solution.py:37
  49.9 1.1 %collective-permute-done.18.r3 = bf16[2,32,128]{2,1,0:T(8,128)(2,1)S(1)} collective-permute-done((bf16[2,32,128]{2,1,0:T(8,128)(2,1)S(1)}, bf16[2,32,128]{2,1,0:T(8,128)(2,1)S(1)}, u32[]{:S(2)}, u32[]{:S(2)}) %collective-permute-start.18) | collective-permute-done | bytes 16416 | tf_op jit(solution)/shard_map/ppermute | solution.py:37
  51.1 0.9 %collective-permute-done.20.r2 = bf16[2,32,128]{2,1,0:T(8,128)(2,1)S(1)} collective-permute-done((bf16[2,32,128]{2,1,0:T(8,128)(2,1)S(1)}, bf16[2,32,128]{2,1,0:T(8,128)(2,1)S(1)}, u32[]{:S(2)}, u32[]{:S(2)}) %collective-permute-start.20) | collective-permute-done | bytes 16416 | tf_op jit(solution)/shard_map/ppermute | solution.py:37
  52.0 0.8 %outputs.1 = (f32[128,128]{1,0:T(8,128)}, bf16[128,128]{1,0:T(8,128)(2,1)}) custom-call(f32[2,32,128]{2,1,0:T(8,128)S(1)} %get-tuple-element.66.r0, bf16[2,32,128]{2,1,0:T(8,128)(2,1)S(1)} %collective-permute-done.18.r3, bf16[2,32,128]{2,1,0:T(8,128)(2,1)S(1)} %collective-permute-done.19.r1, bf16[2,32,128]{2,1,0:T(8,128)(2,1)S(1)} %collective-permute-done.20.r2), custom_call_target="tpu_custom_call" | custom-call | tf_op jit(solution)/shard_map/outputs/pallas_call | solution.py:430
  (32 shorter events, 2.5 us)
Async XLA Ops:
  0.6 7.2 %copy-start = (bf16[128,8,128]{2,1,0:T(8,128)(2,1)S(1)}, bf16[128,8,128]{2,1,0:T(8,128)(2,1)}, u32[]{:S(2)}) copy-start(bf16[128,8,128]{2,1,0:T(8,128)(2,1)} %param.8) | copy-start | bytes 786436
  3.3 8.1 %collective-permute-start = (bf16[80,128]{1,0:T(8,128)(2,1)S(1)}, bf16[80,128]{1,0:T(8,128)(2,1)S(1)}, u32[]{:S(2)}, u32[]{:S(2)}) collective-permute-start(bf16[80,128]{1,0:T(8,128)(2,1)S(1)} %get-tuple-element.38), channel_id=1, source_target_pairs={{0,16},{4,20},{8,24},{12,28},{16,0},{20,4},{24,8},{28,12},{1,17},{... | collective-permute-start | bytes 61448 | tf_op jit(solution)/shard_map/ppermute | solution.py:37
  6.3 5.1 %collective-permute-start.1 = (bf16[80,128]{1,0:T(8,128)(2,1)S(1)}, bf16[80,128]{1,0:T(8,128)(2,1)S(1)}, u32[]{:S(2)}, u32[]{:S(2)}) collective-permute-start(bf16[80,128]{1,0:T(8,128)(2,1)S(1)} %get-tuple-element.39), channel_id=1, source_target_pairs={{0,8},{4,12},{8,0},{12,4},{16,24},{20,28},{24,16},{28,20},{1,9},{5... | collective-permute-start | bytes 61448 | tf_op jit(solution)/shard_map/ppermute | solution.py:37
  7.8 5.0 %collective-permute-start.2 = (bf16[80,128]{1,0:T(8,128)(2,1)S(1)}, bf16[80,128]{1,0:T(8,128)(2,1)S(1)}, u32[]{:S(2)}, u32[]{:S(2)}) collective-permute-start(bf16[80,128]{1,0:T(8,128)(2,1)S(1)} %get-tuple-element.40), channel_id=1, source_target_pairs={{0,24},{4,28},{8,16},{12,20},{16,8},{20,12},{24,0},{28,4},{1,25},{... | collective-permute-start | bytes 61448 | tf_op jit(solution)/shard_map/ppermute | solution.py:37
  7.9 16.6 %collective-permute-start.9 = (bf16[128,1024]{1,0:T(8,128)(2,1)S(1)}, bf16[128,1024]{1,0:T(8,128)(2,1)S(1)}, u32[]{:S(2)}, u32[]{:S(2)}) collective-permute-start(bf16[128,1024]{1,0:T(8,128)(2,1)S(1)} %bitcast.5), channel_id=1, source_target_pairs={{0,24},{4,28},{8,16},{12,20},{16,8},{20,12},{24,0},{28,4},{1,25},{... | collective-permute-start | bytes 786440 | tf_op jit(solution)/shard_map/ppermute | solution.py:37
  10.9 13.6 %collective-permute-start.8 = (bf16[128,1024]{1,0:T(8,128)(2,1)S(1)}, bf16[128,1024]{1,0:T(8,128)(2,1)S(1)}, u32[]{:S(2)}, u32[]{:S(2)}) collective-permute-start(bf16[128,1024]{1,0:T(8,128)(2,1)S(1)} %bitcast.6), channel_id=1, source_target_pairs={{0,8},{4,12},{8,0},{12,4},{16,24},{20,28},{24,16},{28,20},{1,9},{5... | collective-permute-start | bytes 786440 | tf_op jit(solution)/shard_map/ppermute | solution.py:37
  12.9 6.2 %collective-permute-start.5 = (bf16[192,128]{1,0:T(8,128)(2,1)S(1)}, bf16[192,128]{1,0:T(8,128)(2,1)S(1)}, u32[]{:S(2)}, u32[]{:S(2)}) collective-permute-start(bf16[192,128]{1,0:T(8,128)(2,1)S(1)} %get-tuple-element.42.refs_0_.src_ref), channel_id=1, source_target_pairs={{0,3},{1,2},{2,1},{3,0},{4,7},{5,6},{6,5},{7,4},{8,11},{9,10},{10,... | collective-permute-start | bytes 147464 | tf_op jit(solution)/shard_map/ppermute | solution.py:41
  16.5 5.0 %collective-permute-start.4 = (bf16[192,128]{1,0:T(8,128)(2,1)S(1)}, bf16[192,128]{1,0:T(8,128)(2,1)S(1)}, u32[]{:S(2)}, u32[]{:S(2)}) collective-permute-start(bf16[192,128]{1,0:T(8,128)(2,1)S(1)} %get-tuple-element.42.refs_0_.src_ref), channel_id=1, source_target_pairs={{0,2},{1,3},{2,0},{3,1},{4,6},{5,7},{6,4},{7,5},{8,10},{9,11},{10,... | collective-permute-start | bytes 147464 | tf_op jit(solution)/shard_map/ppermute | solution.py:41
  16.5 5.0 %collective-permute-start.3 = (bf16[192,128]{1,0:T(8,128)(2,1)S(1)}, bf16[192,128]{1,0:T(8,128)(2,1)S(1)}, u32[]{:S(2)}, u32[]{:S(2)}) collective-permute-start(bf16[192,128]{1,0:T(8,128)(2,1)S(1)} %get-tuple-element.42.refs_0_.src_ref), channel_id=1, source_target_pairs={{0,1},{1,0},{2,3},{3,2},{4,5},{5,4},{6,7},{7,6},{8,9},{9,8},{10,11... | collective-permute-start | bytes 147464 | tf_op jit(solution)/shard_map/ppermute | solution.py:41
  19.0 6.4 %collective-permute-start.7 = (bf16[128,1024]{1,0:T(8,128)(2,1)S(1)}, bf16[128,1024]{1,0:T(8,128)(2,1)S(1)}, u32[]{:S(2)}, u32[]{:S(2)}) collective-permute-start(bf16[128,1024]{1,0:T(8,128)(2,1)S(1)} %bitcast.7), channel_id=1, source_target_pairs={{0,16},{4,20},{8,24},{12,28},{16,0},{20,4},{24,8},{28,12},{1,17},{... | collective-permute-start | bytes 786440 | tf_op jit(solution)/shard_map/ppermute | solution.py:37
  21.5 3.9 %collective-permute-start.6 = (bf16[4,192,128]{2,1,0:T(8,128)(2,1)S(1)}, bf16[4,192,128]{2,1,0:T(8,128)(2,1)S(1)}, u32[]{:S(2)}, u32[]{:S(2)}) collective-permute-start(bf16[4,192,128]{2,1,0:T(8,128)(2,1)S(1)} %stack.2), channel_id=1, source_target_pairs={{0,4},{4,0},{8,12},{12,8},{1,5},{5,1},{9,13},{13,9},{2,6},{6,2},{1... | collective-permute-start | bytes 589832 | tf_op jit(solution)/shard_map/ppermute | solution.py:45
  25.9 7.3 %collective-permute-start.12 = (bf16[4,32,128]{2,1,0:T(8,128)(2,1)S(1)}, bf16[4,32,128]{2,1,0:T(8,128)(2,1)S(1)}, u32[]{:S(2)}, u32[]{:S(2)}) collective-permute-start(bf16[4,32,128]{2,1,0:T(8,128)(2,1)S(1)} %velocities.1.refs_0_), channel_id=1, source_target_pairs={{0,3},{1,2},{2,1},{3,0},{4,7},{5,6},{6,5},{7,4},{8,11},{9,10},{10,... | collective-permute-start | bytes 98312 | tf_op jit(solution)/shard_map/ppermute | solution.py:41
  29.4 4.8 %collective-permute-start.11 = (bf16[4,32,128]{2,1,0:T(8,128)(2,1)S(1)}, bf16[4,32,128]{2,1,0:T(8,128)(2,1)S(1)}, u32[]{:S(2)}, u32[]{:S(2)}) collective-permute-start(bf16[4,32,128]{2,1,0:T(8,128)(2,1)S(1)} %velocities.1.refs_0_), channel_id=1, source_target_pairs={{0,2},{1,3},{2,0},{3,1},{4,6},{5,7},{6,4},{7,5},{8,10},{9,11},{10,... | collective-permute-start | bytes 98312 | tf_op jit(solution)/shard_map/ppermute | solution.py:41
  29.4 4.8 %collective-permute-start.10 = (bf16[4,32,128]{2,1,0:T(8,128)(2,1)S(1)}, bf16[4,32,128]{2,1,0:T(8,128)(2,1)S(1)}, u32[]{:S(2)}, u32[]{:S(2)}) collective-permute-start(bf16[4,32,128]{2,1,0:T(8,128)(2,1)S(1)} %velocities.1.refs_0_), channel_id=1, source_target_pairs={{0,1},{1,0},{2,3},{3,2},{4,5},{5,4},{6,7},{7,6},{8,9},{9,8},{10,11... | collective-permute-start | bytes 98312 | tf_op jit(solution)/shard_map/ppermute | solution.py:41
  34.2 1.4 %collective-permute-start.13 = (bf16[4,4,32,128]{3,2,1,0:T(8,128)(2,1)S(1)}, bf16[4,4,32,128]{3,2,1,0:T(8,128)(2,1)S(1)}, u32[]{:S(2)}, u32[]{:S(2)}) collective-permute-start(bf16[4,4,32,128]{3,2,1,0:T(8,128)(2,1)S(1)} %stack.3), channel_id=1, source_target_pairs={{0,4},{4,0},{8,12},{12,8},{1,5},{5,1},{9,13},{13,9},{2,6},{6,2},{1... | collective-permute-start | bytes 393224 | tf_op jit(solution)/shard_map/ppermute | solution.py:45
  37.5 1.4 %collective-permute-start.14 = (bf16[16,32,128]{2,1,0:T(8,128)(2,1)S(1)}, bf16[16,32,128]{2,1,0:T(8,128)(2,1)S(1)}, u32[]{:S(2)}, u32[]{:S(2)}) collective-permute-start(bf16[16,32,128]{2,1,0:T(8,128)(2,1)S(1)} %get-tuple-element.60), channel_id=1, source_target_pairs={{0,4},{4,0},{8,12},{12,8},{1,5},{5,1},{9,13},{13,9},{2,6},{6,2},{1... | collective-permute-start | bytes 393224 | tf_op jit(solution)/shard_map/ppermute | solution.py:45
  39.0 6.1 %collective-permute-start.15 = (bf16[4,32,128]{2,1,0:T(8,128)(2,1)S(1)}, bf16[4,32,128]{2,1,0:T(8,128)(2,1)S(1)}, u32[]{:S(2)}, u32[]{:S(2)}) collective-permute-start(bf16[4,32,128]{2,1,0:T(8,128)(2,1)S(1)} %get-tuple-element.62), channel_id=1, source_target_pairs={{0,3},{1,2},{2,1},{3,0},{4,7},{5,6},{6,5},{7,4},{8,11},{9,10},{10,... | collective-permute-start | bytes 98312 | tf_op jit(solution)/shard_map/ppermute | solution.py:41
  41.5 4.8 %collective-permute-start.16 = (bf16[4,32,128]{2,1,0:T(8,128)(2,1)S(1)}, bf16[4,32,128]{2,1,0:T(8,128)(2,1)S(1)}, u32[]{:S(2)}, u32[]{:S(2)}) collective-permute-start(bf16[4,32,128]{2,1,0:T(8,128)(2,1)S(1)} %get-tuple-element.63), channel_id=1, source_target_pairs={{0,2},{1,3},{2,0},{3,1},{4,6},{5,7},{6,4},{7,5},{8,10},{9,11},{10,... | collective-permute-start | bytes 98312 | tf_op jit(solution)/shard_map/ppermute | solution.py:41
  41.5 4.8 %collective-permute-start.17 = (bf16[4,32,128]{2,1,0:T(8,128)(2,1)S(1)}, bf16[4,32,128]{2,1,0:T(8,128)(2,1)S(1)}, u32[]{:S(2)}, u32[]{:S(2)}) collective-permute-start(bf16[4,32,128]{2,1,0:T(8,128)(2,1)S(1)} %get-tuple-element.64), channel_id=1, source_target_pairs={{0,1},{1,0},{2,3},{3,2},{4,5},{5,4},{6,7},{7,6},{8,9},{9,8},{10,11... | collective-permute-start | bytes 98312 | tf_op jit(solution)/shard_map/ppermute | solution.py:41
  46.4 4.7 %collective-permute-start.18 = (bf16[2,32,128]{2,1,0:T(8,128)(2,1)S(1)}, bf16[2,32,128]{2,1,0:T(8,128)(2,1)S(1)}, u32[]{:S(2)}, u32[]{:S(2)}) collective-permute-start(bf16[2,32,128]{2,1,0:T(8,128)(2,1)S(1)} %get-tuple-element.67), channel_id=1, source_target_pairs={{0,24},{4,28},{8,16},{12,20},{16,8},{20,12},{24,0},{28,4},{1,25},{... | collective-permute-start | bytes 49160 | tf_op jit(solution)/shard_map/ppermute | solution.py:37
  46.6 4.4 %collective-permute-start.19 = (bf16[2,32,128]{2,1,0:T(8,128)(2,1)S(1)}, bf16[2,32,128]{2,1,0:T(8,128)(2,1)S(1)}, u32[]{:S(2)}, u32[]{:S(2)}) collective-permute-start(bf16[2,32,128]{2,1,0:T(8,128)(2,1)S(1)} %get-tuple-element.68), channel_id=1, source_target_pairs={{0,16},{4,20},{8,24},{12,28},{16,0},{20,4},{24,8},{28,12},{1,17},{... | collective-permute-start | bytes 49160 | tf_op jit(solution)/shard_map/ppermute | solution.py:37
  48.2 3.7 %collective-permute-start.20 = (bf16[2,32,128]{2,1,0:T(8,128)(2,1)S(1)}, bf16[2,32,128]{2,1,0:T(8,128)(2,1)S(1)}, u32[]{:S(2)}, u32[]{:S(2)}) collective-permute-start(bf16[2,32,128]{2,1,0:T(8,128)(2,1)S(1)} %get-tuple-element.69), channel_id=1, source_target_pairs={{0,8},{4,12},{8,0},{12,4},{16,24},{20,28},{24,16},{28,20},{1,9},{5... | collective-permute-start | bytes 49160 | tf_op jit(solution)/shard_map/ppermute | solution.py:37

commit v7 on v6

--- a/solution.py
+++ b/solution.py
@@ -176,20 +176,20 @@
     )(own, geo, x, y, d)
 
 
-def stack_kernel(*refs):
-    for i, r in enumerate(refs[:-1]):
+def stack_kernel(count, *refs):
+    for i, r in enumerate(refs[:count]):
         refs[-1][i] = r[...]
 
 
-def stack(parts):
-    return pl.pallas_call(
-        stack_kernel,
-        in_specs=[VMEM] * len(parts),
+def stack(parts, after=()):
+    return pl.pallas_call(
+        functools.partial(stack_kernel, len(parts)),
+        in_specs=[VMEM] * len(parts) + [pl.BlockSpec(memory_space=pl.ANY)] * len(after),
         out_specs=VMEM,
         out_shape=jax.ShapeDtypeStruct((len(parts),) + parts[0].shape, parts[0].dtype),
         compiler_params=limit(4),
         name="stack",
-    )(*parts)
+    )(*parts, *after)
 
 
 def velocity_kernel(width, blocks, scale, secs, cpl, *refs):
@@ -300,27 +300,52 @@
     )(targets, payload, *after)
 
 
-def pressure_kernel(secs, tgt_n, cpl, *refs):
-    v_near, v_far = refs[0:secs], refs[secs]
-    mats = refs[secs + 1 : 5 * secs + 1]
-    geo_ref, modes = refs[5 * secs + 1], refs[5 * secs + 2 : 5 * secs + 6]
-    pt_ref, near_ref, far_ref, lead, turned, total = refs[5 * secs + 6 :]
-    groups, width, lanes = v_near[0].shape
-    half = width // 2
-    side = groups * lanes
-    for i in range(2 * secs):
-        for j in range(groups):
-            v = v_near[i][j] if i < secs else v_far[i - secs, j]
+def product(velocity, mats, lead, turned):
+    count = len(mats) // 2
+    side = mats[0].shape[0]
+    lanes = 128
+    half = lead.shape[0] // 2
+    re = im = 0.0
+    for i in range(count):
+        for j in range(side // lanes):
+            v = velocity(i, j)
             col = slice(i * side + j * lanes, i * side + (j + 1) * lanes)
             lead[:, col] = v
             turned[0:half, col] = -v[half:]
             turned[half:, col] = v[0:half]
-    re = im = 0.0
-    for i in range(2 * secs):
+    for i in range(count):
         col = slice(i * side, (i + 1) * side)
         re += jnp.dot(lead[:, col], mats[2 * i][...], preferred_element_type=f32)
         im += jnp.dot(turned[:, col], mats[2 * i + 1][...], preferred_element_type=f32)
-    p = (re + im * cos_terms[3]).astype(bf16)
+    return re + im * cos_terms[3]
+
+
+def near_kernel(secs, *refs):
+    out_ref, lead, turned = refs[-3:]
+    out_ref[...] = product(lambda i, j: refs[i][j], refs[secs : 3 * secs], lead, turned)
+
+
+def near_pressures(v_near, mats):
+    secs = len(v_near)
+    groups, width, lanes = v_near[0].shape
+    side = groups * lanes
+    return pl.pallas_call(
+        functools.partial(near_kernel, secs),
+        in_specs=[VMEM] * (3 * secs),
+        out_specs=VMEM,
+        out_shape=jax.ShapeDtypeStruct((width, side), f32),
+        scratch_shapes=[pltpu.VMEM((width, secs * side), bf16)] * 2,
+        compiler_params=limit(4),
+        cost_estimate=pl.CostEstimate(flops=3900 * side * side, bytes_accessed=1, transcendentals=0),
+        name="near_pressures",
+    )(*v_near, *mats)
+
+
+def pressure_kernel(secs, tgt_n, cpl, part_ref, v_far, *refs):
+    mats, geo_ref, modes = refs[0 : 2 * secs], refs[2 * secs], refs[2 * secs + 1 : 2 * secs + 5]
+    pt_ref, near_ref, far_ref, lead, turned, total = refs[2 * secs + 5 :]
+    _, groups, width, lanes = v_far.shape
+    p = (part_ref[...] + product(lambda i, j: v_far[i, j], mats, lead, turned)).astype(bf16)
     total[...] = jnp.zeros_like(total)
     x, y, c, z = place()
     sec_bits, tgt_bits = bits_of(secs), bits_of(tgt_n)
@@ -342,12 +367,11 @@
     far_ref[...] = total[n:].astype(bf16)
 
 
-def pressures(cpl, v_near, v_far, mats, geo, modes, tgt_n):
-    secs = len(v_near)
-    groups, width, lanes = v_near[0].shape
+def pressures(cpl, part, v_far, mats, geo, modes, tgt_n):
+    secs, groups, width, lanes = v_far.shape
     side = groups * lanes
     n = secs * groups
-    args = [*v_near, v_far, *mats, geo, *modes]
+    args = [part, v_far, *mats, geo, *modes]
     return pl.pallas_call(
         functools.partial(pressure_kernel, secs, tgt_n),
         in_specs=[VMEM] * (1 + len(args)),
@@ -358,8 +382,8 @@
             jax.ShapeDtypeStruct((n, width, lanes), bf16),
         ],
         scratch_shapes=[
-            pltpu.VMEM((width, 2 * secs * side), bf16),
-            pltpu.VMEM((width, 2 * secs * side), bf16),
+            pltpu.VMEM((width, secs * side), bf16),
+            pltpu.VMEM((width, secs * side), bf16),
             pltpu.VMEM((2 * n, width, lanes), f32),
         ],
         compiler_params=limit(8),
@@ -462,8 +486,9 @@
     mats = [helmholtz(across, n) for n in near] + [helmholtz(across, far, i, (vel,), 1.4) for i in range(secs)]
     mats = [m for pair in mats for m in pair]
     v_near = [vel] + [exchange_sec(vel, m) for m in range(1, secs)]
-    v_far = exchange_core(stack(v_near))
-    pt, n_near, n_far = pressures(cpl, v_near, v_far, mats, targets, modes, tgts)
+    v_far = exchange_core(stack(v_near, mats[-1:]))
+    part = near_pressures(v_near, mats[: 2 * secs])
+    pt, n_near, n_far = pressures(cpl, part, v_far, mats[2 * secs :], targets, modes, tgts)
     parts = core_sum(n_near, exchange_core(n_far), secs)
     sec_got = [exchange_sec(p, m) for m, p in zip(range(1, secs), parts[1:])]
     finals = sec_sum(parts[0], sec_got, pt)
@@ -588,6 +613,123 @@
     return body(modal_loads, receptance, shapes, coupling, panel_coords, panel_areas)
 
 
+def rotate_combine(leading, second):
+    half_width = leading.shape[1] // 2
+    return jnp.concatenate(
+        [
+            leading[:, :half_width] - second[:, half_width:],
+            leading[:, half_width:] + second[:, :half_width],
+        ],
+        axis=1,
+    )
+
+
+def pressure_block(target_geometry, source_geometry, source_vel, total_panels):
+    delta_x = target_geometry[0][:, None] - source_geometry[0][None, :]
+    delta_y = target_geometry[1][:, None] - source_geometry[1][None, :]
+    delta_z = target_geometry[2][:, None] - source_geometry[2][None, :]
+    source_area = source_geometry[3][None, :]
+    distance = jnp.sqrt(
+        delta_x * delta_x + delta_y * delta_y + delta_z * delta_z + source_area / total_panels
+    )
+    weight = source_area / (distance * math.sqrt(total_panels))
+    phase_angle = wave_number * distance
+    kernel = jnp.concatenate(
+        [
+            (jnp.cos(phase_angle) * weight).astype(jnp.bfloat16),
+            (jnp.sin(phase_angle) * weight).astype(jnp.bfloat16),
+        ],
+        axis=0,
+    )
+    products = lax.dot_general(
+        kernel, source_vel, (((1,), (1,)), ((), ())), preferred_element_type=jnp.float32
+    )
+    target_count = target_geometry.shape[1]
+    return rotate_combine(products[:target_count], products[target_count:])
+
+
+def on_device_general(modal_loads, receptance, shapes, coupling, panel_coords, panel_areas):
+    pan_dev = panel_coords.shape[1]
+    case_width = modal_loads.shape[1]
+    device_count = lax.axis_size("blk") * lax.axis_size("tgt") * lax.axis_size("sec")
+    total_panels = float(pan_dev * device_count)
+    row_share = receptance.shape[1]
+    stacked = jnp.dot(
+        receptance.reshape(2 * row_share, receptance.shape[2]),
+        modal_loads,
+        preferred_element_type=jnp.float32,
+    )
+    modal_sum = rotate_combine(stacked[:row_share], stacked[row_share:])
+    modal_sum = lax.psum(modal_sum, "blk")
+    amplitudes = lax.all_gather(modal_sum.astype(jnp.bfloat16), ("tgt", "sec"), axis=0, tiled=True)
+    mode_block = shapes.shape[2]
+    blocks = amplitudes.reshape(-1, mode_block, case_width)
+    chosen = blocks[coupling]
+    block_count = coupling.shape[0]
+    shaped = shapes.reshape(block_count, -1, shapes.shape[1], mode_block)
+    vel_t = (
+        jnp.einsum("bpkm,bkmc->cbp", shaped, chosen, preferred_element_type=jnp.float32)
+        .reshape(case_width, pan_dev)
+        .astype(jnp.bfloat16)
+    )
+    geometry = jnp.concatenate([panel_coords, panel_areas[None, :]], axis=0)
+    source_vel, source_geometry = (
+        lax.all_gather(vel_t.astype(jnp.float32), ("tgt", "sec"), axis=1, tiled=True).astype(
+            vel_t.dtype
+        ),
+        lax.all_gather(geometry, ("tgt", "sec"), axis=1, tiled=True),
+    )
+    target_geometry = lax.all_gather(geometry, "blk", axis=1, tiled=True)
+    target_groups = pan_dev * lax.axis_size("blk") // pan_dev
+
+    def single_block(block_index):
+        target_block = lax.dynamic_slice_in_dim(target_geometry, block_index * pan_dev, pan_dev, 1)
+        return pressure_block(target_block, source_geometry, source_vel, total_panels)
+
+    stacked_terms = lax.map(single_block, jnp.arange(target_groups, dtype=jnp.int32))
+    pressure_f = lax.psum_scatter(
+        stacked_terms.reshape(pan_dev * lax.axis_size("blk"), case_width).astype(jnp.bfloat16),
+        "blk",
+        scatter_dimension=0,
+        tiled=True,
+    )
+    weighted = (panel_areas[:, None] * pressure_f.astype(jnp.float32)).astype(jnp.bfloat16)
+    contrib = jnp.einsum(
+        "bpkm,bpc->bkmc",
+        shaped,
+        weighted.reshape(block_count, -1, case_width),
+        preferred_element_type=jnp.float32,
+    )
+    onehot = (
+        coupling[:, :, None] == jnp.arange(blocks.shape[0], dtype=jnp.int32)[None, None, :]
+    ).astype(jnp.float32)
+    partial_loads = jnp.einsum(
+        "bkj,bkmc->jmc", onehot, contrib, precision=lax.Precision.HIGHEST
+    ).reshape(-1, case_width)
+    new_loads = lax.psum_scatter(
+        partial_loads, ("blk", "tgt", "sec"), scatter_dimension=0, tiled=True
+    )
+    return (new_loads, pressure_f)
+
+
+def on_device(modal_loads, receptance, shapes, coupling, panel_coords, panel_areas):
+    lanes = 128
+    secs = lax.axis_size("sec")
+    mine = modal_loads.shape[0] * lax.axis_size("blk") // (lax.axis_size("blk") * lax.axis_size("tgt") * secs)
+    fits = (
+        lax.axis_size("blk") == 2
+        and lax.axis_size("tgt") == 4
+        and secs & (secs - 1) == 0
+        and coupling.shape[0] == 1
+        and shapes.shape[2] == lanes
+        and panel_coords.shape[1] == lanes
+        and modal_loads.shape[1] == lanes
+        and mine == lanes
+    )
+    body = on_device_fast if fits else on_device_general
+    return body(modal_loads, receptance, shapes, coupling, panel_coords, panel_areas)
+
+
 def solution(mesh):
     in_specs = (
         P("blk", None),

time: 52.9 us -> 52.8 us (level)
  waiting for transfers between devices: 12.8 us -> 12.2 us
    pallas_call x2 -> x3, Pallas kernels: 0.02 us -> 0.84 us  [the longest x1 0.81 us: near_pressures(): pl.pallas_call(functools.partial(near_kernel, secs), in_specs=[VMEM] * (3...]
    pallas_call x1, Pallas kernels: 1.9 us -> 1.19 us  [pressures(): pl.pallas_call(functools.partial(pressure_kernel, secs, tgt_n), in_specs=...]
    ppermute x3, waiting for transfers between devices: 1.59 us -> 1.02 us  [exchange_core(): lax.ppermute(x, 'tgt', [(t, t ^ 1) for t in range(lax.axis_size('tgt'))])]
  transfers between devices with their start and end apart: 21 -> 21, of which waited for: 11 -> 10; matrix products, arithmetic and copies ran while one was open for 0% -> 0% of each run, Pallas kernels for 14% -> 16%
where the time goes in v7:
time: 52.8 us; the launch traced here: 52.6 us
  starting transfers between devices  25.9 us (49%)
  Pallas kernels  13.7 us (26%)
  waiting for transfers between devices  12.2 us (23%)
  between operations  0.79 us (1%)
    ppermute x9, starting transfers between devices, exchange_sec(): lax.ppermute(x, 'sec', [(s, s ^ mask) for s in range(lax.axis_size('sec'))])  13.4 us
    ppermute x9, starting transfers between devices, exchange_plane(): return lax.ppermute(x, ('blk', 'tgt'), pairs)  11.8 us
    pallas_call x8, Pallas kernels, helmholtz(): pl.pallas_call(functools.partial(helmholtz_kernel, at), in_specs=[VMEM] *...  7.58 us
    ppermute x9, waiting for transfers between devices, exchange_sec(): lax.ppermute(x, 'sec', [(s, s ^ mask) for s in range(lax.axis_size('sec'))])  6.74 us
    ppermute x9, waiting for transfers between devices, exchange_plane(): return lax.ppermute(x, ('blk', 'tgt'), pairs)  4.47 us
    pallas_call x1, Pallas kernels, amplitude_parts(): pl.pallas_call(functools.partial(amplitude_kernel, panels), in_specs=[HBM...  2.65 us
    pallas_call x1, Pallas kernels, pressures(): pl.pallas_call(functools.partial(pressure_kernel, secs, tgt_n), in_specs=...  1.19 us
  transfers between devices with their start and end apart: 21, of which 10 were waited for; matrix products, arithmetic and copies ran while one was open for 0% of the time, Pallas kernels for 16%

profile of v7, /device:TPU:0, one launch (start us, length us, event | category | flops | bytes accessed | tf_op | source)
XLA Modules:
  0.0 52.6 jit_solution(14545025003416998441)
XLA Ops:
  0.6 2.7 %amplitude_parts.1 = (f32[64,128]{1,0:T(8,128)S(1)}, bf16[80,128]{1,0:T(8,128)(2,1)S(1)}, bf16[80,128]{1,0:T(8,128)(2,1)S(1)}, bf16[80,128]{1,0:T(8,128)(2,1)S(1)}, bf16[16,128]{1,0:T(8,128)(2,1)S(1)}) custom-call(bf16[2,256,2048]{2,1,0:T(8,128)(2,1)} %r_hbm.1, bf16[2048,128]{1,0:T(8,128)(2,1)} %l_hbm.1, f32[3,128]{1,0:T(4,128)} %xyz_hbm.1, ...), custom_call_target="tpu_custom_call" | custom-call | flops 268435456 | bytes 1 | tf_op jit(solution)/shard_map/amplitude_parts/pallas_call | solution.py:135
  3.3 3.0 %collective-permute-start = (bf16[80,128]{1,0:T(8,128)(2,1)S(1)}, bf16[80,128]{1,0:T(8,128)(2,1)S(1)}, u32[]{:S(2)}, u32[]{:S(2)}) collective-permute-start(bf16[80,128]{1,0:T(8,128)(2,1)S(1)} %get-tuple-element.38), channel_id=1, source_target_pairs={{0,16},{4,20},{8,24},{12,28},{16,0},{20,4},{24,8},{28,12},{1,17},{... | collective-permute-start | bytes 61448 | tf_op jit(solution)/shard_map/ppermute | solution.py:37
  6.3 1.5 %collective-permute-start.1 = (bf16[80,128]{1,0:T(8,128)(2,1)S(1)}, bf16[80,128]{1,0:T(8,128)(2,1)S(1)}, u32[]{:S(2)}, u32[]{:S(2)}) collective-permute-start(bf16[80,128]{1,0:T(8,128)(2,1)S(1)} %get-tuple-element.39), channel_id=1, source_target_pairs={{0,8},{4,12},{8,0},{12,4},{16,24},{20,28},{24,16},{28,20},{1,9},{5... | collective-permute-start | bytes 61448 | tf_op jit(solution)/shard_map/ppermute | solution.py:37
  7.9 3.0 %collective-permute-start.9 = (bf16[128,1024]{1,0:T(8,128)(2,1)S(1)}, bf16[128,1024]{1,0:T(8,128)(2,1)S(1)}, u32[]{:S(2)}, u32[]{:S(2)}) collective-permute-start(bf16[128,1024]{1,0:T(8,128)(2,1)S(1)} %bitcast.5), channel_id=1, source_target_pairs={{0,24},{4,28},{8,16},{12,20},{16,8},{20,12},{24,0},{28,4},{1,25},{... | collective-permute-start | bytes 786440 | tf_op jit(solution)/shard_map/ppermute | solution.py:37
  11.4 1.5 %collective-permute-done.2.refs_4_ = bf16[80,128]{1,0:T(8,128)(2,1)S(1)} collective-permute-done((bf16[80,128]{1,0:T(8,128)(2,1)S(1)}, bf16[80,128]{1,0:T(8,128)(2,1)S(1)}, u32[]{:S(2)}, u32[]{:S(2)}) %collective-permute-start.2) | collective-permute-done | bytes 20512 | tf_op jit(solution)/shard_map/ppermute | solution.py:37
  12.9 3.6 %collective-permute-start.5 = (bf16[192,128]{1,0:T(8,128)(2,1)S(1)}, bf16[192,128]{1,0:T(8,128)(2,1)S(1)}, u32[]{:S(2)}, u32[]{:S(2)}) collective-permute-start(bf16[192,128]{1,0:T(8,128)(2,1)S(1)} %get-tuple-element.42.refs_0_.src_ref), channel_id=1, source_target_pairs={{0,3},{1,2},{2,1},{3,0},{4,7},{5,6},{6,5},{7,4},{8,11},{9,10},{10,... | collective-permute-start | bytes 147464 | tf_op jit(solution)/shard_map/ppermute | solution.py:41
  16.5 0.8 %collective-permute-start.3 = (bf16[192,128]{1,0:T(8,128)(2,1)S(1)}, bf16[192,128]{1,0:T(8,128)(2,1)S(1)}, u32[]{:S(2)}, u32[]{:S(2)}) collective-permute-start(bf16[192,128]{1,0:T(8,128)(2,1)S(1)} %get-tuple-element.42.refs_0_.src_ref), channel_id=1, source_target_pairs={{0,1},{1,0},{2,3},{3,2},{4,5},{5,4},{6,7},{7,6},{8,9},{9,8},{10,11... | collective-permute-start | bytes 147464 | tf_op jit(solution)/shard_map/ppermute | solution.py:41
  17.4 0.9 %helmholtz.8 = (bf16[512,512]{1,0:T(8,128)(2,1)S(1)}, bf16[512,512]{1,0:T(8,128)(2,1)S(1)}) custom-call(bf16[64,512]{1,0:T(8,128)(2,1)S(1)} %target_matrix.1.tgt_ref, bf16[192,128]{1,0:T(8,128)(2,1)S(1)} %get-tuple-element.42.refs_0_.src_ref), custom_call_target="tpu_custom_call" | custom-call | flops 1022361600 | bytes 1 | tf_op jit(solution)/shard_map/helmholtz/pallas_call | solution.py:292
  19.3 2.2 %collective-permute-done.4.refs_2_.src_ref = bf16[192,128]{1,0:T(8,128)(2,1)S(1)} collective-permute-done((bf16[192,128]{1,0:T(8,128)(2,1)S(1)}, bf16[192,128]{1,0:T(8,128)(2,1)S(1)}, u32[]{:S(2)}, u32[]{:S(2)}) %collective-permute-start.4) | collective-permute-done | bytes 49184 | tf_op jit(solution)/shard_map/ppermute | solution.py:41
  21.6 0.9 %helmholtz.11 = (bf16[512,512]{1,0:T(8,128)(2,1)S(1)}, bf16[512,512]{1,0:T(8,128)(2,1)S(1)}) custom-call(bf16[64,512]{1,0:T(8,128)(2,1)S(1)} %target_matrix.1.tgt_ref, bf16[192,128]{1,0:T(8,128)(2,1)S(1)} %collective-permute-done.5.refs_3_.src_ref), custom_call_target="tpu_custom_call" | custom-call | flops 1022361600 | bytes 1 | tf_op jit(solution)/shard_map/helmholtz/pallas_call | solution.py:292
  22.6 0.9 %helmholtz.10 = (bf16[512,512]{1,0:T(8,128)(2,1)S(1)}, bf16[512,512]{1,0:T(8,128)(2,1)S(1)}) custom-call(bf16[64,512]{1,0:T(8,128)(2,1)S(1)} %target_matrix.1.tgt_ref, bf16[192,128]{1,0:T(8,128)(2,1)S(1)} %collective-permute-done.4.refs_2_.src_ref), custom_call_target="tpu_custom_call" | custom-call | flops 1022361600 | bytes 1 | tf_op jit(solution)/shard_map/helmholtz/pallas_call | solution.py:292
  23.5 0.9 %helmholtz.9 = (bf16[512,512]{1,0:T(8,128)(2,1)S(1)}, bf16[512,512]{1,0:T(8,128)(2,1)S(1)}) custom-call(bf16[64,512]{1,0:T(8,128)(2,1)S(1)} %target_matrix.1.tgt_ref, bf16[192,128]{1,0:T(8,128)(2,1)S(1)} %collective-permute-done.3.refs_1_.src_ref), custom_call_target="tpu_custom_call" | custom-call | flops 1022361600 | bytes 1 | tf_op jit(solution)/shard_map/helmholtz/pallas_call | solution.py:292
  24.5 0.9 %collective-permute-done.7.refs_6_.refs_10_ = bf16[128,1024]{1,0:T(8,128)(2,1)S(1)} collective-permute-done((bf16[128,1024]{1,0:T(8,128)(2,1)S(1)}, bf16[128,1024]{1,0:T(8,128)(2,1)S(1)}, u32[]{:S(2)}, u32[]{:S(2)}) %collective-permute-start.7) | collective-permute-done | bytes 262176 | tf_op jit(solution)/shard_map/ppermute | solution.py:37
  25.9 3.4 %collective-permute-start.12 = (bf16[4,32,128]{2,1,0:T(8,128)(2,1)S(1)}, bf16[4,32,128]{2,1,0:T(8,128)(2,1)S(1)}, u32[]{:S(2)}, u32[]{:S(2)}) collective-permute-start(bf16[4,32,128]{2,1,0:T(8,128)(2,1)S(1)} %velocities.1.refs_0_), channel_id=1, source_target_pairs={{0,3},{1,2},{2,1},{3,0},{4,7},{5,6},{6,5},{7,4},{8,11},{9,10},{10,... | collective-permute-start | bytes 98312 | tf_op jit(solution)/shard_map/ppermute | solution.py:41
  29.4 1.0 %collective-permute-start.10 = (bf16[4,32,128]{2,1,0:T(8,128)(2,1)S(1)}, bf16[4,32,128]{2,1,0:T(8,128)(2,1)S(1)}, u32[]{:S(2)}, u32[]{:S(2)}) collective-permute-start(bf16[4,32,128]{2,1,0:T(8,128)(2,1)S(1)} %velocities.1.refs_0_), channel_id=1, source_target_pairs={{0,1},{1,0},{2,3},{3,2},{4,5},{5,4},{6,7},{7,6},{8,9},{9,8},{10,11... | collective-permute-start | bytes 98312 | tf_op jit(solution)/shard_map/ppermute | solution.py:41
  30.4 0.9 %helmholtz.15 = (bf16[512,512]{1,0:T(8,128)(2,1)S(1)}, bf16[512,512]{1,0:T(8,128)(2,1)S(1)}) custom-call(bf16[64,512]{1,0:T(8,128)(2,1)S(1)} %target_matrix.1.tgt_ref, bf16[4,192,128]{2,1,0:T(8,128)(2,1)S(1)} %collective-permute-done.6.refs_4_.src_ref, bf16[4,32,128]{2,1,0:T(8,128)(2,1)S(1)} %velocities.1.refs_0_), custom_call_target="tpu_custom_call" | custom-call | flops 1431306240 | bytes 1 | tf_op jit(solution)/shard_map/helmholtz/pallas_call | solution.py:292
  31.3 1.0 %helmholtz.14 = (bf16[512,512]{1,0:T(8,128)(2,1)S(1)}, bf16[512,512]{1,0:T(8,128)(2,1)S(1)}) custom-call(bf16[64,512]{1,0:T(8,128)(2,1)S(1)} %target_matrix.1.tgt_ref, bf16[4,192,128]{2,1,0:T(8,128)(2,1)S(1)} %collective-permute-done.6.refs_4_.src_ref, bf16[4,32,128]{2,1,0:T(8,128)(2,1)S(1)} %velocities.1.refs_0_), custom_call_target="tpu_custom_call" | custom-call | flops 1431306240 | bytes 1 | tf_op jit(solution)/shard_map/helmholtz/pallas_call | solution.py:292
  32.3 1.0 %helmholtz.12 = (bf16[512,512]{1,0:T(8,128)(2,1)S(1)}, bf16[512,512]{1,0:T(8,128)(2,1)S(1)}) custom-call(bf16[64,512]{1,0:T(8,128)(2,1)S(1)} %target_matrix.1.tgt_ref, bf16[4,192,128]{2,1,0:T(8,128)(2,1)S(1)} %collective-permute-done.6.refs_4_.src_ref, bf16[4,32,128]{2,1,0:T(8,128)(2,1)S(1)} %velocities.1.refs_0_), custom_call_target="tpu_custom_call" | custom-call | flops 1431306240 | bytes 1 | tf_op jit(solution)/shard_map/helmholtz/pallas_call | solution.py:292
  33.3 0.9 %collective-permute-done.11.refs_2_ = bf16[4,32,128]{2,1,0:T(8,128)(2,1)S(1)} collective-permute-done((bf16[4,32,128]{2,1,0:T(8,128)(2,1)S(1)}, bf16[4,32,128]{2,1,0:T(8,128)(2,1)S(1)}, u32[]{:S(2)}, u32[]{:S(2)}) %collective-permute-start.11) | collective-permute-done | bytes 32800 | tf_op jit(solution)/shard_map/ppermute | solution.py:41
  34.3 0.9 %helmholtz.13 = (bf16[512,512]{1,0:T(8,128)(2,1)S(1)}, bf16[512,512]{1,0:T(8,128)(2,1)S(1)}) custom-call(bf16[64,512]{1,0:T(8,128)(2,1)S(1)} %target_matrix.1.tgt_ref, bf16[4,192,128]{2,1,0:T(8,128)(2,1)S(1)} %collective-permute-done.6.refs_4_.src_ref, bf16[4,32,128]{2,1,0:T(8,128)(2,1)S(1)} %velocities.1.refs_0_), custom_call_target="tpu_custom_call" | custom-call | flops 1431306240 | bytes 1 | tf_op jit(solution)/shard_map/helmholtz/pallas_call | solution.py:292
  35.2 0.8 %near_pressures.1.part_ref = f32[32,512]{1,0:T(8,128)S(1)} custom-call(bf16[4,32,128]{2,1,0:T(8,128)(2,1)S(1)} %velocities.1.refs_0_, bf16[4,32,128]{2,1,0:T(8,128)(2,1)S(1)} %collective-permute-done.10.refs_1_, bf16[4,32,128]{2,1,0:T(8,128)(2,1)S(1)} %collective-permute-done.11.refs_2_, bf16[4,32,128]{2,1,0:T(8,128)(2,1)S(1)} %collective-permute-done.12.refs_3_, ...), custom_call_target="tpu_custom_call" | custom-call | flops 1022361600 | bytes 1 | tf_op jit(solution)/shard_map/near_pressures/pallas_call | solution.py:332
  36.1 1.2 %pressures.1 = (bf16[4,32,128]{2,1,0:T(8,128)(2,1)S(1)}, f32[16,32,128]{2,1,0:T(8,128)S(1)}, bf16[16,32,128]{2,1,0:T(8,128)(2,1)S(1)}) custom-call(s32[4,128]{1,0:T(4,128)S(1)} %get-tuple-element.41.cpl, f32[32,512]{1,0:T(8,128)S(1)} %near_pressures.1.part_ref, bf16[4,4,32,128]{3,2,1,0:T(8,128)(2,1)S(1)} %collective-permute-done.13.v_far, ...), custom_call_target="tpu_custom_call" | custom-call | tf_op jit(solution)/shard_map/pressures/pallas_call | solution.py:375
  37.8 1.0 %collective-permute-done.14.got_ref = bf16[16,32,128]{2,1,0:T(8,128)(2,1)S(1)} collective-permute-done((bf16[16,32,128]{2,1,0:T(8,128)(2,1)S(1)}, bf16[16,32,128]{2,1,0:T(8,128)(2,1)S(1)}, u32[]{:S(2)}, u32[]{:S(2)}) %collective-permute-start.14) | collective-permute-done | bytes 131104 | tf_op jit(solution)/shard_map/ppermute | solution.py:45
  38.9 2.5 %collective-permute-start.15 = (bf16[4,32,128]{2,1,0:T(8,128)(2,1)S(1)}, bf16[4,32,128]{2,1,0:T(8,128)(2,1)S(1)}, u32[]{:S(2)}, u32[]{:S(2)}) collective-permute-start(bf16[4,32,128]{2,1,0:T(8,128)(2,1)S(1)} %get-tuple-element.62), channel_id=1, source_target_pairs={{0,3},{1,2},{2,1},{3,0},{4,7},{5,6},{6,5},{7,4},{8,11},{9,10},{10,... | collective-permute-start | bytes 98312 | tf_op jit(solution)/shard_map/ppermute | solution.py:41
  41.4 1.9 %collective-permute-start.17 = (bf16[4,32,128]{2,1,0:T(8,128)(2,1)S(1)}, bf16[4,32,128]{2,1,0:T(8,128)(2,1)S(1)}, u32[]{:S(2)}, u32[]{:S(2)}) collective-permute-start(bf16[4,32,128]{2,1,0:T(8,128)(2,1)S(1)} %get-tuple-element.64), channel_id=1, source_target_pairs={{0,1},{1,0},{2,3},{3,2},{4,5},{5,4},{6,7},{7,6},{8,9},{9,8},{10,11... | collective-permute-start | bytes 98312 | tf_op jit(solution)/shard_map/ppermute | solution.py:41
  43.3 1.5 %collective-permute-done.15.refs_1_ = bf16[4,32,128]{2,1,0:T(8,128)(2,1)S(1)} collective-permute-done((bf16[4,32,128]{2,1,0:T(8,128)(2,1)S(1)}, bf16[4,32,128]{2,1,0:T(8,128)(2,1)S(1)}, u32[]{:S(2)}, u32[]{:S(2)}) %collective-permute-start.15) | collective-permute-done | bytes 32800 | tf_op jit(solution)/shard_map/ppermute | solution.py:41
  44.8 1.4 %collective-permute-done.16.refs_2_ = bf16[4,32,128]{2,1,0:T(8,128)(2,1)S(1)} collective-permute-done((bf16[4,32,128]{2,1,0:T(8,128)(2,1)S(1)}, bf16[4,32,128]{2,1,0:T(8,128)(2,1)S(1)}, u32[]{:S(2)}, u32[]{:S(2)}) %collective-permute-start.16) | collective-permute-done | bytes 32800 | tf_op jit(solution)/shard_map/ppermute | solution.py:41
  46.6 1.6 %collective-permute-start.19 = (bf16[2,32,128]{2,1,0:T(8,128)(2,1)S(1)}, bf16[2,32,128]{2,1,0:T(8,128)(2,1)S(1)}, u32[]{:S(2)}, u32[]{:S(2)}) collective-permute-start(bf16[2,32,128]{2,1,0:T(8,128)(2,1)S(1)} %get-tuple-element.68), channel_id=1, source_target_pairs={{0,16},{4,20},{8,24},{12,28},{16,0},{20,4},{24,8},{28,12},{1,17},{... | collective-permute-start | bytes 49160 | tf_op jit(solution)/shard_map/ppermute | solution.py:37
  48.1 1.7 %collective-permute-start.20 = (bf16[2,32,128]{2,1,0:T(8,128)(2,1)S(1)}, bf16[2,32,128]{2,1,0:T(8,128)(2,1)S(1)}, u32[]{:S(2)}, u32[]{:S(2)}) collective-permute-start(bf16[2,32,128]{2,1,0:T(8,128)(2,1)S(1)} %get-tuple-element.69), channel_id=1, source_target_pairs={{0,8},{4,12},{8,0},{12,4},{16,24},{20,28},{24,16},{28,20},{1,9},{5... | collective-permute-start | bytes 49160 | tf_op jit(solution)/shard_map/ppermute | solution.py:37
  49.8 1.1 %collective-permute-done.18.r3 = bf16[2,32,128]{2,1,0:T(8,128)(2,1)S(1)} collective-permute-done((bf16[2,32,128]{2,1,0:T(8,128)(2,1)S(1)}, bf16[2,32,128]{2,1,0:T(8,128)(2,1)S(1)}, u32[]{:S(2)}, u32[]{:S(2)}) %collective-permute-start.18) | collective-permute-done | bytes 16416 | tf_op jit(solution)/shard_map/ppermute | solution.py:37
  51.0 0.9 %collective-permute-done.20.r2 = bf16[2,32,128]{2,1,0:T(8,128)(2,1)S(1)} collective-permute-done((bf16[2,32,128]{2,1,0:T(8,128)(2,1)S(1)}, bf16[2,32,128]{2,1,0:T(8,128)(2,1)S(1)}, u32[]{:S(2)}, u32[]{:S(2)}) %collective-permute-start.20) | collective-permute-done | bytes 16416 | tf_op jit(solution)/shard_map/ppermute | solution.py:37
  51.9 0.8 %outputs.1 = (f32[128,128]{1,0:T(8,128)}, bf16[128,128]{1,0:T(8,128)(2,1)}) custom-call(f32[2,32,128]{2,1,0:T(8,128)S(1)} %get-tuple-element.66.r0, bf16[2,32,128]{2,1,0:T(8,128)(2,1)S(1)} %collective-permute-done.18.r3, bf16[2,32,128]{2,1,0:T(8,128)(2,1)S(1)} %collective-permute-done.19.r1, bf16[2,32,128]{2,1,0:T(8,128)(2,1)S(1)} %collective-permute-done.20.r2), custom_call_target="tpu_custom_call" | custom-call | tf_op jit(solution)/shard_map/outputs/pallas_call | solution.py:454
  (33 shorter events, 3.3 us)
Async XLA Ops:
  0.6 7.2 %copy-start = (bf16[128,8,128]{2,1,0:T(8,128)(2,1)S(1)}, bf16[128,8,128]{2,1,0:T(8,128)(2,1)}, u32[]{:S(2)}) copy-start(bf16[128,8,128]{2,1,0:T(8,128)(2,1)} %param.8) | copy-start | bytes 786436
  3.3 8.1 %collective-permute-start = (bf16[80,128]{1,0:T(8,128)(2,1)S(1)}, bf16[80,128]{1,0:T(8,128)(2,1)S(1)}, u32[]{:S(2)}, u32[]{:S(2)}) collective-permute-start(bf16[80,128]{1,0:T(8,128)(2,1)S(1)} %get-tuple-element.38), channel_id=1, source_target_pairs={{0,16},{4,20},{8,24},{12,28},{16,0},{20,4},{24,8},{28,12},{1,17},{... | collective-permute-start | bytes 61448 | tf_op jit(solution)/shard_map/ppermute | solution.py:37
  6.3 5.1 %collective-permute-start.1 = (bf16[80,128]{1,0:T(8,128)(2,1)S(1)}, bf16[80,128]{1,0:T(8,128)(2,1)S(1)}, u32[]{:S(2)}, u32[]{:S(2)}) collective-permute-start(bf16[80,128]{1,0:T(8,128)(2,1)S(1)} %get-tuple-element.39), channel_id=1, source_target_pairs={{0,8},{4,12},{8,0},{12,4},{16,24},{20,28},{24,16},{28,20},{1,9},{5... | collective-permute-start | bytes 61448 | tf_op jit(solution)/shard_map/ppermute | solution.py:37
  7.8 5.0 %collective-permute-start.2 = (bf16[80,128]{1,0:T(8,128)(2,1)S(1)}, bf16[80,128]{1,0:T(8,128)(2,1)S(1)}, u32[]{:S(2)}, u32[]{:S(2)}) collective-permute-start(bf16[80,128]{1,0:T(8,128)(2,1)S(1)} %get-tuple-element.40), channel_id=1, source_target_pairs={{0,24},{4,28},{8,16},{12,20},{16,8},{20,12},{24,0},{28,4},{1,25},{... | collective-permute-start | bytes 61448 | tf_op jit(solution)/shard_map/ppermute | solution.py:37
  7.9 16.6 %collective-permute-start.9 = (bf16[128,1024]{1,0:T(8,128)(2,1)S(1)}, bf16[128,1024]{1,0:T(8,128)(2,1)S(1)}, u32[]{:S(2)}, u32[]{:S(2)}) collective-permute-start(bf16[128,1024]{1,0:T(8,128)(2,1)S(1)} %bitcast.5), channel_id=1, source_target_pairs={{0,24},{4,28},{8,16},{12,20},{16,8},{20,12},{24,0},{28,4},{1,25},{... | collective-permute-start | bytes 786440 | tf_op jit(solution)/shard_map/ppermute | solution.py:37
  10.9 13.6 %collective-permute-start.8 = (bf16[128,1024]{1,0:T(8,128)(2,1)S(1)}, bf16[128,1024]{1,0:T(8,128)(2,1)S(1)}, u32[]{:S(2)}, u32[]{:S(2)}) collective-permute-start(bf16[128,1024]{1,0:T(8,128)(2,1)S(1)} %bitcast.6), channel_id=1, source_target_pairs={{0,8},{4,12},{8,0},{12,4},{16,24},{20,28},{24,16},{28,20},{1,9},{5... | collective-permute-start | bytes 786440 | tf_op jit(solution)/shard_map/ppermute | solution.py:37
  12.9 6.2 %collective-permute-start.5 = (bf16[192,128]{1,0:T(8,128)(2,1)S(1)}, bf16[192,128]{1,0:T(8,128)(2,1)S(1)}, u32[]{:S(2)}, u32[]{:S(2)}) collective-permute-start(bf16[192,128]{1,0:T(8,128)(2,1)S(1)} %get-tuple-element.42.refs_0_.src_ref), channel_id=1, source_target_pairs={{0,3},{1,2},{2,1},{3,0},{4,7},{5,6},{6,5},{7,4},{8,11},{9,10},{10,... | collective-permute-start | bytes 147464 | tf_op jit(solution)/shard_map/ppermute | solution.py:41
  16.5 5.0 %collective-permute-start.4 = (bf16[192,128]{1,0:T(8,128)(2,1)S(1)}, bf16[192,128]{1,0:T(8,128)(2,1)S(1)}, u32[]{:S(2)}, u32[]{:S(2)}) collective-permute-start(bf16[192,128]{1,0:T(8,128)(2,1)S(1)} %get-tuple-element.42.refs_0_.src_ref), channel_id=1, source_target_pairs={{0,2},{1,3},{2,0},{3,1},{4,6},{5,7},{6,4},{7,5},{8,10},{9,11},{10,... | collective-permute-start | bytes 147464 | tf_op jit(solution)/shard_map/ppermute | solution.py:41
  16.5 5.0 %collective-permute-start.3 = (bf16[192,128]{1,0:T(8,128)(2,1)S(1)}, bf16[192,128]{1,0:T(8,128)(2,1)S(1)}, u32[]{:S(2)}, u32[]{:S(2)}) collective-permute-start(bf16[192,128]{1,0:T(8,128)(2,1)S(1)} %get-tuple-element.42.refs_0_.src_ref), channel_id=1, source_target_pairs={{0,1},{1,0},{2,3},{3,2},{4,5},{5,4},{6,7},{7,6},{8,9},{9,8},{10,11... | collective-permute-start | bytes 147464 | tf_op jit(solution)/shard_map/ppermute | solution.py:41
  19.0 6.4 %collective-permute-start.7 = (bf16[128,1024]{1,0:T(8,128)(2,1)S(1)}, bf16[128,1024]{1,0:T(8,128)(2,1)S(1)}, u32[]{:S(2)}, u32[]{:S(2)}) collective-permute-start(bf16[128,1024]{1,0:T(8,128)(2,1)S(1)} %bitcast.7), channel_id=1, source_target_pairs={{0,16},{4,20},{8,24},{12,28},{16,0},{20,4},{24,8},{28,12},{1,17},{... | collective-permute-start | bytes 786440 | tf_op jit(solution)/shard_map/ppermute | solution.py:37
  21.5 3.9 %collective-permute-start.6 = (bf16[4,192,128]{2,1,0:T(8,128)(2,1)S(1)}, bf16[4,192,128]{2,1,0:T(8,128)(2,1)S(1)}, u32[]{:S(2)}, u32[]{:S(2)}) collective-permute-start(bf16[4,192,128]{2,1,0:T(8,128)(2,1)S(1)} %stack.2), channel_id=1, source_target_pairs={{0,4},{4,0},{8,12},{12,8},{1,5},{5,1},{9,13},{13,9},{2,6},{6,2},{1... | collective-permute-start | bytes 589832 | tf_op jit(solution)/shard_map/ppermute | solution.py:45
  25.9 7.3 %collective-permute-start.12 = (bf16[4,32,128]{2,1,0:T(8,128)(2,1)S(1)}, bf16[4,32,128]{2,1,0:T(8,128)(2,1)S(1)}, u32[]{:S(2)}, u32[]{:S(2)}) collective-permute-start(bf16[4,32,128]{2,1,0:T(8,128)(2,1)S(1)} %velocities.1.refs_0_), channel_id=1, source_target_pairs={{0,3},{1,2},{2,1},{3,0},{4,7},{5,6},{6,5},{7,4},{8,11},{9,10},{10,... | collective-permute-start | bytes 98312 | tf_op jit(solution)/shard_map/ppermute | solution.py:41
  29.4 4.8 %collective-permute-start.11 = (bf16[4,32,128]{2,1,0:T(8,128)(2,1)S(1)}, bf16[4,32,128]{2,1,0:T(8,128)(2,1)S(1)}, u32[]{:S(2)}, u32[]{:S(2)}) collective-permute-start(bf16[4,32,128]{2,1,0:T(8,128)(2,1)S(1)} %velocities.1.refs_0_), channel_id=1, source_target_pairs={{0,2},{1,3},{2,0},{3,1},{4,6},{5,7},{6,4},{7,5},{8,10},{9,11},{10,... | collective-permute-start | bytes 98312 | tf_op jit(solution)/shard_map/ppermute | solution.py:41
  29.4 4.8 %collective-permute-start.10 = (bf16[4,32,128]{2,1,0:T(8,128)(2,1)S(1)}, bf16[4,32,128]{2,1,0:T(8,128)(2,1)S(1)}, u32[]{:S(2)}, u32[]{:S(2)}) collective-permute-start(bf16[4,32,128]{2,1,0:T(8,128)(2,1)S(1)} %velocities.1.refs_0_), channel_id=1, source_target_pairs={{0,1},{1,0},{2,3},{3,2},{4,5},{5,4},{6,7},{7,6},{8,9},{9,8},{10,11... | collective-permute-start | bytes 98312 | tf_op jit(solution)/shard_map/ppermute | solution.py:41
  34.2 1.9 %collective-permute-start.13 = (bf16[4,4,32,128]{3,2,1,0:T(8,128)(2,1)S(1)}, bf16[4,4,32,128]{3,2,1,0:T(8,128)(2,1)S(1)}, u32[]{:S(2)}, u32[]{:S(2)}) collective-permute-start(bf16[4,4,32,128]{3,2,1,0:T(8,128)(2,1)S(1)} %stack.3), channel_id=1, source_target_pairs={{0,4},{4,0},{8,12},{12,8},{1,5},{5,1},{9,13},{13,9},{2,6},{6,2},{1... | collective-permute-start | bytes 393224 | tf_op jit(solution)/shard_map/ppermute | solution.py:45
  37.3 1.5 %collective-permute-start.14 = (bf16[16,32,128]{2,1,0:T(8,128)(2,1)S(1)}, bf16[16,32,128]{2,1,0:T(8,128)(2,1)S(1)}, u32[]{:S(2)}, u32[]{:S(2)}) collective-permute-start(bf16[16,32,128]{2,1,0:T(8,128)(2,1)S(1)} %get-tuple-element.60), channel_id=1, source_target_pairs={{0,4},{4,0},{8,12},{12,8},{1,5},{5,1},{9,13},{13,9},{2,6},{6,2},{1... | collective-permute-start | bytes 393224 | tf_op jit(solution)/shard_map/ppermute | solution.py:45
  38.9 5.9 %collective-permute-start.15 = (bf16[4,32,128]{2,1,0:T(8,128)(2,1)S(1)}, bf16[4,32,128]{2,1,0:T(8,128)(2,1)S(1)}, u32[]{:S(2)}, u32[]{:S(2)}) collective-permute-start(bf16[4,32,128]{2,1,0:T(8,128)(2,1)S(1)} %get-tuple-element.62), channel_id=1, source_target_pairs={{0,3},{1,2},{2,1},{3,0},{4,7},{5,6},{6,5},{7,4},{8,11},{9,10},{10,... | collective-permute-start | bytes 98312 | tf_op jit(solution)/shard_map/ppermute | solution.py:41
  41.4 4.8 %collective-permute-start.16 = (bf16[4,32,128]{2,1,0:T(8,128)(2,1)S(1)}, bf16[4,32,128]{2,1,0:T(8,128)(2,1)S(1)}, u32[]{:S(2)}, u32[]{:S(2)}) collective-permute-start(bf16[4,32,128]{2,1,0:T(8,128)(2,1)S(1)} %get-tuple-element.63), channel_id=1, source_target_pairs={{0,2},{1,3},{2,0},{3,1},{4,6},{5,7},{6,4},{7,5},{8,10},{9,11},{10,... | collective-permute-start | bytes 98312 | tf_op jit(solution)/shard_map/ppermute | solution.py:41
  41.4 4.8 %collective-permute-start.17 = (bf16[4,32,128]{2,1,0:T(8,128)(2,1)S(1)}, bf16[4,32,128]{2,1,0:T(8,128)(2,1)S(1)}, u32[]{:S(2)}, u32[]{:S(2)}) collective-permute-start(bf16[4,32,128]{2,1,0:T(8,128)(2,1)S(1)} %get-tuple-element.64), channel_id=1, source_target_pairs={{0,1},{1,0},{2,3},{3,2},{4,5},{5,4},{6,7},{7,6},{8,9},{9,8},{10,11... | collective-permute-start | bytes 98312 | tf_op jit(solution)/shard_map/ppermute | solution.py:41
  46.3 4.7 %collective-permute-start.18 = (bf16[2,32,128]{2,1,0:T(8,128)(2,1)S(1)}, bf16[2,32,128]{2,1,0:T(8,128)(2,1)S(1)}, u32[]{:S(2)}, u32[]{:S(2)}) collective-permute-start(bf16[2,32,128]{2,1,0:T(8,128)(2,1)S(1)} %get-tuple-element.67), channel_id=1, source_target_pairs={{0,24},{4,28},{8,16},{12,20},{16,8},{20,12},{24,0},{28,4},{1,25},{... | collective-permute-start | bytes 49160 | tf_op jit(solution)/shard_map/ppermute | solution.py:37
  46.6 4.4 %collective-permute-start.19 = (bf16[2,32,128]{2,1,0:T(8,128)(2,1)S(1)}, bf16[2,32,128]{2,1,0:T(8,128)(2,1)S(1)}, u32[]{:S(2)}, u32[]{:S(2)}) collective-permute-start(bf16[2,32,128]{2,1,0:T(8,128)(2,1)S(1)} %get-tuple-element.68), channel_id=1, source_target_pairs={{0,16},{4,20},{8,24},{12,28},{16,0},{20,4},{24,8},{28,12},{1,17},{... | collective-permute-start | bytes 49160 | tf_op jit(solution)/shard_map/ppermute | solution.py:37
  48.1 3.7 %collective-permute-start.20 = (bf16[2,32,128]{2,1,0:T(8,128)(2,1)S(1)}, bf16[2,32,128]{2,1,0:T(8,128)(2,1)S(1)}, u32[]{:S(2)}, u32[]{:S(2)}) collective-permute-start(bf16[2,32,128]{2,1,0:T(8,128)(2,1)S(1)} %get-tuple-element.69), channel_id=1, source_target_pairs={{0,8},{4,12},{8,0},{12,4},{16,24},{20,28},{24,16},{28,20},{1,9},{5... | collective-permute-start | bytes 49160 | tf_op jit(solution)/shard_map/ppermute | solution.py:37
